TPU v7x, 32 devices: a whole 2x2x4 slice. The times are simulated.
32 devices in a mesh: seq: 16 (over z, x, core), tp: 2 (over y).
Axes of the slice: x: 2, y: 2, z: 4, core: 2. Of those that a mesh axis runs over, the one named last changes fastest.
Arguments:
- hidden: bfloat16 [2048, 3072], P('seq'), may hold values from -6 to 6
- latent: float32 [2048, 64], P('seq'), may hold values from -6 to 6
- key_cache: bfloat16 [2048, 2048], P('seq', 'tp'), may hold values from -8 to 8
- value_cache: bfloat16 [2048, 2048], P('seq', 'tp'), may hold values from -6 to 6
- text_keys: bfloat16 [4, 512, 2048], P(None, None, 'tp'), may hold values from -128 to 128
- text_values: bfloat16 [4, 512, 2048], P(None, None, 'tp'), may hold values from -6 to 6
- query_weight: bfloat16 [3072, 2048], P('seq', 'tp'), may hold values from -0.109375 to 0.109375
- key_weight: bfloat16 [3072, 2048], P('seq', 'tp'), may hold values from -0.109375 to 0.109375
- value_weight: bfloat16 [3072, 2048], P('seq', 'tp'), may hold values from -0.109375 to 0.109375
- out_weight: bfloat16 [3072, 2048], P('seq', 'tp'), may hold values from -0.1875 to 0.1875
- query_gain: float32 [128], replicated, may hold values from 1.2 to 2.5
- key_gain: float32 [128], replicated, may hold values from 1.2 to 2.5
- mod_shift: float32 [4, 3072], replicated, may hold values from -3 to 3
- mod_scale: float32 [4, 3072], replicated, may hold values from -0.9 to 0.9
- mod_gate: float32 [4, 3072], replicated, may hold values from -4 to 4
- final_weight: bfloat16 [3072, 64], P('tp'), may hold values from -0.109375 to 0.109375
- conv_weight: bfloat16 [144, 512], P(None, 'tp'), may hold values from -0.5 to 0.5
- image_rows: int32 [4], replicated, may hold values from 1 to 24, as said below
- tile_owner: int32 [16], replicated, may hold values from 0 to 4, as said below
- listed: int32 [16, 32], P('seq'), may hold values from 0 to 127, as said below
- step_index: int32 [4], replicated, may hold values from 0 to 7
Outputs:
- hidden_next: bfloat16 [2048, 3072], P('seq', 'tp')
- latent_next: float32 [2048, 64], P('seq')
- decoded: bfloat16 [8192, 512], P('seq', 'tp')
Inputs may be any that keep to these rules, and one draw needn't show every extreme that they name: `image_rows`: one request has exactly 24 rows. `tile_owner`: the tiles of each request are consecutive and in request order, a request of r rows holds ceil(r * 64 / 128) tiles, and every tile after them holds 4, meaning no request. The rows listed for one tile are distinct.
All inputs are finite; a program needn't handle non-finite values.
Results may differ from a plain program's by a relative error of at most 0.009.
Values may be sent and summed in bfloat16 or wider, within the bound.
A program may use at most 64 MiB of HBM per device.

v0:
```python
import math

import jax
import jax.numpy as jnp
from jax import lax
from jax.sharding import PartitionSpec as P

HD = 128
LAT_CH = 64
IMG_W = 64
STEPS = 8


EPSILON = 1e-06
SIGMA_SHIFT = 3.0


def with_halo(shard, sides, width):
    for axis, dim in sides:
        devices, length = (lax.axis_size(axis), shard.shape[dim])
        up = [(i, (i + 1) % devices) for i in range(devices - 1)]
        down = [(j, i) for i, j in up]
        last = lax.slice_in_dim(shard, length - width, length, axis=dim)
        first = lax.slice_in_dim(shard, 0, width, axis=dim)
        before = lax.ppermute(last, axis, up)
        after = lax.ppermute(first, axis, down)
        shard = jnp.concatenate([before, shard, after], axis=dim)
    return shard


def tile_layout(tile_owner, image_rows, tile_rows, row_width):
    request_count = image_rows.shape[0]
    tile_count = tile_owner.shape[0]
    earlier = jnp.sum((tile_owner[None, :] < tile_owner[:, None]).astype(jnp.int32), axis=1)
    ordinal = jnp.arange(tile_count, dtype=jnp.int32) - earlier
    mod_req = jnp.minimum(tile_owner, request_count - 1)
    picked = jnp.sum(
        jnp.where(
            mod_req[:, None] == jnp.arange(request_count, dtype=jnp.int32)[None, :],
            image_rows[None, :],
            0,
        ),
        axis=1,
    )
    live_rows = jnp.where(
        tile_owner < request_count,
        jnp.clip(picked * row_width - ordinal * tile_rows, 0, tile_rows),
        0,
    )
    return (mod_req, live_rows)


def sigma_of(step_index):
    fraction = 1.0 - step_index.astype(jnp.float32) / STEPS
    return SIGMA_SHIFT * fraction / (1.0 + (SIGMA_SHIFT - 1.0) * fraction)


def head_norm(projected, head_gain):
    row_count = projected.shape[0]
    shaped = projected.reshape(row_count, -1, HD)
    inverse = lax.rsqrt(jnp.mean(jnp.square(shaped), axis=2, keepdims=True) + EPSILON)
    return shaped * inverse * head_gain


def shards(
    hidden,
    latent,
    key_cache,
    value_cache,
    text_keys,
    text_values,
    query_weight,
    key_weight,
    value_weight,
    out_weight,
    query_gain,
    key_gain,
    mod_shift,
    mod_scale,
    mod_gate,
    final_weight,
    conv_weight,
    image_rows,
    tile_owner,
    listed,
    step_index,
):
    tile_rows = hidden.shape[0]
    seq_count = lax.axis_size("seq")
    seq_index = lax.axis_index("seq")
    tp_index = lax.axis_index("tp")
    request_count = image_rows.shape[0]
    mod_req, live_rows = tile_layout(tile_owner, image_rows, tile_rows, IMG_W)
    row_index = jnp.arange(tile_rows, dtype=jnp.int32)
    token_req = jnp.where(row_index[None, :] < live_rows[:, None], tile_owner[:, None], -1).reshape(
        -1
    )
    own_tokens = lax.dynamic_slice_in_dim(token_req, seq_index * tile_rows, tile_rows)
    own_request = mod_req[seq_index]
    own_owner = tile_owner[seq_index]
    select = (jnp.arange(request_count, dtype=jnp.int32) == own_request).astype(jnp.float32)

    def choose_row(table):
        return jnp.dot(select, table, precision=lax.Precision.HIGHEST)

    hidden_f32 = hidden.astype(jnp.float32)
    row_mean = jnp.mean(hidden_f32, axis=1, keepdims=True)
    row_var = jnp.mean(jnp.square(hidden_f32 - row_mean), axis=1, keepdims=True)
    normed = (hidden_f32 - row_mean) * lax.rsqrt(row_var + EPSILON)
    modulated = (
        (1.0 + choose_row(mod_scale))[None, :] * normed + choose_row(mod_shift)[None, :]
    ).astype(jnp.bfloat16)
    listed_rows = listed[0]
    listed_x = modulated[listed_rows]
    local_width = key_cache.shape[1]
    local_heads = local_width // HD
    gathered_q, gathered_k, gathered_v, gathered_out = (
        lax.all_gather(query_weight, "seq", axis=0, tiled=True),
        lax.all_gather(key_weight, "seq", axis=0, tiled=True),
        lax.all_gather(value_weight, "seq", axis=0, tiled=True),
        lax.all_gather(out_weight, "seq", axis=0, tiled=True),
    )
    query_raw = jnp.dot(modulated, gathered_q, preferred_element_type=jnp.float32)
    key_raw = jnp.dot(listed_x, gathered_k, preferred_element_type=jnp.float32)
    value_raw = jnp.dot(listed_x, gathered_v, preferred_element_type=jnp.float32)
    queries = head_norm(query_raw, query_gain).astype(jnp.bfloat16)
    fresh_keys = head_norm(key_raw, key_gain).astype(jnp.bfloat16).reshape(-1, local_width)
    fresh_values = value_raw.astype(jnp.bfloat16)
    local_keys = key_cache.at[listed_rows].set(fresh_keys)
    local_values = value_cache.at[listed_rows].set(fresh_values)
    score_scale = 1.0 / math.sqrt(HD)
    text_key_tile = lax.dynamic_index_in_dim(text_keys, own_request, 0, keepdims=False).reshape(
        -1, local_heads, HD
    )
    text_value_tile = lax.dynamic_index_in_dim(text_values, own_request, 0, keepdims=False).reshape(
        -1, local_heads, HD
    )
    text_scores = (
        jnp.einsum("qhd,khd->hqk", queries, text_key_tile, preferred_element_type=jnp.float32)
        * score_scale
    )
    row_max = jnp.max(text_scores, axis=2)
    text_exp = jnp.exp(text_scores - row_max[..., None])
    row_sum = jnp.sum(text_exp, axis=2)
    weighted = jnp.einsum(
        "hqk,khd->hqd",
        text_exp.astype(jnp.bfloat16),
        text_value_tile,
        preferred_element_type=jnp.float32,
    )

    def attend(state_now, key_tile, value_tile, key_owner):
        old_max, old_sum, old_weighted = state_now
        allowed = (key_owner[None, :] == own_tokens[:, None]) & (own_tokens[:, None] >= 0)
        key_heads = key_tile.reshape(-1, local_heads, HD)
        value_heads = value_tile.reshape(-1, local_heads, HD)
        scores = (
            jnp.einsum("qhd,khd->hqk", queries, key_heads, preferred_element_type=jnp.float32)
            * score_scale
        )
        scores = jnp.where(allowed[None], scores, -jnp.inf)
        new_max = jnp.maximum(old_max, jnp.max(scores, axis=2))
        shrink = jnp.exp(old_max - new_max)
        exp_scores = jnp.exp(scores - new_max[..., None])
        new_sum = old_sum * shrink + jnp.sum(exp_scores, axis=2)
        new_weighted = old_weighted * shrink[..., None] + jnp.einsum(
            "hqk,khd->hqd",
            exp_scores.astype(jnp.bfloat16),
            value_heads,
            preferred_element_type=jnp.float32,
        )
        return (new_max, new_sum, new_weighted)

    pieces = (
        lax.all_gather(local_keys, "seq", axis=0, tiled=True),
        lax.all_gather(local_values, "seq", axis=0, tiled=True),
    )
    length = pieces[0].shape[0]
    key_owner = token_req
    key_block = 1024
    block_count = length // key_block
    stacked = (
        pieces[0].reshape(block_count, key_block, -1),
        pieces[1].reshape(block_count, key_block, -1),
        key_owner.reshape(block_count, key_block),
    )

    def scan_step(state_mid, blocks):
        return (attend(state_mid, blocks[0], blocks[1], blocks[2]), None)

    row_max, row_sum, weighted = lax.scan(scan_step, (row_max, row_sum, weighted), stacked)[0]
    attended = (
        jnp.transpose(weighted / row_sum[..., None], (1, 0, 2))
        .reshape(tile_rows, local_width)
        .astype(jnp.bfloat16)
    )
    partial_out = lax.dot_general(
        attended, gathered_out, (((1,), (1,)), ((), ())), preferred_element_type=jnp.float32
    )
    reduced = lax.psum_scatter(
        partial_out.astype(jnp.bfloat16), "tp", scatter_dimension=1, tiled=True
    ).astype(jnp.float32)
    col_count = reduced.shape[1]
    hidden_cols = lax.dynamic_slice_in_dim(hidden_f32, tp_index * col_count, col_count, 1)
    gate_cols = lax.dynamic_slice_in_dim(choose_row(mod_gate), tp_index * col_count, col_count)
    hidden_next = (hidden_cols + gate_cols[None, :] * reduced).astype(jnp.bfloat16)
    velocity = lax.psum(
        jnp.dot(hidden_next, final_weight, preferred_element_type=jnp.float32).astype(jnp.bfloat16),
        "tp",
    ).astype(jnp.float32)
    step_delta = sigma_of(step_index + 1) - sigma_of(step_index)
    own_delta = jnp.sum(select * step_delta)
    latent_next = latent + own_delta * velocity
    token_live = own_tokens >= 0
    dec_input = jnp.where(token_live[:, None], latent_next, 0.0).astype(jnp.bfloat16)
    padded = with_halo(dec_input, (("seq", 0),), IMG_W)
    prev_owner = tile_owner[jnp.maximum(seq_index - 1, 0)]
    next_owner = tile_owner[jnp.minimum(seq_index + 1, seq_count - 1)]
    same_prev = (seq_index > 0) & (prev_owner == own_owner)
    same_next = (seq_index < seq_count - 1) & (next_owner == own_owner)
    upper = jnp.where(same_prev, padded[:IMG_W], 0.0)
    lower = jnp.where(same_next, padded[IMG_W + tile_rows :], 0.0)
    framed_tokens = jnp.concatenate([upper, padded[IMG_W : IMG_W + tile_rows], lower], axis=0)
    token_rows = tile_rows // IMG_W
    pixel_ch = LAT_CH // 4
    pixels = framed_tokens.reshape(token_rows + 2, IMG_W, pixel_ch, 2, 2)
    pixels = jnp.transpose(pixels, (0, 3, 1, 4, 2)).reshape(
        2 * (token_rows + 2), 2 * IMG_W, pixel_ch
    )
    framed = pixels[1 : 2 * token_rows + 3]
    framed = jnp.pad(framed, ((0, 0), (1, 1), (0, 0)))
    patches = jnp.concatenate(
        [
            framed[row_shift : row_shift + 2 * token_rows, col_shift : col_shift + 2 * IMG_W, :]
            for row_shift in range(3)
            for col_shift in range(3)
        ],
        axis=-1,
    )
    convolved = jnp.dot(
        patches.reshape(-1, 9 * pixel_ch), conv_weight, preferred_element_type=jnp.float32
    )
    pixel_live = jnp.broadcast_to(
        token_live.reshape(token_rows, 1, IMG_W, 1), (token_rows, 2, IMG_W, 2)
    ).reshape(-1)
    decoded = jnp.where(pixel_live[:, None], convolved, 0.0).astype(jnp.bfloat16)
    return (hidden_next, latent_next, decoded)


def solution(mesh):
    return jax.shard_map(
        shards,
        mesh=mesh,
        in_specs=(
            P("seq", None),
            P("seq", None),
            P("seq", "tp"),
            P("seq", "tp"),
            P(None, None, "tp"),
            P(None, None, "tp"),
            P("seq", "tp"),
            P("seq", "tp"),
            P("seq", "tp"),
            P("seq", "tp"),
            P(),
            P(),
            P(),
            P(),
            P(),
            P("tp", None),
            P(None, "tp"),
            P(),
            P(),
            P("seq", None),
            P(),
        ),
        out_specs=(P("seq", "tp"), P("seq", None), P("seq", "tp")),
        check_vma=False,
    )
```

profile of v0, /device:TPU:1, one launch (start us, length us, event | category | flops | bytes accessed | tf_op | source)
XLA Modules:
  0.0 419.2 jit_solution(14163381144841639630)
XLA Ops:
  8.0 0.7 all-gather.13.cloned.1.call-update
  10.8 0.9 fusion.30
  11.7 0.8 fusion.28
  13.6 61.1 %all-gather.9.cloned.1.call-done = bf16[3072,1024]{1,0:T(8,128)(2,1)} async-done(((bf16[192,1024]{1,0:T(8,128)(2,1)}), bf16[3072,1024]{1,0:T(8,128)(2,1)}) %all-gather.9.cloned.1.call-update) | async-done | bytes 6291472 | tf_op jit(solution)/shard_map/all_gather | solution.py:119
  74.7 4.0 fusion.43
  79.0 0.9 scatter_custom_fusion
  80.7 56.8 %all-gather.13.cloned.1.call-done = bf16[3072,1024]{1,0:T(8,128)(2,1)} async-done(((bf16[192,1024]{1,0:T(8,128)(2,1)}), bf16[3072,1024]{1,0:T(8,128)(2,1)}) %all-gather.13.cloned.1.call-update) | async-done | bytes 6291472 | tf_op jit(solution)/shard_map/all_gather | solution.py:120
  137.5 4.0 convolution_convert_fusion.1
  141.5 0.9 scatter_fusion
  146.1 2.8 constant_dynamic-slice_fusion.3
  148.8 2.3 copy.84
  151.1 1.3 copy.85
  153.1 47.2 %all-gather.7.cloned.1.call-done = bf16[3072,1024]{1,0:T(8,128)(2,1)} async-done(((bf16[192,1024]{1,0:T(8,128)(2,1)}), bf16[3072,1024]{1,0:T(8,128)(2,1)}) %all-gather.7.cloned.1.call-update) | async-done | bytes 6291472 | tf_op jit(solution)/shard_map/all_gather | solution.py:118
  200.3 3.8 fusion.42
  204.7 1.8 multiply_reduce_fusion
  207.1 1.4 fusion.17
  208.5 43.6 %all-gather.11.cloned.1.call-done = bf16[2048,1024]{1,0:T(8,128)(2,1)} async-done(((bf16[128,1024]{1,0:T(8,128)(2,1)}), bf16[2048,1024]{1,0:T(8,128)(2,1)}) %all-gather.11.cloned.1.call-update) | async-done | bytes 4194320 | tf_op jit(solution)/shard_map/all_gather | solution.py:175
  252.0 51.7 %all-gather.15.cloned.1.call-done = bf16[2048,1024]{1,0:T(8,128)(2,1)} async-done(((bf16[128,1024]{1,0:T(8,128)(2,1)}), bf16[2048,1024]{1,0:T(8,128)(2,1)}) %all-gather.15.cloned.1.call-update) | async-done | bytes 4194320 | tf_op jit(solution)/shard_map/all_gather | solution.py:176
  303.7 39.5 %while.14 = (s32[]{:T(128)}, f32[8,128]{1,0:T(8,128)S(1)}, f32[8,128]{1,0:T(8,128)S(1)}, f32[8,128,128]{2,1,0:T(8,128)}, s32[2,1024]{1,0:T(2,128)S(1)}, /*index=...) while((s32[]{:T(128)}, f32[8,128]{1,0:T(8,128)S(1)}, ...), condition=%wide.region_13.14_spmd, body=%wide.region_10.13_spmd.sunk | while | flops 548931712 | bytes 60634532 | solution.py:191
  304.0 4.7 %constant_dynamic-slice_fusion.8 = (bf16[1,1024,1024]{2,1,0:T(8,128)(2,1)}, bf16[1,1024,1024]{2,1,0:T(8,128)(2,1)}) fusion(bf16[2,1024,1024]{2,1,0:T(8,128)(2,1)} %get-tuple-element.231, s32[]{:T(128)} %get-tuple-element.213, bf16[2,1024,1024]{2,1,0:T(8,128)(2,1)} %get-tuple-element.229), kind=kLoop, calls=%fused_computation.17.clone.1 | loop fusion | bytes 8388612 | tf_op jit(solution)/shard_map/while/body/jit(dynamic_index_in_dim)/dynamic_slice | solution.py:191
  308.7 2.9 copy.99
  311.5 1.1 fusion.77
  312.7 0.9 fusion.78
  313.5 1.2 copy-done.1
  314.8 1.0 copy-done.2
  315.8 2.6 copy.100
  318.3 5.1 %fusion.79 = f32[8,128,128]{2,1,0:T(8,128)} fusion(bf16[1024,8,128]{0,2,1:T(8,128)(2,1)} %bitcast.132, f32[8,1024,128]{2,1,0:T(8,128)} %copy-done.1, f32[8,128]{1,0:T(8,128)S(1)} %max.16, pred[128,1024]{0,1:T(8,128)(4,1)S(1)} %compare_and_fusion.2, f32[8,128,128]{2,1,0:T(8,128)} %get-tuple-element.216, f32[8,128]{1,0:T(8,128)S(1)} %get-tuple-element.202), kind=kOutput, calls=%fused_computation.13.clone.1 | convolution fusion | flops 272891904 | bytes 7479296 | tf_op jit(solution)/shard_map/while/body/eval_jaxpr/hqk,khd->hqd/dot_general | solution.py:166
  323.7 4.7 %constant_dynamic-slice_fusion.8 = (bf16[1,1024,1024]{2,1,0:T(8,128)(2,1)}, bf16[1,1024,1024]{2,1,0:T(8,128)(2,1)}) fusion(bf16[2,1024,1024]{2,1,0:T(8,128)(2,1)} %get-tuple-element.231, s32[]{:T(128)} %get-tuple-element.213, bf16[2,1024,1024]{2,1,0:T(8,128)(2,1)} %get-tuple-element.229), kind=kLoop, calls=%fused_computation.17.clone.1 | loop fusion | bytes 8388612 | tf_op jit(solution)/shard_map/while/body/jit(dynamic_index_in_dim)/dynamic_slice | solution.py:191
  328.4 2.9 copy.99
  331.3 1.1 fusion.77
  332.4 0.9 fusion.78
  333.3 1.3 copy-done.1
  334.6 1.0 copy-done.2
  335.6 2.6 copy.100
  338.2 5.1 %fusion.79 = f32[8,128,128]{2,1,0:T(8,128)} fusion(bf16[1024,8,128]{0,2,1:T(8,128)(2,1)} %bitcast.132, f32[8,1024,128]{2,1,0:T(8,128)} %copy-done.1, f32[8,128]{1,0:T(8,128)S(1)} %max.16, pred[128,1024]{0,1:T(8,128)(4,1)S(1)} %compare_and_fusion.2, f32[8,128,128]{2,1,0:T(8,128)} %get-tuple-element.216, f32[8,128]{1,0:T(8,128)S(1)} %get-tuple-element.202), kind=kOutput, calls=%fused_computation.13.clone.1 | convolution fusion | flops 272891904 | bytes 7479296 | tf_op jit(solution)/shard_map/while/body/eval_jaxpr/hqk,khd->hqd/dot_general | solution.py:166
  343.3 1.2 copy.75
  344.6 21.7 %all-gather.17.cloned.1.call-done = bf16[3072,1024]{1,0:T(8,128)(2,1)} async-done(((bf16[192,1024]{1,0:T(8,128)(2,1)}), bf16[3072,1024]{1,0:T(8,128)(2,1)}) %all-gather.17.cloned.1.call-update) | async-done | bytes 6291472 | tf_op jit(solution)/shard_map/all_gather | solution.py:121
  366.2 5.9 %convolution_convert_fusion = bf16[128,3072]{1,0:T(8,128)(2,1)} fusion(bf16[128,1024]{0,1:T(8,128)(2,1)S(1)} %bitcast.142, bf16[3072,1024]{1,0:T(8,128)(2,1)} %all-gather.17.cloned.1.call-done), kind=kOutput, calls=%fused_computation.23 | convolution fusion | flops 805699584 | bytes 7340032 | tf_op jit(solution)/shard_map/dot_general | solution.py:197
  372.9 0.8 fusion.32
  373.9 1.3 select_reduce_fusion.1
  375.2 12.8 %reduce-scatter.2.cloned.1.call-done = bf16[128,1536]{1,0:T(8,128)(2,1)} async-done(((bf16[128,3072]{1,0:T(8,128)(2,1)}), bf16[128,1536]{1,0:T(8,128)(2,1)}) %reduce-scatter.2.cloned.1.call-update) | async-done | bytes 393232 | tf_op jit(solution)/shard_map/reduce_scatter | solution.py:200
  387.9 1.1 add_convert_fusion.1
  389.3 5.3 %psum.7 = bf16[128,64]{0,1:T(8,128)(2,1)S(1)} all-reduce(bf16[128,64]{0,1:T(8,128)(2,1)S(1)} %convolution_convert_fusion.2), channel_id=1, replica_groups=mesh['seq'=16,'tp'=2] {'tp'}, use_global_device_ids=true, to_apply=%region_16.17 | all-reduce | flops 8192 | bytes 32768 | tf_op jit(solution)/shard_map/psum | solution.py:207
  394.6 1.3 select_convert_fusion
  396.0 5.5 %collective-permute-start = (bf16[64,64]{0,1:T(8,128)(2,1)S(1)}, bf16[64,64]{0,1:T(8,128)(2,1)S(1)}, u32[]{:S(2)}, u32[]{:S(2)}) collective-permute-start(bf16[64,64]{0,1:T(8,128)(2,1)S(1)} %get-tuple-element.125), channel_id=1, source_target_pairs={{0,2},{2,4},{4,6},{6,8},{8,10},{10,12},{12,14},{14,16},{16,18},{18... | collective-permute-start | bytes 24584 | tf_op jit(solution)/shard_map/ppermute | solution.py:25
  405.0 1.9 collective-permute-start.1
  407.0 3.1 collective-permute-done.1
  411.4 0.9 fusion.16
  (120 shorter events, 12.2 us)
Async XLA Ops:
  7.2 381.9 %copy-start = (bf16[1536,64]{0,1:T(8,128)(2,1)S(1)}, bf16[1536,64]{0,1:T(8,128)(2,1)}, u32[]{:S(2)}) copy-start(bf16[1536,64]{0,1:T(8,128)(2,1)} %param.38) | copy-start | bytes 589828
  7.2 3.0 copy-start.3
  7.2 4.5 %copy-start.11 = (f32[4,3072]{1,0:T(4,128)S(1)}, f32[4,3072]{1,0:T(4,128)}, u32[]{:S(2)}) copy-start(f32[4,3072]{1,0:T(4,128)} %param.35) | copy-start | bytes 147460
  7.2 3.6 copy-start.10
  7.2 2.3 copy-start.14
  7.2 3.0 copy-start.18
  7.2 67.5 %all-gather.9.cloned.1.call-start = ((), (), s32[]{:S(2)}) async-start(), calls=%async_computation.2 | async-start | bytes 6684672 | tf_op jit(solution)/shard_map/all_gather | solution.py:119
  8.0 129.5 %all-gather.13.cloned.1.call-start = ((), (), s32[]{:S(2)}) async-start(), calls=%async_computation.4 | async-start | bytes 6684672 | tf_op jit(solution)/shard_map/all_gather | solution.py:120
  8.7 191.6 %all-gather.7.cloned.1.call-start = ((), (), s32[]{:S(2)}) async-start(), calls=%async_computation.1 | async-start | bytes 6684672 | tf_op jit(solution)/shard_map/all_gather | solution.py:118
  9.4 242.6 %all-gather.11.cloned.1.call-start = ((), (), s32[]{:S(2)}) async-start(), calls=%async_computation.3 | async-start | bytes 4456448 | tf_op jit(solution)/shard_map/all_gather | solution.py:175
  10.4 3.2 copy-start.15
  13.6 65.4 %copy-start.9 = (bf16[128,1024]{1,0:T(8,128)(2,1)S(1)}, bf16[128,1024]{1,0:T(8,128)(2,1)}, u32[]{:S(2)}) copy-start(bf16[128,1024]{1,0:T(8,128)(2,1)} %param.25) | copy-start | bytes 786436
  79.9 0.7 copy-start.8
  80.7 60.8 %copy-start.5 = (bf16[128,1024]{1,0:T(8,128)(2,1)S(1)}, bf16[128,1024]{1,0:T(8,128)(2,1)}, u32[]{:S(2)}) copy-start(bf16[128,1024]{1,0:T(8,128)(2,1)} %param.26) | copy-start | bytes 786436
  80.7 223.0 %all-gather.15.cloned.1.call-start = ((), (), s32[]{:S(2)}) async-start(), calls=%async_computation.5 | async-start | bytes 4456448 | tf_op jit(solution)/shard_map/all_gather | solution.py:176
  142.4 0.7 copy-start.4
  143.1 223.1 %all-gather.17.cloned.1.call-start = ((), (), s32[]{:S(2)}) async-start(), calls=%async_computation.6 | async-start | bytes 6684672 | tf_op jit(solution)/shard_map/all_gather | solution.py:121
  143.7 244.2 %reduce-scatter.2.cloned.1.call-start = ((), (), s32[]{:S(2)}) async-start(), calls=%async_computation.7 | async-start | bytes 1179648 | tf_op jit(solution)/shard_map/reduce_scatter | solution.py:200
  148.8 3.8 copy-start.19
  153.1 51.3 %copy-start.16 = (f32[128]{0:T(128)S(1)}, f32[128]{0:T(128)}, u32[]{:S(2)}) copy-start(f32[128]{0:T(128)} %param.33) | copy-start | bytes 1540
  204.7 2.4 copy-start.6
  312.6 2.1 copy-start.1
  312.7 3.1 copy-start.2
  332.4 2.2 copy-start.1
  332.4 3.2 copy-start.2
  372.1 0.8 copy-start.12
  372.1 1.7 copy-start.20
  372.2 22.5 %copy-start.13 = (f32[128,64]{0,1:T(8,128)S(1)}, f32[128,64]{0,1:T(8,128)}, u32[]{:S(2)}) copy-start(f32[128,64]{0,1:T(8,128)} %param.24) | copy-start | bytes 98308
  389.0 22.4 %copy-start.7 = (bf16[128,1536]{1,0:T(8,128)(2,1)}, bf16[128,1536]{1,0:T(8,128)(2,1)S(1)}, u32[]{:S(2)}) copy-start(bf16[128,1536]{1,0:T(8,128)(2,1)S(1)} %add_convert_fusion.1) | copy-start | bytes 1179652
  396.0 11.0 %collective-permute-start = (bf16[64,64]{0,1:T(8,128)(2,1)S(1)}, bf16[64,64]{0,1:T(8,128)(2,1)S(1)}, u32[]{:S(2)}, u32[]{:S(2)}) collective-permute-start(bf16[64,64]{0,1:T(8,128)(2,1)S(1)} %get-tuple-element.125), channel_id=1, source_target_pairs={{0,2},{2,4},{4,6},{6,8},{8,10},{10,12},{12,14},{14,16},{16,18},{18... | collective-permute-start | bytes 24584 | tf_op jit(solution)/shard_map/ppermute | solution.py:25
  405.0 5.1 %collective-permute-start.1 = (bf16[64,64]{0,1:T(8,128)(2,1)S(1)}, bf16[64,64]{0,1:T(8,128)(2,1)S(1)}, u32[]{:S(2)}, u32[]{:S(2)}) collective-permute-start(bf16[64,64]{0,1:T(8,128)(2,1)S(1)} %get-tuple-element.126), channel_id=1, source_target_pairs={{2,0},{4,2},{6,4},{8,6},{10,8},{12,10},{14,12},{16,14},{18,16},{20... | collective-permute-start | bytes 24584 | tf_op jit(solution)/shard_map/ppermute | solution.py:26
  407.0 4.4 %copy-start.17 = (bf16[144,256]{1,0:T(8,128)(2,1)S(1)}, bf16[144,256]{1,0:T(8,128)(2,1)}, u32[]{:S(2)}) copy-start(bf16[144,256]{1,0:T(8,128)(2,1)} %param.39) | copy-start | bytes 221188
Sparse Core Ops, SparseCore 0:
  10.3 64.3 all-gather.8
  77.0 60.4 all-gather.12
  139.8 60.4 all-gather.6
  202.9 49.1 all-gather.10
  254.6 49.0 all-gather.14
  305.9 60.3 all-gather.16
  372.3 15.5 reduce-scatter.1
where the time goes:
time: 420 us; the launch traced here: 419 us
  waiting for transfers between devices  300 us (71%)
  local copies, waits for them, and re-layouts  39.6 us (9%)
  matrix products  36.9 us (9%)
  between operations  19.2 us (5%)
  other arithmetic  9.63 us (2%)
  starting transfers between devices  7.89 us (2%)
  blocking collectives  5.35 us (1%)
    all_gather x1, waiting for transfers between devices, shards(): lax.all_gather(key_weight, 'seq', axis=0, tiled=True)  61.1 us
    all_gather x1, waiting for transfers between devices, shards(): lax.all_gather(value_weight, 'seq', axis=0, tiled=True)  56.8 us
    all_gather x1, waiting for transfers between devices, shards(): lax.all_gather(local_values, 'seq', axis=0, tiled=True)  51.7 us
    all_gather x1, waiting for transfers between devices, shards(): lax.all_gather(query_weight, 'seq', axis=0, tiled=True)  47.2 us
    all_gather x1, waiting for transfers between devices, shards(): lax.all_gather(local_keys, 'seq', axis=0, tiled=True)  43.6 us
    all_gather x1, waiting for transfers between devices, shards(): lax.all_gather(out_weight, 'seq', axis=0, tiled=True)  21.7 us
    dynamic_slice x8, local copies, waits for them, and re-layouts, shards(): lax.scan(scan_step, (row_max, row_sum, weighted), stacked)[0]  20.3 us
    reduce_scatter x1, waiting for transfers between devices, shards(): lax.psum_scatter(partial_out.astype(jnp.bfloat16), 'tp', scatter_dimensio...  12.8 us
  transfers between devices with their start and end apart: 9, of which 8 were waited for; matrix products, arithmetic and copies ran while one was open for 16% of the time, Pallas kernels for 0%

commit v1 on v0

--- a/solution.py
+++ b/solution.py
@@ -3,6 +3,8 @@
 import jax
 import jax.numpy as jnp
 from jax import lax
+from jax.experimental import pallas as pl
+from jax.experimental.pallas import tpu as pltpu
 from jax.sharding import PartitionSpec as P
 
 HD = 128
@@ -60,6 +62,242 @@
     shaped = projected.reshape(row_count, -1, HD)
     inverse = lax.rsqrt(jnp.mean(jnp.square(shaped), axis=2, keepdims=True) + EPSILON)
     return shaped * inverse * head_gain
+
+
+def plain_branch(
+    modulated, listed_rows, key_cache, value_cache, text_keys, text_values,
+    query_weight, key_weight, value_weight, out_weight, query_gain, key_gain,
+    token_req, own_tokens, own_request,
+):
+    tile_rows = modulated.shape[0]
+    listed_x = modulated[listed_rows]
+    local_width = key_cache.shape[1]
+    local_heads = local_width // HD
+    gathered_q, gathered_k, gathered_v, gathered_out = (
+        lax.all_gather(query_weight, "seq", axis=0, tiled=True),
+        lax.all_gather(key_weight, "seq", axis=0, tiled=True),
+        lax.all_gather(value_weight, "seq", axis=0, tiled=True),
+        lax.all_gather(out_weight, "seq", axis=0, tiled=True),
+    )
+    query_raw = jnp.dot(modulated, gathered_q, preferred_element_type=jnp.float32)
+    key_raw = jnp.dot(listed_x, gathered_k, preferred_element_type=jnp.float32)
+    value_raw = jnp.dot(listed_x, gathered_v, preferred_element_type=jnp.float32)
+    queries = head_norm(query_raw, query_gain).astype(jnp.bfloat16)
+    fresh_keys = head_norm(key_raw, key_gain).astype(jnp.bfloat16).reshape(-1, local_width)
+    fresh_values = value_raw.astype(jnp.bfloat16)
+    local_keys = key_cache.at[listed_rows].set(fresh_keys)
+    local_values = value_cache.at[listed_rows].set(fresh_values)
+    score_scale = 1.0 / math.sqrt(HD)
+    text_key_tile = lax.dynamic_index_in_dim(text_keys, own_request, 0, keepdims=False).reshape(
+        -1, local_heads, HD
+    )
+    text_value_tile = lax.dynamic_index_in_dim(text_values, own_request, 0, keepdims=False).reshape(
+        -1, local_heads, HD
+    )
+    text_scores = (
+        jnp.einsum("qhd,khd->hqk", queries, text_key_tile, preferred_element_type=jnp.float32)
+        * score_scale
+    )
+    row_max = jnp.max(text_scores, axis=2)
+    text_exp = jnp.exp(text_scores - row_max[..., None])
+    row_sum = jnp.sum(text_exp, axis=2)
+    weighted = jnp.einsum(
+        "hqk,khd->hqd",
+        text_exp.astype(jnp.bfloat16),
+        text_value_tile,
+        preferred_element_type=jnp.float32,
+    )
+
+    def attend(state_now, key_tile, value_tile, key_owner):
+        old_max, old_sum, old_weighted = state_now
+        allowed = (key_owner[None, :] == own_tokens[:, None]) & (own_tokens[:, None] >= 0)
+        key_heads = key_tile.reshape(-1, local_heads, HD)
+        value_heads = value_tile.reshape(-1, local_heads, HD)
+        scores = (
+            jnp.einsum("qhd,khd->hqk", queries, key_heads, preferred_element_type=jnp.float32)
+            * score_scale
+        )
+        scores = jnp.where(allowed[None], scores, -jnp.inf)
+        new_max = jnp.maximum(old_max, jnp.max(scores, axis=2))
+        shrink = jnp.exp(old_max - new_max)
+        exp_scores = jnp.exp(scores - new_max[..., None])
+        new_sum = old_sum * shrink + jnp.sum(exp_scores, axis=2)
+        new_weighted = old_weighted * shrink[..., None] + jnp.einsum(
+            "hqk,khd->hqd",
+            exp_scores.astype(jnp.bfloat16),
+            value_heads,
+            preferred_element_type=jnp.float32,
+        )
+        return (new_max, new_sum, new_weighted)
+
+    pieces = (
+        lax.all_gather(local_keys, "seq", axis=0, tiled=True),
+        lax.all_gather(local_values, "seq", axis=0, tiled=True),
+    )
+    length = pieces[0].shape[0]
+    key_owner = token_req
+    key_block = 1024
+    block_count = length // key_block
+    stacked = (
+        pieces[0].reshape(block_count, key_block, -1),
+        pieces[1].reshape(block_count, key_block, -1),
+        key_owner.reshape(block_count, key_block),
+    )
+
+    def scan_step(state_mid, blocks):
+        return (attend(state_mid, blocks[0], blocks[1], blocks[2]), None)
+
+    row_max, row_sum, weighted = lax.scan(scan_step, (row_max, row_sum, weighted), stacked)[0]
+    attended = (
+        jnp.transpose(weighted / row_sum[..., None], (1, 0, 2))
+        .reshape(tile_rows, local_width)
+        .astype(jnp.bfloat16)
+    )
+    partial_out = lax.dot_general(
+        attended, gathered_out, (((1,), (1,)), ((), ())), preferred_element_type=jnp.float32
+    )
+    reduced = lax.psum_scatter(
+        partial_out.astype(jnp.bfloat16), "tp", scatter_dimension=1, tiled=True
+    ).astype(jnp.float32)
+    return reduced
+
+
+GROUP = 4
+
+
+def group_size(seq_count, local_heads):
+    if seq_count % GROUP == 0 and local_heads % GROUP == 0 and seq_count // GROUP == 4:
+        return GROUP
+    return 1
+
+
+def attention_kernel(
+    request_ref, place_ref, q_ref, k_ref, v_ref, tk_ref, tv_ref, key_req_ref, tok_req_ref, o_ref
+):
+    scale = 1.0 / math.sqrt(HD)
+    q = q_ref[...]
+    dims = (((1,), (1,)), ((), ()))
+    s_text = lax.dot_general(q, tk_ref[0], dims, preferred_element_type=jnp.float32) * scale
+    s_img = lax.dot_general(q, k_ref[...], dims, preferred_element_type=jnp.float32) * scale
+    own = tok_req_ref[...]
+    allowed = (key_req_ref[...] == own) & (own >= 0)
+    s_img = jnp.where(allowed, s_img, -jnp.inf)
+    top = jnp.maximum(
+        jnp.max(s_text, axis=1, keepdims=True), jnp.max(s_img, axis=1, keepdims=True)
+    )
+    e_text = jnp.exp(s_text - top)
+    e_img = jnp.exp(s_img - top)
+    total = jnp.sum(e_text, axis=1, keepdims=True) + jnp.sum(e_img, axis=1, keepdims=True)
+    acc = jnp.dot(e_text.astype(jnp.bfloat16), tv_ref[0], preferred_element_type=jnp.float32)
+    acc += jnp.dot(e_img.astype(jnp.bfloat16), v_ref[...], preferred_element_type=jnp.float32)
+    o_ref[...] = (acc / total).astype(jnp.bfloat16)
+
+
+def attention(queries, keys, values, text_keys, text_values, requests, place, token_req, own_req):
+    rows, width = queries.shape
+    length = keys.shape[0]
+    text = text_keys.shape[1]
+    heads = width // HD
+    tiles = requests.shape[0]
+    tile_rows = rows // tiles
+    grid_spec = pltpu.PrefetchScalarGridSpec(
+        num_scalar_prefetch=2,
+        grid=(heads, tiles),
+        in_specs=[
+            pl.BlockSpec((tile_rows, HD), lambda h, t, req, pos: (t, h)),
+            pl.BlockSpec((length, HD), lambda h, t, req, pos: (0, h)),
+            pl.BlockSpec((length, HD), lambda h, t, req, pos: (0, h)),
+            pl.BlockSpec((1, text, HD), lambda h, t, req, pos: (req[t], 0, pos[0] * heads + h)),
+            pl.BlockSpec((1, text, HD), lambda h, t, req, pos: (req[t], 0, pos[0] * heads + h)),
+            pl.BlockSpec((1, length), lambda h, t, req, pos: (0, 0)),
+            pl.BlockSpec((tile_rows, 1), lambda h, t, req, pos: (t, 0)),
+        ],
+        out_specs=pl.BlockSpec((tile_rows, HD), lambda h, t, req, pos: (t, h)),
+    )
+    return pl.pallas_call(
+        attention_kernel,
+        grid_spec=grid_spec,
+        out_shape=jax.ShapeDtypeStruct((rows, width), jnp.bfloat16),
+        compiler_params=pltpu.CompilerParams(vmem_limit_bytes=32 * 1024 * 1024),
+        cost_estimate=pl.CostEstimate(
+            flops=4 * rows * width * (length + text),
+            bytes_accessed=8 * length * width,
+            transcendentals=rows * heads * (length + text),
+        ),
+    )(
+        requests, place, queries, keys, values, text_keys, text_values,
+        token_req.reshape(1, -1), own_req.reshape(-1, 1),
+    )
+
+
+def grouped_branch(
+    group, modulated, listed_rows, key_cache, value_cache, text_keys, text_values,
+    query_weight, key_weight, value_weight, out_weight, query_gain, key_gain,
+    token_req, mod_req,
+):
+    tile_rows, model = modulated.shape
+    seq_count = lax.axis_size("seq")
+    seq_index = lax.axis_index("seq")
+    lines = seq_count // group
+    place = lax.rem(seq_index, group)
+    first_tile = seq_index - place
+    width = key_cache.shape[1] // group
+    depth = query_weight.shape[0]
+    inner = [[z * group + p for p in range(group)] for z in range(lines)]
+    outer = [[z * group + p for z in range(lines)] for p in range(group)]
+
+    def spread(block):
+        return lax.all_to_all(
+            block, "seq", split_axis=1, concat_axis=0, axis_index_groups=inner, tiled=True
+        )
+
+    def line_gather(block):
+        return lax.all_gather(block, "seq", axis=0, axis_index_groups=outer, tiled=True)
+
+    row_index = jnp.arange(tile_rows, dtype=jnp.int32)
+    is_listed = jnp.any(row_index[:, None] == listed_rows[None, :], axis=1)
+    flagged = jnp.concatenate(
+        [
+            modulated,
+            jnp.broadcast_to(is_listed[:, None], (tile_rows, HD)).astype(jnp.bfloat16),
+        ],
+        axis=1,
+    )
+    everyone = lax.all_gather(flagged, "seq", axis=0, axis_index_groups=inner, tiled=True)
+    tokens = everyone[:, :model]
+    fresh = everyone[:, model : model + 1] > 0
+    key_w = line_gather(spread(key_weight))
+    value_w = line_gather(spread(value_weight))
+    query_w = line_gather(spread(query_weight))
+    key_tiles = spread(key_cache)
+    value_tiles = spread(value_cache)
+    key_raw = jnp.dot(tokens, key_w, preferred_element_type=jnp.float32)
+    fresh_keys = head_norm(key_raw, key_gain).astype(jnp.bfloat16).reshape(-1, width)
+    keys = line_gather(jnp.where(fresh, fresh_keys, key_tiles))
+    value_raw = jnp.dot(tokens, value_w, preferred_element_type=jnp.float32)
+    values = line_gather(jnp.where(fresh, value_raw.astype(jnp.bfloat16), value_tiles))
+    query_raw = jnp.dot(tokens, query_w, preferred_element_type=jnp.float32)
+    queries = head_norm(query_raw, query_gain).astype(jnp.bfloat16).reshape(-1, width)
+    out_w = line_gather(out_weight)
+    requests = lax.dynamic_slice_in_dim(mod_req, first_tile, group)
+    own_req = lax.dynamic_slice_in_dim(token_req, first_tile * tile_rows, group * tile_rows)
+    attended = attention(
+        queries, keys, values, text_keys, text_values, requests, place.reshape(1),
+        token_req, own_req,
+    )
+    attended = lax.all_gather(attended, "seq", axis=1, axis_index_groups=inner, tiled=True)
+    partial_out = lax.dot_general(
+        attended, out_w, (((1,), (1,)), ((), ())), preferred_element_type=jnp.float32
+    )
+    halves = lax.psum_scatter(
+        partial_out.astype(jnp.bfloat16), "tp", scatter_dimension=1, tiled=True
+    )
+    own = lax.all_to_all(
+        halves.reshape(group, tile_rows, -1), "seq", split_axis=0, concat_axis=0,
+        axis_index_groups=inner, tiled=True,
+    )
+    own = own.reshape(group, tile_rows, -1, depth)
+    return jnp.transpose(own, (1, 2, 0, 3)).reshape(tile_rows, -1).astype(jnp.float32)
 
 
 def shards(
@@ -110,96 +348,20 @@
     modulated = (
         (1.0 + choose_row(mod_scale))[None, :] * normed + choose_row(mod_shift)[None, :]
     ).astype(jnp.bfloat16)
-    listed_rows = listed[0]
-    listed_x = modulated[listed_rows]
     local_width = key_cache.shape[1]
-    local_heads = local_width // HD
-    gathered_q, gathered_k, gathered_v, gathered_out = (
-        lax.all_gather(query_weight, "seq", axis=0, tiled=True),
-        lax.all_gather(key_weight, "seq", axis=0, tiled=True),
-        lax.all_gather(value_weight, "seq", axis=0, tiled=True),
-        lax.all_gather(out_weight, "seq", axis=0, tiled=True),
-    )
-    query_raw = jnp.dot(modulated, gathered_q, preferred_element_type=jnp.float32)
-    key_raw = jnp.dot(listed_x, gathered_k, preferred_element_type=jnp.float32)
-    value_raw = jnp.dot(listed_x, gathered_v, preferred_element_type=jnp.float32)
-    queries = head_norm(query_raw, query_gain).astype(jnp.bfloat16)
-    fresh_keys = head_norm(key_raw, key_gain).astype(jnp.bfloat16).reshape(-1, local_width)
-    fresh_values = value_raw.astype(jnp.bfloat16)
-    local_keys = key_cache.at[listed_rows].set(fresh_keys)
-    local_values = value_cache.at[listed_rows].set(fresh_values)
-    score_scale = 1.0 / math.sqrt(HD)
-    text_key_tile = lax.dynamic_index_in_dim(text_keys, own_request, 0, keepdims=False).reshape(
-        -1, local_heads, HD
-    )
-    text_value_tile = lax.dynamic_index_in_dim(text_values, own_request, 0, keepdims=False).reshape(
-        -1, local_heads, HD
-    )
-    text_scores = (
-        jnp.einsum("qhd,khd->hqk", queries, text_key_tile, preferred_element_type=jnp.float32)
-        * score_scale
-    )
-    row_max = jnp.max(text_scores, axis=2)
-    text_exp = jnp.exp(text_scores - row_max[..., None])
-    row_sum = jnp.sum(text_exp, axis=2)
-    weighted = jnp.einsum(
-        "hqk,khd->hqd",
-        text_exp.astype(jnp.bfloat16),
-        text_value_tile,
-        preferred_element_type=jnp.float32,
-    )
-
-    def attend(state_now, key_tile, value_tile, key_owner):
-        old_max, old_sum, old_weighted = state_now
-        allowed = (key_owner[None, :] == own_tokens[:, None]) & (own_tokens[:, None] >= 0)
-        key_heads = key_tile.reshape(-1, local_heads, HD)
-        value_heads = value_tile.reshape(-1, local_heads, HD)
-        scores = (
-            jnp.einsum("qhd,khd->hqk", queries, key_heads, preferred_element_type=jnp.float32)
-            * score_scale
+    group = group_size(seq_count, local_width // HD)
+    if group > 1:
+        reduced = grouped_branch(
+            group, modulated, listed[0], key_cache, value_cache, text_keys, text_values,
+            query_weight, key_weight, value_weight, out_weight, query_gain, key_gain,
+            token_req, mod_req,
         )
-        scores = jnp.where(allowed[None], scores, -jnp.inf)
-        new_max = jnp.maximum(old_max, jnp.max(scores, axis=2))
-        shrink = jnp.exp(old_max - new_max)
-        exp_scores = jnp.exp(scores - new_max[..., None])
-        new_sum = old_sum * shrink + jnp.sum(exp_scores, axis=2)
-        new_weighted = old_weighted * shrink[..., None] + jnp.einsum(
-            "hqk,khd->hqd",
-            exp_scores.astype(jnp.bfloat16),
-            value_heads,
-            preferred_element_type=jnp.float32,
+    else:
+        reduced = plain_branch(
+            modulated, listed[0], key_cache, value_cache, text_keys, text_values,
+            query_weight, key_weight, value_weight, out_weight, query_gain, key_gain,
+            token_req, own_tokens, own_request,
         )
-        return (new_max, new_sum, new_weighted)
-
-    pieces = (
-        lax.all_gather(local_keys, "seq", axis=0, tiled=True),
-        lax.all_gather(local_values, "seq", axis=0, tiled=True),
-    )
-    length = pieces[0].shape[0]
-    key_owner = token_req
-    key_block = 1024
-    block_count = length // key_block
-    stacked = (
-        pieces[0].reshape(block_count, key_block, -1),
-        pieces[1].reshape(block_count, key_block, -1),
-        key_owner.reshape(block_count, key_block),
-    )
-
-    def scan_step(state_mid, blocks):
-        return (attend(state_mid, blocks[0], blocks[1], blocks[2]), None)
-
-    row_max, row_sum, weighted = lax.scan(scan_step, (row_max, row_sum, weighted), stacked)[0]
-    attended = (
-        jnp.transpose(weighted / row_sum[..., None], (1, 0, 2))
-        .reshape(tile_rows, local_width)
-        .astype(jnp.bfloat16)
-    )
-    partial_out = lax.dot_general(
-        attended, gathered_out, (((1,), (1,)), ((), ())), preferred_element_type=jnp.float32
-    )
-    reduced = lax.psum_scatter(
-        partial_out.astype(jnp.bfloat16), "tp", scatter_dimension=1, tiled=True
-    ).astype(jnp.float32)
     col_count = reduced.shape[1]
     hidden_cols = lax.dynamic_slice_in_dim(hidden_f32, tp_index * col_count, col_count, 1)
     gate_cols = lax.dynamic_slice_in_dim(choose_row(mod_gate), tp_index * col_count, col_count)

time: 420 us -> 344 us (0.82)
  waiting for transfers between devices: 300 us -> 217 us
  blocking collectives: 5.35 us -> 34.5 us
  matrix products: 36.9 us -> 17 us
  local copies, waits for them, and re-layouts: 39.6 us -> 19.9 us
  starting transfers between devices: 7.89 us -> 19.6 us
  Pallas kernels: 0 us -> 9.03 us
    all_gather x6 -> x8, waiting for transfers between devices: 282 us -> 187 us  [the longest x6 138 us: line_gather(): lax.all_gather(block, 'seq', axis=0, axis_index_groups=outer, tiled=True)]
    all_to_all x0 -> x3, blocking collectives: none -> 29.5 us  [spread(): lax.all_to_all(block, 'seq', split_axis=1, concat_axis=0, axis_index_grou...]
    dynamic_slice x9 -> x2, local copies, waits for them, and re-layouts: 23.1 us -> 0.15 us  [the longest x1 0.08 us: grouped_branch(): requests = lax.dynamic_slice_in_dim(mod_req, first_tile, group)]
    dot_general x10 -> x4, matrix products: 33.2 us -> 13.6 us  [the longest x1 4.11 us: grouped_branch(): value_raw = jnp.dot(tokens, value_w, preferred_element_type=jnp.float32)]
    unnamed x7 -> x10, waiting for transfers between devices: 2.63 us -> 18 us
    reduce_scatter x1 -> x0, waiting for transfers between devices: 12.8 us -> none  [shards(): lax.psum_scatter(partial_out.astype(jnp.bfloat16), 'tp', scatter_dimensio...]
    all_to_all x0 -> x3, starting transfers between devices: none -> 12.6 us  [the longest x2 8.38 us: spread(): lax.all_to_all(block, 'seq', split_axis=1, concat_axis=0, axis_index_grou...]
    all_to_all x0 -> x3, waiting for transfers between devices: none -> 9.91 us  [the longest x2 5.54 us: spread(): lax.all_to_all(block, 'seq', split_axis=1, concat_axis=0, axis_index_grou...]
  transfers between devices with their start and end apart: 9 -> 14, of which waited for: 8 -> 12; matrix products, arithmetic and copies ran while one was open for 16% -> 8% of each run, Pallas kernels for 0% -> 3%
where the time goes in v1:
time: 344 us; the launch traced here: 342 us
  waiting for transfers between devices  217 us (63%)
  blocking collectives  34.5 us (10%)
  local copies, waits for them, and re-layouts  19.9 us (6%)
  starting transfers between devices  19.6 us (6%)
  matrix products  17 us (5%)
  between operations  16.8 us (5%)
  Pallas kernels  9.03 us (3%)
  other arithmetic  8.67 us (3%)
    all_gather x6, waiting for transfers between devices, line_gather(): lax.all_gather(block, 'seq', axis=0, axis_index_groups=outer, tiled=True)  138 us
    all_gather x1, waiting for transfers between devices, grouped_branch(): lax.all_gather(flagged, 'seq', axis=0, axis_index_groups=inner, tiled=True)  30.7 us
    all_to_all x3, blocking collectives, spread(): lax.all_to_all(block, 'seq', split_axis=1, concat_axis=0, axis_index_grou...  29.5 us
    all_gather x1, waiting for transfers between devices, grouped_branch(): lax.all_gather(attended, 'seq', axis=1, axis_index_groups=inner, tiled=True)  18.4 us
    unnamed x10, waiting for transfers between devices  18 us
    unnamed x48, local copies, waits for them, and re-layouts  12.1 us
    pallas_call x1, Pallas kernels, attention(): pl.pallas_call(attention_kernel, grid_spec=grid_spec, out_shape=jax.Shape...  9.03 us
    all_to_all x2, starting transfers between devices, spread(): lax.all_to_all(block, 'seq', split_axis=1, concat_axis=0, axis_index_grou...  8.38 us
  transfers between devices with their start and end apart: 14, of which 12 were waited for; matrix products, arithmetic and copies ran while one was open for 8% of the time, Pallas kernels for 3%

profile of v1, /device:TPU:1, one launch (start us, length us, event | category | flops | bytes accessed | tf_op | source)
XLA Modules:
  0.0 342.0 jit_solution(803868547993428861)
XLA Ops:
  7.2 1.8 copy.115
  9.0 4.3 %all-to-all-start.1 = ((bf16[192,4,256]{2,0,1:T(8,128)(2,1)}), bf16[192,4,256]{2,0,1:T(8,128)(2,1)S(1)}, u32[]{:S(2)}, u32[]{:S(2)}) async-start(bf16[192,4,256]{2,0,1:T(8,128)(2,1)} %bitcast.117), calls=%async_computation.1 | async-start | bytes 786432 | tf_op jit(solution)/shard_map/all_to_all | solution.py:250
  14.2 5.5 %all-to-all-done.1 = bf16[192,4,256]{2,0,1:T(8,128)(2,1)S(1)} async-done(((bf16[192,4,256]{2,0,1:T(8,128)(2,1)}), bf16[192,4,256]{2,0,1:T(8,128)(2,1)S(1)}, u32[]{:S(2)}, u32[]{:S(2)}) %all-to-all-start.1) | async-done | bytes 393248 | tf_op jit(solution)/shard_map/all_to_all | solution.py:250
  19.7 0.7 copy-done.5
  21.7 0.7 fusion.25
  22.4 0.7 fusion.23
  23.2 1.7 add_convert_fusion
  24.9 1.0 pad_maximum_fusion
  26.0 10.9 %all_to_all.100 = bf16[192,4,256]{2,0,1:T(8,128)(2,1)} all-to-all(bf16[192,4,256]{2,0,1:T(8,128)(2,1)S(1)} %bitcast.132), channel_id=1, replica_groups={{0,2,4,6},{8,10,12,14},{16,18,20,22},{24,26,28,30},{1,3,5,7},{9,11,13,1..., dimensions={1} | all-to-all | bytes 786432 | tf_op jit(solution)/shard_map/all_to_all | solution.py:250
  37.0 10.5 %all_to_all.101 = bf16[192,4,256]{2,0,1:T(8,128)(2,1)} all-to-all(bf16[192,4,256]{2,0,1:T(8,128)(2,1)S(1)} %bitcast.133), channel_id=1, replica_groups={{0,2,4,6},{8,10,12,14},{16,18,20,22},{24,26,28,30},{1,3,5,7},{9,11,13,1..., dimensions={1} | all-to-all | bytes 786432 | tf_op jit(solution)/shard_map/all_to_all | solution.py:250
  47.6 0.7 copy.118
  48.3 4.1 %all-to-all-start.2 = ((bf16[128,4,256]{2,0,1:T(8,128)(2,1)}), bf16[128,4,256]{2,0,1:T(8,128)(2,1)S(1)}, u32[]{:S(2)}, u32[]{:S(2)}) async-start(bf16[128,4,256]{2,0,1:T(8,128)(2,1)} %bitcast.120), calls=%async_computation.2 | async-start | bytes 524288 | tf_op jit(solution)/shard_map/all_to_all | solution.py:250
  52.4 6.5 %all-gather.13.cloned.1.call-done = bf16[3072,256]{1,0:T(8,128)(2,1)} async-done(((bf16[768,256]{1,0:T(8,128)(2,1)}), bf16[3072,256]{1,0:T(8,128)(2,1)}) %all-gather.13.cloned.1.call-update) | async-done | bytes 1572880 | tf_op jit(solution)/shard_map/all_gather | solution.py:255
  59.0 30.7 %all-gather.9.cloned.1.call-done = bf16[512,3200]{0,1:T(8,128)(2,1)} async-done(((bf16[128,3200]{0,1:T(8,128)(2,1)}), bf16[512,3200]{0,1:T(8,128)(2,1)}) %all-gather.9.cloned.1.call-update) | async-done | bytes 3276816 | tf_op jit(solution)/shard_map/all_gather | solution.py:266
  89.7 3.4 bitcast_reduce_fusion
  93.4 0.7 compare_reduce_fusion
  94.8 0.9 fusion.19
  95.7 8.0 %all_to_all.102 = bf16[128,4,256]{2,0,1:T(8,128)(2,1)S(1)} all-to-all(bf16[128,4,256]{2,0,1:T(8,128)(2,1)S(1)} %bitcast.134), channel_id=1, replica_groups={{0,2,4,6},{8,10,12,14},{16,18,20,22},{24,26,28,30},{1,3,5,7},{9,11,13,1..., dimensions={1} | all-to-all | bytes 524288 | tf_op jit(solution)/shard_map/all_to_all | solution.py:250
  103.8 24.0 %all-gather.17.cloned.1.call-done = bf16[3072,256]{1,0:T(8,128)(2,1)} async-done(((bf16[768,256]{1,0:T(8,128)(2,1)}), bf16[3072,256]{1,0:T(8,128)(2,1)}) %all-gather.17.cloned.1.call-update) | async-done | bytes 1572880 | tf_op jit(solution)/shard_map/all_gather | solution.py:255
  127.8 4.1 %fusion.10 = bf16[512,256]{1,0:T(8,128)(2,1)} fusion(bf16[512,256]{1,0:T(8,128)(2,1)S(1)} %bitcast.150, bf16[3072,256]{1,0:T(8,128)(2,1)} %all-gather.17.cloned.1.call-done, bf16[512,3200]{0,1:T(8,128)(2,1)} %all-gather.9.cloned.1.call-done, pred[512]{0:T(512)(128)(4,1)S(1)} %compare_reduce_fusion), kind=kOutput, calls=%fused_computation.14 | convolution fusion | flops 805568512 | bytes 5243392 | tf_op jit(solution)/shard_map/dot_general | solution.py:277
  132.0 0.7 all-gather.23.cloned.1.call-update
  133.5 31.8 %all-gather.11.cloned.1.call-done = bf16[3072,256]{1,0:T(8,128)(2,1)} async-done(((bf16[768,256]{1,0:T(8,128)(2,1)}), bf16[3072,256]{1,0:T(8,128)(2,1)}) %all-gather.11.cloned.1.call-update) | async-done | bytes 1572880 | tf_op jit(solution)/shard_map/all_gather | solution.py:255
  165.2 3.4 bitcast_reduce_fusion.1
  169.0 0.6 mul.115
  169.7 24.3 %all-gather.15.cloned.1.call-done.k_ref = bf16[2048,256]{1,0:T(8,128)(2,1)} async-done(((bf16[512,256]{1,0:T(8,128)(2,1)}), bf16[2048,256]{1,0:T(8,128)(2,1)}) %all-gather.15.cloned.1.call-update) | async-done | bytes 1048592 | tf_op jit(solution)/shard_map/all_gather | solution.py:255
  194.1 29.5 %all-gather.19.cloned.1.call-done.v_ref = bf16[2048,256]{1,0:T(8,128)(2,1)} async-done(((bf16[512,256]{1,0:T(8,128)(2,1)}), bf16[2048,256]{1,0:T(8,128)(2,1)}) %all-gather.19.cloned.1.call-update) | async-done | bytes 1048592 | tf_op jit(solution)/shard_map/all_gather | solution.py:255
  223.5 2.2 copy-done.1
  225.7 2.2 copy-done.2
  227.9 1.2 copy-done.3
  229.1 1.2 copy-done.4
  230.3 9.0 %shard_map.220 = bf16[512,256]{1,0:T(8,128)(2,1)} custom-call(s32[4]{0:T(128)S(1)} %dynamic_slice.30.request_ref, s32[1]{0:T(128)} %bitcast.3.place_ref, bf16[512,256]{1,0:T(8,128)(2,1)S(1)} %fusion.18.q_ref, bf16[2048,256]{1,0:T(8,128)(2,1)S(1)} %copy-done.3, bf16[2048,256]{1,0:T(8,128)(2,1)S(1)} %copy-done.4, bf16[4,512,1024]{2,1,0:T(8,128)(2,1)S(1)} %copy-done.1, ...), custom_call_target="tpu_custom_call" | custom-call | flops 1342177280 | bytes 4194304 | tf_op jit(solution)/shard_map/pallas_call | solution.py:217
  239.4 22.3 %all-gather.23.cloned.1.call-done = bf16[768,1024]{1,0:T(8,128)(2,1)} async-done(((bf16[192,1024]{1,0:T(8,128)(2,1)}), bf16[768,1024]{1,0:T(8,128)(2,1)}) %all-gather.23.cloned.1.call-update) | async-done | bytes 1572880 | tf_op jit(solution)/shard_map/all_gather | solution.py:255
  261.7 18.4 %all-gather.21.cloned.1.call-done = bf16[512,1024]{1,0:T(8,128)(2,1)} async-done(((bf16[512,256]{1,0:T(8,128)(2,1)}), bf16[512,1024]{1,0:T(8,128)(2,1)}) %all-gather.21.cloned.1.call-update) | async-done | bytes 1048592 | tf_op jit(solution)/shard_map/all_gather | solution.py:288
  280.1 2.7 convolution_convert_fusion
  282.9 1.2 copy.96
  284.1 17.2 %reduce-scatter.4.cloned.1.call-done = bf16[384,512]{1,0:T(8,128)(2,1)} async-done(((bf16[768,512]{1,0:T(8,128)(2,1)}), bf16[384,512]{1,0:T(8,128)(2,1)}) %reduce-scatter.4.cloned.1.call-update) | async-done | bytes 393232
  301.3 1.9 copy.97
  303.2 4.2 %all-to-all-start.5 = ((bf16[4,128,384]{2,1,0:T(8,128)(2,1)}), bf16[4,128,384]{2,1,0:T(8,128)(2,1)S(1)}, u32[]{:S(2)}, u32[]{:S(2)}) async-start(bf16[4,128,384]{2,1,0:T(8,128)(2,1)} %bitcast.26), calls=%async_computation.5 | async-start | bytes 786432 | tf_op jit(solution)/shard_map/all_to_all | solution.py:295
  307.4 0.7 fusion.27
  308.5 1.2 select_reduce_fusion.1
  309.6 4.4 %all-to-all-done.5 = bf16[4,128,384]{2,1,0:T(8,128)(2,1)S(1)} async-done(((bf16[4,128,384]{2,1,0:T(8,128)(2,1)}), bf16[4,128,384]{2,1,0:T(8,128)(2,1)S(1)}, u32[]{:S(2)}, u32[]{:S(2)}) %all-to-all-start.5) | async-done | bytes 393248 | tf_op jit(solution)/shard_map/all_to_all | solution.py:295
  314.8 5.0 %psum.7 = bf16[128,64]{0,1:T(8,128)(2,1)S(1)} all-reduce(bf16[128,64]{0,1:T(8,128)(2,1)S(1)} %convolution_convert_fusion.1), channel_id=1, replica_groups=mesh['seq'=16,'tp'=2] {'tp'}, use_global_device_ids=true, to_apply=%region_9.10 | all-reduce | flops 8192 | bytes 32768 | tf_op jit(solution)/shard_map/psum | solution.py:369
  319.7 1.3 select_convert_fusion
  321.1 4.7 %collective-permute-start.1 = (bf16[64,64]{0,1:T(8,128)(2,1)S(1)}, bf16[64,64]{0,1:T(8,128)(2,1)S(1)}, u32[]{:S(2)}, u32[]{:S(2)}) collective-permute-start(bf16[64,64]{0,1:T(8,128)(2,1)S(1)} %get-tuple-element.29), channel_id=1, source_target_pairs={{2,0},{4,2},{6,4},{8,6},{10,8},{12,10},{14,12},{16,14},{18,16},{20... | collective-permute-start | bytes 24584 | tf_op jit(solution)/shard_map/ppermute | solution.py:28
  329.2 0.9 copy.95
  330.1 1.9 collective-permute-start
  332.1 1.1 collective-permute-done
  334.5 0.9 fusion.9
  (111 shorter events, 7.8 us)
Async XLA Ops:
  7.2 307.4 %copy-start = (bf16[1536,64]{0,1:T(8,128)(2,1)S(1)}, bf16[1536,64]{0,1:T(8,128)(2,1)}, u32[]{:S(2)}) copy-start(bf16[1536,64]{0,1:T(8,128)(2,1)} %param.36) | copy-start | bytes 589828
  7.2 6.1 %copy-start.15 = (s32[16]{0:T(128)S(1)}, s32[16]{0:T(128)}, u32[]{:S(2)}) copy-start(s32[16]{0:T(128)} %param.39) | copy-start | bytes 196
  7.2 6.1 %copy-start.6 = (bf16[128,3072]{1,0:T(8,128)(2,1)S(1)}, bf16[128,3072]{1,0:T(8,128)(2,1)}, u32[]{:S(2)}) copy-start(bf16[128,3072]{1,0:T(8,128)(2,1)} %param.21) | copy-start | bytes 2359300
  9.0 10.7 %all-to-all-start.1 = ((bf16[192,4,256]{2,0,1:T(8,128)(2,1)}), bf16[192,4,256]{2,0,1:T(8,128)(2,1)S(1)}, u32[]{:S(2)}, u32[]{:S(2)}) async-start(bf16[192,4,256]{2,0,1:T(8,128)(2,1)} %bitcast.117), calls=%async_computation.1 | async-start | bytes 786432 | tf_op jit(solution)/shard_map/all_to_all | solution.py:250
  13.3 7.2 %copy-start.17 = (s32[1,32]{1,0:T(1,128)S(1)}, s32[1,32]{1,0:T(1,128)}, u32[]{:S(2)}) copy-start(s32[1,32]{1,0:T(1,128)} %param.40) | copy-start | bytes 388
  13.3 45.7 %all-gather.13.cloned.1.call-start = ((), (), s32[]{:S(2)}) async-start(), calls=%async_computation.9 | async-start | bytes 1966080 | tf_op jit(solution)/shard_map/all_gather | solution.py:255
  13.3 8.3 %copy-start.11 = (f32[4,3072]{1,0:T(4,128)S(1)}, f32[4,3072]{1,0:T(4,128)}, u32[]{:S(2)}) copy-start(f32[4,3072]{1,0:T(4,128)} %param.34) | copy-start | bytes 147460
  13.4 9.1 %copy-start.12 = (f32[4,3072]{1,0:T(4,128)S(1)}, f32[4,3072]{1,0:T(4,128)}, u32[]{:S(2)}) copy-start(f32[4,3072]{1,0:T(4,128)} %param.33) | copy-start | bytes 147460
  19.7 0.7 copy-start.5
  20.5 69.2 %all-gather.9.cloned.1.call-start = ((), (), s32[]{:S(2)}) async-start(), calls=%async_computation.7 | async-start | bytes 4096000 | tf_op jit(solution)/shard_map/all_gather | solution.py:266
  24.9 1.1 copy-start.7
  25.8 11.2 %copy-start.8 = (bf16[192,1024]{1,0:T(8,128)(2,1)S(1)}, bf16[192,1024]{1,0:T(8,128)(2,1)}, u32[]{:S(2)}) copy-start(bf16[192,1024]{1,0:T(8,128)(2,1)} %param.27) | copy-start | bytes 1179652
  25.9 102.0 %all-gather.17.cloned.1.call-start = ((), (), s32[]{:S(2)}) async-start(), calls=%async_computation.11 | async-start | bytes 1966080 | tf_op jit(solution)/shard_map/all_gather | solution.py:255
  26.0 21.6 %copy-start.9 = (bf16[128,1024]{1,0:T(8,128)(2,1)S(1)}, bf16[128,1024]{1,0:T(8,128)(2,1)}, u32[]{:S(2)}) copy-start(bf16[128,1024]{1,0:T(8,128)(2,1)} %param.23) | copy-start | bytes 786436
  36.9 15.5 %copy-start.18 = (f32[128]{0:T(128)S(1)}, f32[128]{0:T(128)}, u32[]{:S(2)}) copy-start(f32[128]{0:T(128)} %param.32) | copy-start | bytes 1540
  37.0 128.3 %all-gather.11.cloned.1.call-start = ((), (), s32[]{:S(2)}) async-start(), calls=%async_computation.8 | async-start | bytes 1966080 | tf_op jit(solution)/shard_map/all_gather | solution.py:255
  48.3 45.9 %all-to-all-start.2 = ((bf16[128,4,256]{2,0,1:T(8,128)(2,1)}), bf16[128,4,256]{2,0,1:T(8,128)(2,1)S(1)}, u32[]{:S(2)}, u32[]{:S(2)}) async-start(bf16[128,4,256]{2,0,1:T(8,128)(2,1)} %bitcast.120), calls=%async_computation.2 | async-start | bytes 524288 | tf_op jit(solution)/shard_map/all_to_all | solution.py:250
  52.4 141.6 %all-gather.15.cloned.1.call-start = ((), (), s32[]{:S(2)}) async-start(), calls=%async_computation.10 | async-start | bytes 1310720 | tf_op jit(solution)/shard_map/all_gather | solution.py:255
  93.3 2.4 copy-start.10
  95.7 127.9 %all-gather.19.cloned.1.call-start = ((), (), s32[]{:S(2)}) async-start(), calls=%async_computation.12 | async-start | bytes 1310720 | tf_op jit(solution)/shard_map/all_gather | solution.py:255
  127.8 5.2 %copy-start.19 = (s32[4]{0:T(128)S(1)}, s32[4]{0:T(128)}, u32[]{:S(2)}) copy-start(s32[4]{0:T(128)} %param.38) | copy-start | bytes 52
  127.8 5.6 %copy-start.20 = (f32[128]{0:T(128)S(1)}, f32[128]{0:T(128)}, u32[]{:S(2)}) copy-start(f32[128]{0:T(128)} %param.31) | copy-start | bytes 1540
  132.0 129.8 %all-gather.23.cloned.1.call-start = ((), (), s32[]{:S(2)}) async-start(), calls=%async_computation.14 | async-start | bytes 1966080 | tf_op jit(solution)/shard_map/all_gather | solution.py:255
  132.7 147.4 %all-gather.21.cloned.1.call-start = ((), (), s32[]{:S(2)}) async-start(), calls=%async_computation.13 | async-start | bytes 1310720 | tf_op jit(solution)/shard_map/all_gather | solution.py:288
  223.5 2.2 copy-start.1
  225.7 2.2 copy-start.2
  227.9 1.2 copy-start.3
  229.1 1.2 copy-start.4
  239.4 61.9 %reduce-scatter.4.cloned.1.call-start = ((), (), s32[]{:S(2)}) async-start(), calls=%async_computation.15 | async-start | bytes 1179648
  284.1 23.4 %copy-start.13 = (f32[4,3072]{1,0:T(4,128)S(1)}, f32[4,3072]{1,0:T(4,128)}, u32[]{:S(2)}) copy-start(f32[4,3072]{1,0:T(4,128)} %param.35) | copy-start | bytes 147460
  303.2 5.3 %copy-start.21 = (s32[4]{0:T(128)S(1)}, s32[4]{0:T(128)}, u32[]{:S(2)}) copy-start(s32[4]{0:T(128)} %param.41) | copy-start | bytes 52
  303.2 10.8 %all-to-all-start.5 = ((bf16[4,128,384]{2,1,0:T(8,128)(2,1)}), bf16[4,128,384]{2,1,0:T(8,128)(2,1)S(1)}, u32[]{:S(2)}, u32[]{:S(2)}) async-start(bf16[4,128,384]{2,1,0:T(8,128)(2,1)} %bitcast.26), calls=%async_computation.5 | async-start | bytes 786432 | tf_op jit(solution)/shard_map/all_to_all | solution.py:295
  314.2 5.5 %copy-start.14 = (f32[128,64]{0,1:T(8,128)S(1)}, f32[128,64]{0,1:T(8,128)}, u32[]{:S(2)}) copy-start(f32[128,64]{0,1:T(8,128)} %param.22) | copy-start | bytes 98308
  321.1 11.0 %collective-permute-start.1 = (bf16[64,64]{0,1:T(8,128)(2,1)S(1)}, bf16[64,64]{0,1:T(8,128)(2,1)S(1)}, u32[]{:S(2)}, u32[]{:S(2)}) collective-permute-start(bf16[64,64]{0,1:T(8,128)(2,1)S(1)} %get-tuple-element.29), channel_id=1, source_target_pairs={{2,0},{4,2},{6,4},{8,6},{10,8},{12,10},{14,12},{16,14},{18,16},{20... | collective-permute-start | bytes 24584 | tf_op jit(solution)/shard_map/ppermute | solution.py:28
  330.1 3.1 collective-permute-start
  333.6 0.9 copy-start.16
Sparse Core Ops, SparseCore 0:
  20.6 38.3 all-gather.12
  60.5 29.0 all-gather.8
  91.2 36.5 all-gather.16
  129.2 35.9 all-gather.10
  167.2 26.7 all-gather.14
  196.1 27.4 all-gather.18
  225.1 36.5 all-gather.22
  263.8 16.2 all-gather.20
  284.2 17.0 reduce-scatter.3

commit v2 on v1

--- a/solution.py
+++ b/solution.py
@@ -166,7 +166,7 @@
 
 
 def group_size(seq_count, local_heads):
-    if seq_count % GROUP == 0 and local_heads % GROUP == 0 and seq_count // GROUP == 4:
+    if seq_count == GROUP * GROUP and seq_count == 2 * local_heads:
         return GROUP
     return 1
 
@@ -230,6 +230,12 @@
     )
 
 
+def interleave(first, second):
+    rows = first.shape[0]
+    both = jnp.stack([first.reshape(rows, -1, HD), second.reshape(rows, -1, HD)], axis=2)
+    return both.reshape(rows, -1)
+
+
 def grouped_branch(
     group, modulated, listed_rows, key_cache, value_cache, text_keys, text_values,
     query_weight, key_weight, value_weight, out_weight, query_gain, key_gain,
@@ -237,67 +243,129 @@
 ):
     tile_rows, model = modulated.shape
     seq_count = lax.axis_size("seq")
+    tp_count = lax.axis_size("tp")
     seq_index = lax.axis_index("seq")
+    tp_index = lax.axis_index("tp")
     lines = seq_count // group
     place = lax.rem(seq_index, group)
-    first_tile = seq_index - place
+    line = seq_index // group
+    core = lax.rem(seq_index, 2)
+    side = place // 2
     width = key_cache.shape[1] // group
     depth = query_weight.shape[0]
+    half_rows = group * tile_rows // 2
     inner = [[z * group + p for p in range(group)] for z in range(lines)]
     outer = [[z * group + p for z in range(lines)] for p in range(group)]
-
-    def spread(block):
-        return lax.all_to_all(
-            block, "seq", split_axis=1, concat_axis=0, axis_index_groups=inner, tiled=True
-        )
+    turns = [
+        [(z * group + p, p * group + (z + k) % group) for z in range(lines) for p in range(group)]
+        for k in range(group)
+    ]
 
     def line_gather(block):
         return lax.all_gather(block, "seq", axis=0, axis_index_groups=outer, tiled=True)
 
-    row_index = jnp.arange(tile_rows, dtype=jnp.int32)
-    is_listed = jnp.any(row_index[:, None] == listed_rows[None, :], axis=1)
-    flagged = jnp.concatenate(
+    moved = jnp.concatenate(
+        [interleave(key_weight, value_weight), interleave(key_cache, value_cache)], axis=0
+    )
+    moved = lax.all_to_all(moved, "seq", split_axis=1, concat_axis=0, tiled=True)
+    moved = moved.reshape(seq_count, -1, HD)
+    head_weight = moved[:, :depth].reshape(-1, HD)
+    head_cache = moved[:, depth:]
+
+    listed_x = jnp.concatenate(
         [
-            modulated,
-            jnp.broadcast_to(is_listed[:, None], (tile_rows, HD)).astype(jnp.bfloat16),
+            modulated[listed_rows],
+            jnp.broadcast_to(listed_rows[:, None], (listed_rows.shape[0], HD)).astype(
+                jnp.bfloat16
+            ),
         ],
         axis=1,
     )
-    everyone = lax.all_gather(flagged, "seq", axis=0, axis_index_groups=inner, tiled=True)
-    tokens = everyone[:, :model]
-    fresh = everyone[:, model : model + 1] > 0
-    key_w = line_gather(spread(key_weight))
-    value_w = line_gather(spread(value_weight))
-    query_w = line_gather(spread(query_weight))
-    key_tiles = spread(key_cache)
-    value_tiles = spread(value_cache)
-    key_raw = jnp.dot(tokens, key_w, preferred_element_type=jnp.float32)
-    fresh_keys = head_norm(key_raw, key_gain).astype(jnp.bfloat16).reshape(-1, width)
-    keys = line_gather(jnp.where(fresh, fresh_keys, key_tiles))
-    value_raw = jnp.dot(tokens, value_w, preferred_element_type=jnp.float32)
-    values = line_gather(jnp.where(fresh, value_raw.astype(jnp.bfloat16), value_tiles))
+    all_listed = lax.all_gather(listed_x, "seq", axis=0, tiled=True)
+    tokens = modulated
+    query_w = line_gather(
+        lax.all_to_all(
+            query_weight, "seq", split_axis=1, concat_axis=0, axis_index_groups=inner, tiled=True
+        )
+    )
+    tokens = lax.all_gather(modulated, "seq", axis=0, axis_index_groups=inner, tiled=True)
+    fresh_raw = jnp.dot(all_listed[:, :model], head_weight, preferred_element_type=jnp.float32)
+    fresh_keys = head_norm(fresh_raw, key_gain).reshape(-1, HD)
+    fresh = jnp.where(core == 0, fresh_keys, fresh_raw).astype(jnp.bfloat16)
+    fresh = fresh.reshape(seq_count, -1, HD)
+    spots = all_listed[:, model].astype(jnp.int32).reshape(seq_count, 1, -1)
+    onehot = spots == jnp.arange(tile_rows, dtype=jnp.int32)[None, :, None]
+    placed = jnp.einsum(
+        "trl,tld->trd", onehot.astype(jnp.bfloat16), fresh, preferred_element_type=jnp.float32
+    ).astype(jnp.bfloat16)
+    mine = jnp.where(jnp.any(onehot, axis=2, keepdims=True), placed, head_cache)
+    mine = mine.reshape(-1, HD)
+    other = lax.ppermute(mine, "seq", [(i, i ^ 1) for i in range(seq_count)])
+    keys = jnp.where(core == 0, mine, other)
+    values = jnp.where(core == 0, other, mine)
+
     query_raw = jnp.dot(tokens, query_w, preferred_element_type=jnp.float32)
     queries = head_norm(query_raw, query_gain).astype(jnp.bfloat16).reshape(-1, width)
+    got_queries, got_requests, got_tokens = [], [], []
+    for k in range(group):
+        target = lax.rem(line + k, group)
+        block = lax.dynamic_slice(
+            queries, (lax.rem(target, 2) * half_rows, (target // 2) * HD), (half_rows, HD)
+        )
+        got_queries.append(lax.ppermute(block, "seq", turns[k]))
+        tile = lax.rem(place + group - k, group) * group + core * (group // 2)
+        got_requests.append(lax.dynamic_slice_in_dim(mod_req, tile, group // 2))
+        got_tokens.append(lax.dynamic_slice_in_dim(token_req, tile * tile_rows, half_rows))
     out_w = line_gather(out_weight)
-    requests = lax.dynamic_slice_in_dim(mod_req, first_tile, group)
-    own_req = lax.dynamic_slice_in_dim(token_req, first_tile * tile_rows, group * tile_rows)
     attended = attention(
-        queries, keys, values, text_keys, text_values, requests, place.reshape(1),
-        token_req, own_req,
-    )
-    attended = lax.all_gather(attended, "seq", axis=1, axis_index_groups=inner, tiled=True)
+        jnp.concatenate(got_queries, axis=0), keys, values, text_keys, text_values,
+        jnp.concatenate(got_requests), (seq_index // 2).reshape(1),
+        token_req, jnp.concatenate(got_tokens),
+    )
+    own_heads = jnp.zeros((2 * half_rows, width), jnp.bfloat16)
+    for k in range(group):
+        block = attended[k * half_rows : (k + 1) * half_rows]
+        back = lax.ppermute(block, "seq", [(j, i) for i, j in turns[k]])
+        origin = lax.rem(line + k, group)
+        own_heads = lax.dynamic_update_slice(
+            own_heads, back, (lax.rem(origin, 2) * half_rows, (origin // 2) * HD)
+        )
+    all_heads = jnp.zeros((2 * half_rows, group * width), jnp.bfloat16)
+    for k in range(group):
+        got = own_heads
+        if k > 0:
+            got = lax.ppermute(own_heads, "seq", [(i, i ^ k) for i in range(seq_count)])
+        all_heads = lax.dynamic_update_slice(
+            all_heads, got, (jnp.int32(0), jnp.bitwise_xor(place, k) * width)
+        )
     partial_out = lax.dot_general(
-        attended, out_w, (((1,), (1,)), ((), ())), preferred_element_type=jnp.float32
-    )
-    halves = lax.psum_scatter(
-        partial_out.astype(jnp.bfloat16), "tp", scatter_dimension=1, tiled=True
-    )
-    own = lax.all_to_all(
-        halves.reshape(group, tile_rows, -1), "seq", split_axis=0, concat_axis=0,
-        axis_index_groups=inner, tiled=True,
-    )
-    own = own.reshape(group, tile_rows, -1, depth)
-    return jnp.transpose(own, (1, 2, 0, 3)).reshape(tile_rows, -1).astype(jnp.float32)
+        all_heads, out_w, (((1,), (1,)), ((), ())), preferred_element_type=jnp.float32
+    ).astype(jnp.bfloat16)
+    share = partial_out.shape[1] // tp_count
+    pieces = jnp.zeros((group, tile_rows, share), jnp.float32)
+    for k in range(group):
+        peer = jnp.bitwise_xor(place, k)
+        total = 0.0
+        for j in range(tp_count):
+            block = lax.dynamic_slice(
+                partial_out,
+                (peer * tile_rows, lax.rem(tp_index + j, tp_count) * share),
+                (tile_rows, share),
+            )
+            if k > 0 or j > 0:
+                block = lax.ppermute(
+                    block,
+                    ("seq", "tp"),
+                    [
+                        (i * tp_count + t, (i ^ k) * tp_count + (t + j) % tp_count)
+                        for i in range(seq_count)
+                        for t in range(tp_count)
+                    ],
+                )
+            total = total + block.astype(jnp.float32)
+        pieces = lax.dynamic_update_slice(pieces, total[None], (peer, jnp.int32(0), jnp.int32(0)))
+    pieces = pieces.reshape(group, tile_rows, -1, depth)
+    return jnp.transpose(pieces, (1, 2, 0, 3)).reshape(tile_rows, -1)
 
 
 def shards(
@@ -366,10 +434,15 @@
     hidden_cols = lax.dynamic_slice_in_dim(hidden_f32, tp_index * col_count, col_count, 1)
     gate_cols = lax.dynamic_slice_in_dim(choose_row(mod_gate), tp_index * col_count, col_count)
     hidden_next = (hidden_cols + gate_cols[None, :] * reduced).astype(jnp.bfloat16)
-    velocity = lax.psum(
-        jnp.dot(hidden_next, final_weight, preferred_element_type=jnp.float32).astype(jnp.bfloat16),
-        "tp",
-    ).astype(jnp.float32)
+    velocity = jnp.dot(hidden_next, final_weight, preferred_element_type=jnp.float32).astype(
+        jnp.bfloat16
+    )
+    if lax.axis_size("tp") == 2:
+        velocity = velocity.astype(jnp.float32) + lax.ppermute(
+            velocity, "tp", [(0, 1), (1, 0)]
+        ).astype(jnp.float32)
+    else:
+        velocity = lax.psum(velocity, "tp").astype(jnp.float32)
     step_delta = sigma_of(step_index + 1) - sigma_of(step_index)
     own_delta = jnp.sum(select * step_delta)
     latent_next = latent + own_delta * velocity

time: 344 us -> 286 us (0.83)
  waiting for transfers between devices: 217 us -> 171 us
  blocking collectives: 34.5 us -> 0 us
  starting transfers between devices: 19.6 us -> 41.5 us
    all_gather x6 -> x2, waiting for transfers between devices: 138 us -> 0.01 us  [line_gather(): lax.all_gather(block, 'seq', axis=0, axis_index_groups=outer, tiled=True)]
    ppermute x0 -> x20, waiting for transfers between devices: none -> 46.2 us  [the longest x4 27.5 us: grouped_branch(): got_queries.append(lax.ppermute(block, 'seq', turns[k]))]
    all_to_all x3 -> x2, waiting for transfers between devices: 9.91 us -> 50.4 us  [the longest x1 44 us: grouped_branch(): lax.all_to_all(moved, 'seq', split_axis=1, concat_axis=0, tiled=True)]
    all_to_all x3 -> x0, blocking collectives: 29.5 us -> none  [spread(): lax.all_to_all(block, 'seq', split_axis=1, concat_axis=0, axis_index_grou...]
    ppermute x0 -> x20, starting transfers between devices: none -> 23 us  [the longest x4 7.23 us: grouped_branch(): got_queries.append(lax.ppermute(block, 'seq', turns[k]))]
    all_gather x2, waiting for transfers between devices: 49.1 us -> 70.3 us  [the longest x1 41.8 us: grouped_branch(): all_listed = lax.all_gather(listed_x, 'seq', axis=0, tiled=True)]
    unnamed x10 -> x4, waiting for transfers between devices: 18 us -> 0.57 us
    unnamed x48 -> x52, local copies, waits for them, and re-layouts: 12.1 us -> 4.94 us
  transfers between devices with their start and end apart: 14 -> 28, of which waited for: 12 -> 17; matrix products, arithmetic and copies ran while one was open for 8% -> 12% of each run, Pallas kernels for 3% -> 3%
where the time goes in v2:
time: 286 us
  waiting for transfers between devices  171 us (60%)
  starting transfers between devices  41.5 us (15%)
  local copies, waits for them, and re-layouts  22.8 us (8%)
  between operations  17.6 us (6%)
  matrix products  15.3 us (5%)
  other arithmetic  9.92 us (3%)
  Pallas kernels  8 us (3%)
    all_to_all x1, waiting for transfers between devices, grouped_branch(): lax.all_to_all(moved, 'seq', split_axis=1, concat_axis=0, tiled=True)  44 us
    all_gather x1, waiting for transfers between devices, grouped_branch(): all_listed = lax.all_gather(listed_x, 'seq', axis=0, tiled=True)  41.8 us
    all_gather x1, waiting for transfers between devices, grouped_branch(): lax.all_gather(modulated, 'seq', axis=0, axis_index_groups=inner, tiled=T...  28.5 us
    ppermute x4, waiting for transfers between devices, grouped_branch(): got_queries.append(lax.ppermute(block, 'seq', turns[k]))  27.5 us
    pallas_call x1, Pallas kernels, attention(): pl.pallas_call(attention_kernel, grid_spec=grid_spec, out_shape=jax.Shape...  8 us
    ppermute x3, waiting for transfers between devices, grouped_branch(): got = lax.ppermute(own_heads, 'seq', [(i, i ^ k) for i in range(seq_count)])  7.59 us
    ppermute x4, starting transfers between devices, grouped_branch(): got_queries.append(lax.ppermute(block, 'seq', turns[k]))  7.23 us
    all_to_all x1, starting transfers between devices, grouped_branch(): lax.all_to_all(moved, 'seq', split_axis=1, concat_axis=0, tiled=True)  6.75 us
  transfers between devices with their start and end apart: 28, of which 17 were waited for; matrix products, arithmetic and copies ran while one was open for 12% of the time, Pallas kernels for 3%

profile of v2, /device:TPU:1, one launch (start us, length us, event | category | flops | bytes accessed | tf_op | source)
XLA Modules:
  0.0 285.8 jit_solution(6803287048048587042)
XLA Ops:
  7.2 1.8 copy.94
  9.1 4.4 %all-to-all-start = ((bf16[192,4,256]{2,0,1:T(8,128)(2,1)}), bf16[192,4,256]{2,0,1:T(8,128)(2,1)S(1)}, u32[]{:S(2)}, u32[]{:S(2)}) async-start(bf16[192,4,256]{2,0,1:T(8,128)(2,1)} %bitcast.108), calls=%async_computation | async-start | bytes 786432 | tf_op jit(solution)/shard_map/all_to_all | solution.py:287
  13.5 6.4 %all-to-all-done = bf16[192,4,256]{2,0,1:T(8,128)(2,1)S(1)} async-done(((bf16[192,4,256]{2,0,1:T(8,128)(2,1)}), bf16[192,4,256]{2,0,1:T(8,128)(2,1)S(1)}, u32[]{:S(2)}, u32[]{:S(2)}) %all-to-all-start) | async-done | bytes 393248 | tf_op jit(solution)/shard_map/all_to_all | solution.py:287
  23.7 1.3 add_convert_fusion
  25.1 1.0 copy-done.4
  28.9 1.2 pad_maximum_fusion
  30.0 6.8 %all-to-all-start.1 = ((bf16[320,16,128]{2,0,1:T(8,128)(2,1)}), bf16[320,16,128]{2,0,1:T(8,128)(2,1)S(1)}, u32[]{:S(2)}, u32[]{:S(2)}) async-start(bf16[320,16,128]{2,0,1:T(8,128)(2,1)} %pad_maximum_fusion), calls=%async_computation.1 | async-start | bytes 2621440 | tf_op jit(solution)/shard_map/all_to_all | solution.py:270
  38.5 44.0 %all-to-all-done.1 = bf16[320,16,128]{2,0,1:T(8,128)(2,1)S(1)} async-done(((bf16[320,16,128]{2,0,1:T(8,128)(2,1)}), bf16[320,16,128]{2,0,1:T(8,128)(2,1)S(1)}, u32[]{:S(2)}, u32[]{:S(2)}) %all-to-all-start.1) | async-done | bytes 1310752 | tf_op jit(solution)/shard_map/all_to_all | solution.py:270
  82.5 1.0 slice.91
  83.5 28.5 %all-gather.5.cloned.1.call-done = bf16[512,3072]{1,0:T(8,128)(2,1)} async-done(((bf16[128,3072]{1,0:T(8,128)(2,1)}), bf16[512,3072]{1,0:T(8,128)(2,1)}) %all-gather.5.cloned.1.call-update) | async-done | bytes 3145744 | tf_op jit(solution)/shard_map/all_gather | solution.py:291
  112.0 4.2 %bitcast_reduce_fusion = (f32[512,2]{0,1:T(2,128)S(1)}, f32[512,256]{0,1:T(8,128)}) fusion(bf16[512,3072]{1,0:T(8,128)(2,1)} %all-gather.5.cloned.1.call-done, bf16[3072,256]{1,0:T(8,128)(2,1)} %all-gather.7.cloned.1.call-done), kind=kOutput, calls=%fused_computation.19 | convolution fusion | flops 805567488 | bytes 5246976 | tf_op jit(solution)/shard_map/dot_general | solution.py:307
  117.0 1.2 copy.73
  118.2 41.8 %all-gather.9.cloned.1.call-done = bf16[512,3200]{1,0:T(8,128)(2,1)} async-done(((bf16[32,3200]{1,0:T(8,128)(2,1)}), bf16[512,3200]{1,0:T(8,128)(2,1)}) %all-gather.9.cloned.1.call-update) | async-done | bytes 3276816 | tf_op jit(solution)/shard_map/all_gather | solution.py:284
  160.1 3.8 %multiply_reduce_fusion.1 = (f32[512]{0:T(512)S(1)}, f32[512,128]{1,0:T(8,128)}) fusion(bf16[3072,128]{1,0:T(8,128)(2,1)} %bitcast.125, bf16[512,3200]{1,0:T(8,128)(2,1)} %all-gather.9.cloned.1.call-done), kind=kOutput, calls=%fused_computation.26 | convolution fusion | flops 402783744 | bytes 4196352 | tf_op jit(solution)/shard_map/dot_general | solution.py:292
  163.9 1.1 convert_reduce_fusion.1
  165.2 1.1 select_convert_fusion
  166.3 0.9 fusion.2
  168.3 4.0 %collective-permute-start = (bf16[256,128]{1,0:T(8,128)(2,1)S(1)}, bf16[256,128]{1,0:T(8,128)(2,1)S(1)}, u32[]{:S(2)}, u32[]{:S(2)}) collective-permute-start(bf16[256,128]{1,0:T(8,128)(2,1)S(1)} %get-tuple-element.20), channel_id=1, source_target_pairs={{0,0},{2,8},{4,16},{6,24},{8,2},{10,10},{12,18},{14,26},{16,4},{18... | collective-permute-start | bytes 196616 | tf_op jit(solution)/shard_map/ppermute | solution.py:315
  172.4 1.6 collective-permute-start.2
  174.0 1.6 collective-permute-start.3
  175.6 2.7 collective-permute-done
  178.3 5.4 %collective-permute-done.2 = bf16[256,128]{1,0:T(8,128)(2,1)S(1)} collective-permute-done((bf16[256,128]{1,0:T(8,128)(2,1)S(1)}, bf16[256,128]{1,0:T(8,128)(2,1)S(1)}, u32[]{:S(2)}, u32[]{:S(2)}) %collective-permute-start.2) | collective-permute-done | bytes 65568 | tf_op jit(solution)/shard_map/ppermute | solution.py:315
  183.7 19.4 %collective-permute-done.3 = bf16[256,128]{1,0:T(8,128)(2,1)S(1)} collective-permute-done((bf16[256,128]{1,0:T(8,128)(2,1)S(1)}, bf16[256,128]{1,0:T(8,128)(2,1)S(1)}, u32[]{:S(2)}, u32[]{:S(2)}) %collective-permute-start.3) | collective-permute-done | bytes 65568 | tf_op jit(solution)/shard_map/ppermute | solution.py:315
  203.3 2.2 copy-done.2
  205.5 8.0 %shard_map.220 = bf16[1024,128]{1,0:T(8,128)(2,1)S(1)} custom-call(s32[8]{0:T(128)S(1)} %pad_add_fusion.1.request_ref, s32[1]{0:T(128)} %bitcast.3.place_ref, bf16[1024,128]{1,0:T(8,128)(2,1)S(1)} %pad_maximum_fusion.3.q_ref, bf16[2048,128]{1,0:T(8,128)(2,1)S(1)} %get-tuple-element.6.k_ref, bf16[2048,128]{1,0:T(8,128)(2,1)S(1)} %get-tuple-element.5.v_ref, ...), custom_call_target="tpu_custom_call" | custom-call | flops 1342177280 | bytes 2097152 | tf_op jit(solution)/shard_map/pallas_call | solution.py:217
  213.5 1.9 collective-permute-start.5
  215.5 1.2 collective-permute-start.7
  216.8 3.9 %collective-permute-done.5 = bf16[256,128]{1,0:T(8,128)(2,1)S(1)} collective-permute-done((bf16[256,128]{1,0:T(8,128)(2,1)S(1)}, bf16[256,128]{1,0:T(8,128)(2,1)S(1)}, u32[]{:S(2)}, u32[]{:S(2)}) %collective-permute-start.5) | collective-permute-done | bytes 65568 | tf_op jit(solution)/shard_map/ppermute | solution.py:328
  224.3 3.2 %collective-permute-start.10 = (bf16[512,256]{1,0:T(8,128)(2,1)S(1)}, bf16[512,256]{1,0:T(8,128)(2,1)S(1)}, u32[]{:S(2)}, u32[]{:S(2)}) collective-permute-start(bf16[512,256]{1,0:T(8,128)(2,1)S(1)} %dynamic_update_slice.39), channel_id=1, source_target_pairs={{0,4},{2,6},{4,0},{6,2},{8,12},{10,14},{12,8},{14,10},{16,20},{18,... | collective-permute-start | bytes 786440 | tf_op jit(solution)/shard_map/ppermute | solution.py:337
  228.8 1.1 broadcast_in_dim.120
  231.4 2.7 collective-permute-done.10
  234.8 4.9 %collective-permute-done.11 = bf16[512,256]{1,0:T(8,128)(2,1)S(1)} collective-permute-done((bf16[512,256]{1,0:T(8,128)(2,1)S(1)}, bf16[512,256]{1,0:T(8,128)(2,1)S(1)}, u32[]{:S(2)}, u32[]{:S(2)}) %collective-permute-start.11) | collective-permute-done | bytes 262176 | tf_op jit(solution)/shard_map/ppermute | solution.py:337
  240.5 2.8 convolution_convert_fusion
  243.3 1.6 collective-permute-start.17
  245.0 1.1 collective-permute-start.18
  246.1 1.3 select_reduce_fusion.1
  247.4 1.4 collective-permute-start.15
  248.8 0.9 collective-permute-start.13
  249.7 1.1 collective-permute-start.14
  252.6 2.8 collective-permute-done.16
  255.4 1.5 collective-permute-done.14
  259.1 1.5 collective-permute-start.19
  260.6 1.1 collective-permute-done.19
  261.7 1.3 select_convert_fusion.1
  263.1 5.3 %collective-permute-start.20 = (bf16[64,64]{0,1:T(8,128)(2,1)S(1)}, bf16[64,64]{0,1:T(8,128)(2,1)S(1)}, u32[]{:S(2)}, u32[]{:S(2)}) collective-permute-start(bf16[64,64]{0,1:T(8,128)(2,1)S(1)} %get-tuple-element.30), channel_id=1, source_target_pairs={{0,2},{2,4},{4,6},{6,8},{8,10},{10,12},{12,14},{14,16},{16,18},{18... | collective-permute-start | bytes 24584 | tf_op jit(solution)/shard_map/ppermute | solution.py:27
  271.9 1.9 collective-permute-start.21
  273.9 3.1 %collective-permute-done.21 = bf16[64,64]{0,1:T(8,128)(2,1)S(1)} collective-permute-done((bf16[64,64]{0,1:T(8,128)(2,1)S(1)}, bf16[64,64]{0,1:T(8,128)(2,1)S(1)}, u32[]{:S(2)}, u32[]{:S(2)}) %collective-permute-start.21) | collective-permute-done | bytes 8224 | tf_op jit(solution)/shard_map/ppermute | solution.py:28
  278.3 0.9 fusion.3
  (168 shorter events, 24.5 us)
Async XLA Ops:
  7.2 251.6 %copy-start = (bf16[1536,64]{0,1:T(8,128)(2,1)S(1)}, bf16[1536,64]{0,1:T(8,128)(2,1)}, u32[]{:S(2)}) copy-start(bf16[1536,64]{0,1:T(8,128)(2,1)} %param.36) | copy-start | bytes 589828
  7.2 13.5 %copy-start.16 = (s32[16]{0:T(128)S(1)}, s32[16]{0:T(128)}, u32[]{:S(2)}) copy-start(s32[16]{0:T(128)} %param.39) | copy-start | bytes 196
  7.2 14.2 %copy-start.3 = (bf16[128,3072]{1,0:T(8,128)(2,1)S(1)}, bf16[128,3072]{1,0:T(8,128)(2,1)}, u32[]{:S(2)}) copy-start(bf16[128,3072]{1,0:T(8,128)(2,1)} %param.21) | copy-start | bytes 2359300
  9.1 12.9 %copy-start.12 = (f32[4,3072]{1,0:T(4,128)S(1)}, f32[4,3072]{1,0:T(4,128)}, u32[]{:S(2)}) copy-start(f32[4,3072]{1,0:T(4,128)} %param.34) | copy-start | bytes 147460
  9.1 13.8 %copy-start.13 = (f32[4,3072]{1,0:T(4,128)S(1)}, f32[4,3072]{1,0:T(4,128)}, u32[]{:S(2)}) copy-start(f32[4,3072]{1,0:T(4,128)} %param.33) | copy-start | bytes 147460
  9.1 10.8 %all-to-all-start = ((bf16[192,4,256]{2,0,1:T(8,128)(2,1)}), bf16[192,4,256]{2,0,1:T(8,128)(2,1)S(1)}, u32[]{:S(2)}, u32[]{:S(2)}) async-start(bf16[192,4,256]{2,0,1:T(8,128)(2,1)} %bitcast.108), calls=%async_computation | async-start | bytes 786432 | tf_op jit(solution)/shard_map/all_to_all | solution.py:287
  13.4 70.0 %all-gather.7.cloned.1.call-start = ((), (), s32[]{:S(2)}) async-start(), calls=%async_computation.3 | async-start | bytes 1966080 | tf_op jit(solution)/shard_map/all_gather | solution.py:265
  20.6 91.3 %all-gather.5.cloned.1.call-start = ((), (), s32[]{:S(2)}) async-start(), calls=%async_computation.2 | async-start | bytes 3932160 | tf_op jit(solution)/shard_map/all_gather | solution.py:291
  21.6 3.5 %copy-start.20 = (s32[1,32]{1,0:T(1,128)S(1)}, s32[1,32]{1,0:T(1,128)}, u32[]{:S(2)}) copy-start(s32[1,32]{1,0:T(1,128)} %param.40) | copy-start | bytes 388
  24.9 1.1 copy-start.4
  24.9 2.6 copy-start.8
  25.0 135.1 %all-gather.9.cloned.1.call-start = ((), (), s32[]{:S(2)}) async-start(), calls=%async_computation.4 | async-start | bytes 3481600 | tf_op jit(solution)/shard_map/all_gather | solution.py:284
  26.1 1.7 copy-start.9
  30.0 7.8 %copy-start.21 = (s32[4]{0:T(128)S(1)}, s32[4]{0:T(128)}, u32[]{:S(2)}) copy-start(s32[4]{0:T(128)} %param.38) | copy-start | bytes 52
  30.0 8.4 %copy-start.22 = (f32[128]{0:T(128)S(1)}, f32[128]{0:T(128)}, u32[]{:S(2)}) copy-start(f32[128]{0:T(128)} %param.31) | copy-start | bytes 1540
  30.0 52.5 %all-to-all-start.1 = ((bf16[320,16,128]{2,0,1:T(8,128)(2,1)}), bf16[320,16,128]{2,0,1:T(8,128)(2,1)S(1)}, u32[]{:S(2)}, u32[]{:S(2)}) async-start(bf16[320,16,128]{2,0,1:T(8,128)(2,1)} %pad_maximum_fusion), calls=%async_computation.1 | async-start | bytes 2621440 | tf_op jit(solution)/shard_map/all_to_all | solution.py:270
  36.8 203.7 %all-gather.11.cloned.1.call-start = ((), (), s32[]{:S(2)}) async-start(), calls=%async_computation.5 | async-start | bytes 1966080 | tf_op jit(solution)/shard_map/all_gather | solution.py:265
  160.1 5.1 %copy-start.18 = (f32[128]{0:T(128)S(1)}, f32[128]{0:T(128)}, u32[]{:S(2)}) copy-start(f32[128]{0:T(128)} %param.32) | copy-start | bytes 1540
  165.0 2.5 copy-start.7
  167.2 35.9 %collective-permute-start.4 = (bf16[2048,128]{1,0:T(8,128)(2,1)S(1)}, bf16[2048,128]{1,0:T(8,128)(2,1)S(1)}, u32[]{:S(2)}, u32[]{:S(2)}) collective-permute-start(bf16[2048,128]{1,0:T(8,128)(2,1)S(1)} %bitcast.126), channel_id=1, source_target_pairs={{0,2},{2,0},{4,6},{6,4},{8,10},{10,8},{12,14},{14,12},{16,18},{18,... | collective-permute-start | bytes 1572872 | tf_op jit(solution)/shard_map/ppermute | solution.py:303
  168.1 35.1 %copy-start.1 = (bf16[4,512,1024]{2,1,0:T(8,128)(2,1)S(1)}, bf16[4,512,1024]{2,1,0:T(8,128)(2,1)}, u32[]{:S(2)}) copy-start(bf16[4,512,1024]{2,1,0:T(8,128)(2,1)} %tk_ref.1) | copy-start | bytes 12582916
  168.3 10.0 %collective-permute-start = (bf16[256,128]{1,0:T(8,128)(2,1)S(1)}, bf16[256,128]{1,0:T(8,128)(2,1)S(1)}, u32[]{:S(2)}, u32[]{:S(2)}) collective-permute-start(bf16[256,128]{1,0:T(8,128)(2,1)S(1)} %get-tuple-element.20), channel_id=1, source_target_pairs={{0,0},{2,8},{4,16},{6,24},{8,2},{10,10},{12,18},{14,26},{16,4},{18... | collective-permute-start | bytes 196616 | tf_op jit(solution)/shard_map/ppermute | solution.py:315
  172.3 6.0 %collective-permute-start.1 = (bf16[256,128]{1,0:T(8,128)(2,1)S(1)}, bf16[256,128]{1,0:T(8,128)(2,1)S(1)}, u32[]{:S(2)}, u32[]{:S(2)}) collective-permute-start(bf16[256,128]{1,0:T(8,128)(2,1)S(1)} %get-tuple-element.23), channel_id=1, source_target_pairs={{0,2},{2,10},{4,18},{6,26},{8,4},{10,12},{12,20},{14,28},{16,6},{1... | collective-permute-start | bytes 196616 | tf_op jit(solution)/shard_map/ppermute | solution.py:315
  172.4 11.3 %collective-permute-start.2 = (bf16[256,128]{1,0:T(8,128)(2,1)S(1)}, bf16[256,128]{1,0:T(8,128)(2,1)S(1)}, u32[]{:S(2)}, u32[]{:S(2)}) collective-permute-start(bf16[256,128]{1,0:T(8,128)(2,1)S(1)} %get-tuple-element.22), channel_id=1, source_target_pairs={{0,4},{2,12},{4,20},{6,28},{8,6},{10,14},{12,22},{14,30},{16,0},{1... | collective-permute-start | bytes 196616 | tf_op jit(solution)/shard_map/ppermute | solution.py:315
  174.0 29.1 %collective-permute-start.3 = (bf16[256,128]{1,0:T(8,128)(2,1)S(1)}, bf16[256,128]{1,0:T(8,128)(2,1)S(1)}, u32[]{:S(2)}, u32[]{:S(2)}) collective-permute-start(bf16[256,128]{1,0:T(8,128)(2,1)S(1)} %get-tuple-element.21), channel_id=1, source_target_pairs={{0,6},{2,14},{4,22},{6,30},{8,0},{10,8},{12,16},{14,24},{16,2},{18... | collective-permute-start | bytes 196616 | tf_op jit(solution)/shard_map/ppermute | solution.py:315
  203.3 2.2 copy-start.2
  205.5 22.0 %copy-start.14 = (f32[4,3072]{1,0:T(4,128)S(1)}, f32[4,3072]{1,0:T(4,128)}, u32[]{:S(2)}) copy-start(f32[4,3072]{1,0:T(4,128)} %param.35) | copy-start | bytes 147460
  213.5 7.1 %collective-permute-start.5 = (bf16[256,128]{1,0:T(8,128)(2,1)S(1)}, bf16[256,128]{1,0:T(8,128)(2,1)S(1)}, u32[]{:S(2)}, u32[]{:S(2)}) collective-permute-start(bf16[256,128]{1,0:T(8,128)(2,1)S(1)} %get-tuple-element.19), channel_id=1, source_target_pairs={{0,0},{8,2},{16,4},{24,6},{2,8},{10,10},{18,12},{26,14},{4,16},{12... | collective-permute-start | bytes 196616 | tf_op jit(solution)/shard_map/ppermute | solution.py:328
  215.4 6.0 %collective-permute-start.6 = (bf16[256,128]{1,0:T(8,128)(2,1)S(1)}, bf16[256,128]{1,0:T(8,128)(2,1)S(1)}, u32[]{:S(2)}, u32[]{:S(2)}) collective-permute-start(bf16[256,128]{1,0:T(8,128)(2,1)S(1)} %get-tuple-element.18), channel_id=1, source_target_pairs={{2,0},{10,2},{18,4},{26,6},{4,8},{12,10},{20,12},{28,14},{6,16},{1... | collective-permute-start | bytes 196616 | tf_op jit(solution)/shard_map/ppermute | solution.py:328
  215.5 6.6 %collective-permute-start.7 = (bf16[256,128]{1,0:T(8,128)(2,1)S(1)}, bf16[256,128]{1,0:T(8,128)(2,1)S(1)}, u32[]{:S(2)}, u32[]{:S(2)}) collective-permute-start(bf16[256,128]{1,0:T(8,128)(2,1)S(1)} %get-tuple-element.17), channel_id=1, source_target_pairs={{4,0},{12,2},{20,4},{28,6},{6,8},{14,10},{22,12},{30,14},{0,16},{8... | collective-permute-start | bytes 196616 | tf_op jit(solution)/shard_map/ppermute | solution.py:328
  216.8 6.1 %collective-permute-start.8 = (bf16[256,128]{1,0:T(8,128)(2,1)S(1)}, bf16[256,128]{1,0:T(8,128)(2,1)S(1)}, u32[]{:S(2)}, u32[]{:S(2)}) collective-permute-start(bf16[256,128]{1,0:T(8,128)(2,1)S(1)} %get-tuple-element.16), channel_id=1, source_target_pairs={{6,0},{14,2},{22,4},{30,6},{0,8},{8,10},{16,12},{24,14},{2,16},{10... | collective-permute-start | bytes 196616 | tf_op jit(solution)/shard_map/ppermute | solution.py:328
  223.5 7.2 %collective-permute-start.9 = (bf16[512,256]{1,0:T(8,128)(2,1)S(1)}, bf16[512,256]{1,0:T(8,128)(2,1)S(1)}, u32[]{:S(2)}, u32[]{:S(2)}) collective-permute-start(bf16[512,256]{1,0:T(8,128)(2,1)S(1)} %dynamic_update_slice.39), channel_id=1, source_target_pairs={{0,2},{2,0},{4,6},{6,4},{8,10},{10,8},{12,14},{14,12},{16,18},{18,... | collective-permute-start | bytes 786440 | tf_op jit(solution)/shard_map/ppermute | solution.py:337
  224.3 9.8 %collective-permute-start.10 = (bf16[512,256]{1,0:T(8,128)(2,1)S(1)}, bf16[512,256]{1,0:T(8,128)(2,1)S(1)}, u32[]{:S(2)}, u32[]{:S(2)}) collective-permute-start(bf16[512,256]{1,0:T(8,128)(2,1)S(1)} %dynamic_update_slice.39), channel_id=1, source_target_pairs={{0,4},{2,6},{4,0},{6,2},{8,12},{10,14},{12,8},{14,10},{16,20},{18,... | collective-permute-start | bytes 786440 | tf_op jit(solution)/shard_map/ppermute | solution.py:337
  228.7 11.0 %collective-permute-start.11 = (bf16[512,256]{1,0:T(8,128)(2,1)S(1)}, bf16[512,256]{1,0:T(8,128)(2,1)S(1)}, u32[]{:S(2)}, u32[]{:S(2)}) collective-permute-start(bf16[512,256]{1,0:T(8,128)(2,1)S(1)} %dynamic_update_slice.39), channel_id=1, source_target_pairs={{0,6},{2,4},{4,2},{6,0},{8,14},{10,12},{12,10},{14,8},{16,22},{18,... | collective-permute-start | bytes 786440 | tf_op jit(solution)/shard_map/ppermute | solution.py:337
  240.5 5.6 %copy-start.23 = (s32[4]{0:T(128)S(1)}, s32[4]{0:T(128)}, u32[]{:S(2)}) copy-start(s32[4]{0:T(128)} %param.41) | copy-start | bytes 52
  243.3 6.4 %collective-permute-start.17 = (bf16[128,384]{1,0:T(8,128)(2,1)S(1)}, bf16[128,384]{1,0:T(8,128)(2,1)S(1)}, u32[]{:S(2)}, u32[]{:S(2)}) collective-permute-start(bf16[128,384]{1,0:T(8,128)(2,1)S(1)} %get-tuple-element.7), channel_id=1, source_target_pairs={{0,6},{1,7},{2,4},{3,5},{4,2},{5,3},{6,0},{7,1},{8,14},{9,15},{10,... | collective-permute-start | bytes 294920 | tf_op jit(solution)/shard_map/ppermute | solution.py:356
  245.0 6.6 %collective-permute-start.18 = (bf16[128,384]{1,0:T(8,128)(2,1)S(1)}, bf16[128,384]{1,0:T(8,128)(2,1)S(1)}, u32[]{:S(2)}, u32[]{:S(2)}) collective-permute-start(bf16[128,384]{1,0:T(8,128)(2,1)S(1)} %get-tuple-element.8), channel_id=1, source_target_pairs={{0,7},{1,6},{2,5},{3,4},{4,3},{5,2},{6,1},{7,0},{8,15},{9,14},{10,... | collective-permute-start | bytes 294920 | tf_op jit(solution)/shard_map/ppermute | solution.py:356
  247.4 5.2 %collective-permute-start.15 = (bf16[128,384]{1,0:T(8,128)(2,1)S(1)}, bf16[128,384]{1,0:T(8,128)(2,1)S(1)}, u32[]{:S(2)}, u32[]{:S(2)}) collective-permute-start(bf16[128,384]{1,0:T(8,128)(2,1)S(1)} %get-tuple-element.10), channel_id=1, source_target_pairs={{0,4},{1,5},{2,6},{3,7},{4,0},{5,1},{6,2},{7,3},{8,12},{9,13},{10,... | collective-permute-start | bytes 294920 | tf_op jit(solution)/shard_map/ppermute | solution.py:356
  248.8 6.6 %collective-permute-start.16 = (bf16[128,384]{1,0:T(8,128)(2,1)S(1)}, bf16[128,384]{1,0:T(8,128)(2,1)S(1)}, u32[]{:S(2)}, u32[]{:S(2)}) collective-permute-start(bf16[128,384]{1,0:T(8,128)(2,1)S(1)} %get-tuple-element.9), channel_id=1, source_target_pairs={{0,5},{1,4},{2,7},{3,6},{4,1},{5,0},{6,3},{7,2},{8,13},{9,12},{10,... | collective-permute-start | bytes 294920 | tf_op jit(solution)/shard_map/ppermute | solution.py:356
  248.8 6.6 %collective-permute-start.13 = (bf16[128,384]{1,0:T(8,128)(2,1)S(1)}, bf16[128,384]{1,0:T(8,128)(2,1)S(1)}, u32[]{:S(2)}, u32[]{:S(2)}) collective-permute-start(bf16[128,384]{1,0:T(8,128)(2,1)S(1)} %get-tuple-element.12), channel_id=1, source_target_pairs={{0,2},{1,3},{2,0},{3,1},{4,6},{5,7},{6,4},{7,5},{8,10},{9,11},{10,... | collective-permute-start | bytes 294920 | tf_op jit(solution)/shard_map/ppermute | solution.py:356
  249.7 7.2 %collective-permute-start.14 = (bf16[128,384]{1,0:T(8,128)(2,1)S(1)}, bf16[128,384]{1,0:T(8,128)(2,1)S(1)}, u32[]{:S(2)}, u32[]{:S(2)}) collective-permute-start(bf16[128,384]{1,0:T(8,128)(2,1)S(1)} %get-tuple-element.11), channel_id=1, source_target_pairs={{0,3},{1,2},{2,1},{3,0},{4,7},{5,6},{6,5},{7,4},{8,11},{9,10},{10,... | collective-permute-start | bytes 294920 | tf_op jit(solution)/shard_map/ppermute | solution.py:356
  251.5 6.5 %collective-permute-start.12 = (bf16[128,384]{1,0:T(8,128)(2,1)S(1)}, bf16[128,384]{1,0:T(8,128)(2,1)S(1)}, u32[]{:S(2)}, u32[]{:S(2)}) collective-permute-start(bf16[128,384]{1,0:T(8,128)(2,1)S(1)} %get-tuple-element.13), channel_id=1, source_target_pairs={{0,1},{1,0},{2,3},{3,2},{4,5},{5,4},{6,7},{7,6},{8,9},{9,8},{10,11... | collective-permute-start | bytes 294920 | tf_op jit(solution)/shard_map/ppermute | solution.py:356
  258.7 3.1 %copy-start.15 = (f32[128,64]{0,1:T(8,128)S(1)}, f32[128,64]{0,1:T(8,128)}, u32[]{:S(2)}) copy-start(f32[128,64]{0,1:T(8,128)} %param.22) | copy-start | bytes 98308
  258.7 9.8 %copy-start.17 = (s32[16]{0:T(128)S(1)}, s32[16]{0:T(128)}, u32[]{:S(2)}) copy-start(s32[16]{0:T(128)} %param.39) | copy-start | bytes 196
  258.8 18.8 %copy-start.6 = (bf16[128,1536]{1,0:T(8,128)(2,1)}, bf16[128,1536]{1,0:T(8,128)(2,1)S(1)}, u32[]{:S(2)}) copy-start(bf16[128,1536]{1,0:T(8,128)(2,1)S(1)} %add_convert_fusion.1) | copy-start | bytes 1179652
  259.1 2.7 collective-permute-start.19
  263.1 10.8 %collective-permute-start.20 = (bf16[64,64]{0,1:T(8,128)(2,1)S(1)}, bf16[64,64]{0,1:T(8,128)(2,1)S(1)}, u32[]{:S(2)}, u32[]{:S(2)}) collective-permute-start(bf16[64,64]{0,1:T(8,128)(2,1)S(1)} %get-tuple-element.30), channel_id=1, source_target_pairs={{0,2},{2,4},{4,6},{6,8},{8,10},{10,12},{12,14},{14,16},{16,18},{18... | collective-permute-start | bytes 24584 | tf_op jit(solution)/shard_map/ppermute | solution.py:27
  271.9 5.1 %collective-permute-start.21 = (bf16[64,64]{0,1:T(8,128)(2,1)S(1)}, bf16[64,64]{0,1:T(8,128)(2,1)S(1)}, u32[]{:S(2)}, u32[]{:S(2)}) collective-permute-start(bf16[64,64]{0,1:T(8,128)(2,1)S(1)} %get-tuple-element.31), channel_id=1, source_target_pairs={{2,0},{4,2},{6,4},{8,6},{10,8},{12,10},{14,12},{16,14},{18,16},{20... | collective-permute-start | bytes 24584 | tf_op jit(solution)/shard_map/ppermute | solution.py:28
  (4 other events, 3.6 us)
Sparse Core Ops, SparseCore 0:
  20.7 61.2 all-gather.6
  83.6 28.2 all-gather.4
  114.2 45.7 all-gather.8
  161.5 46.7 all-gather.10

commit v3 on v2

--- a/solution.py
+++ b/solution.py
@@ -255,14 +255,39 @@
     depth = query_weight.shape[0]
     half_rows = group * tile_rows // 2
     inner = [[z * group + p for p in range(group)] for z in range(lines)]
-    outer = [[z * group + p for z in range(lines)] for p in range(group)]
     turns = [
         [(z * group + p, p * group + (z + k) % group) for z in range(lines) for p in range(group)]
         for k in range(group)
     ]
 
     def line_gather(block):
-        return lax.all_gather(block, "seq", axis=0, axis_index_groups=outer, tiled=True)
+        full = jnp.zeros((lines,) + block.shape, block.dtype)
+        for k in range(lines):
+            got = block
+            if k > 0:
+                got = lax.ppermute(
+                    block, "seq", [(i, (i + k * group) % seq_count) for i in range(seq_count)]
+                )
+            full = lax.dynamic_update_slice(
+                full, got[None], (lax.rem(line + lines - k, lines), jnp.int32(0), jnp.int32(0))
+            )
+        return full.reshape(-1, block.shape[1])
+
+    def paired(block, flip, position):
+        got = lax.ppermute(block, "seq", [(i, i ^ flip) for i in range(seq_count)])
+        first = jnp.where(position == 0, block, got)
+        second = jnp.where(position == 0, got, block)
+        return jnp.concatenate([first, second], axis=0)
+
+    def plane_gather(block):
+        return paired(paired(block, 2, side), 1, core)
+
+    def spot_of(at):
+        return lax.rem(at, 2) * 2 + at // 2
+
+    def tile_order(rows):
+        shaped = rows.reshape((2, 2, lines, -1) + rows.shape[1:])
+        return jnp.swapaxes(shaped, 0, 2).reshape((seq_count, -1) + rows.shape[1:])
 
     moved = jnp.concatenate(
         [interleave(key_weight, value_weight), interleave(key_cache, value_cache)], axis=0
@@ -281,19 +306,18 @@
         ],
         axis=1,
     )
-    all_listed = lax.all_gather(listed_x, "seq", axis=0, tiled=True)
-    tokens = modulated
+    all_listed = plane_gather(line_gather(listed_x))
     query_w = line_gather(
         lax.all_to_all(
             query_weight, "seq", split_axis=1, concat_axis=0, axis_index_groups=inner, tiled=True
         )
     )
-    tokens = lax.all_gather(modulated, "seq", axis=0, axis_index_groups=inner, tiled=True)
+    tokens = plane_gather(modulated)
     fresh_raw = jnp.dot(all_listed[:, :model], head_weight, preferred_element_type=jnp.float32)
     fresh_keys = head_norm(fresh_raw, key_gain).reshape(-1, HD)
     fresh = jnp.where(core == 0, fresh_keys, fresh_raw).astype(jnp.bfloat16)
-    fresh = fresh.reshape(seq_count, -1, HD)
-    spots = all_listed[:, model].astype(jnp.int32).reshape(seq_count, 1, -1)
+    fresh = tile_order(fresh)
+    spots = tile_order(all_listed[:, model].astype(jnp.int32))[:, None, :]
     onehot = spots == jnp.arange(tile_rows, dtype=jnp.int32)[None, :, None]
     placed = jnp.einsum(
         "trl,tld->trd", onehot.astype(jnp.bfloat16), fresh, preferred_element_type=jnp.float32
@@ -313,10 +337,11 @@
             queries, (lax.rem(target, 2) * half_rows, (target // 2) * HD), (half_rows, HD)
         )
         got_queries.append(lax.ppermute(block, "seq", turns[k]))
-        tile = lax.rem(place + group - k, group) * group + core * (group // 2)
-        got_requests.append(lax.dynamic_slice_in_dim(mod_req, tile, group // 2))
-        got_tokens.append(lax.dynamic_slice_in_dim(token_req, tile * tile_rows, half_rows))
-    out_w = line_gather(out_weight)
+        for half in range(2):
+            tile = lax.rem(place + group - k, group) * group + core + 2 * half
+            got_requests.append(lax.dynamic_slice_in_dim(mod_req, tile, 1))
+            got_tokens.append(lax.dynamic_slice_in_dim(token_req, tile * tile_rows, tile_rows))
+    out_w = line_gather(lax.optimization_barrier((out_weight, moved))[0])
     attended = attention(
         jnp.concatenate(got_queries, axis=0), keys, values, text_keys, text_values,
         jnp.concatenate(got_requests), (seq_index // 2).reshape(1),
@@ -349,7 +374,7 @@
         for j in range(tp_count):
             block = lax.dynamic_slice(
                 partial_out,
-                (peer * tile_rows, lax.rem(tp_index + j, tp_count) * share),
+                (spot_of(peer) * tile_rows, lax.rem(tp_index + j, tp_count) * share),
                 (tile_rows, share),
             )
             if k > 0 or j > 0:

time: 286 us -> 243 us (0.85)
  waiting for transfers between devices: 171 us -> 80.8 us
  starting transfers between devices: 41.5 us -> 67 us
  other arithmetic: 9.92 us -> 29.4 us
  local copies, waits for them, and re-layouts: 22.8 us -> 39 us
  between operations: 17.6 us -> 4.53 us
  matrix products: 15.3 us -> 12 us
    all_gather x4 -> x0, waiting for transfers between devices: 70.3 us -> none  [the longest x1 41.8 us: grouped_branch(): all_listed = lax.all_gather(listed_x, 'seq', axis=0, tiled=True)]
    ppermute x0 -> x13, waiting for transfers between devices: none -> 47.7 us  [the longest x9 47.6 us: line_gather(): lax.ppermute(block, 'seq', [(i, (i + k * group) % seq_count) for i in ran...]
    all_to_all x1, waiting for transfers between devices: 44 us -> 0.01 us  [grouped_branch(): lax.all_to_all(moved, 'seq', split_axis=1, concat_axis=0, tiled=True)]
    ppermute x4, waiting for transfers between devices: 27.5 us -> 2.58 us  [grouped_branch(): got_queries.append(lax.ppermute(block, 'seq', turns[k]))]
    ppermute x0 -> x13, starting transfers between devices: none -> 17.2 us  [the longest x9 13.5 us: line_gather(): lax.ppermute(block, 'seq', [(i, (i + k * group) % seq_count) for i in ran...]
    dynamic_update_slice x0 -> x11, local copies, waits for them, and re-layouts: none -> 9.28 us  [line_gather(): lax.dynamic_update_slice(full, got[None], (lax.rem(line + lines - k, line...]
    select_n x0 -> x4, other arithmetic: none -> 9.24 us  [paired(): first = jnp.where(position == 0, block, got)]
    all_to_all x1, waiting for transfers between devices: 6.4 us -> 0.01 us  [grouped_branch(): lax.all_to_all(query_weight, 'seq', split_axis=1, concat_axis=0, axis_ind...]
  transfers between devices with their start and end apart: 28 -> 37, of which waited for: 17 -> 15; matrix products, arithmetic and copies ran while one was open for 12% -> 26% of each run, Pallas kernels for 3% -> 3%
where the time goes in v3:
time: 243 us; the launch traced here: 241 us
  waiting for transfers between devices  80.8 us (33%)
  starting transfers between devices  67 us (28%)
  local copies, waits for them, and re-layouts  39 us (16%)
  other arithmetic  29.4 us (12%)
  matrix products  12 us (5%)
  Pallas kernels  7.98 us (3%)
  between operations  4.53 us (2%)
    ppermute x9, waiting for transfers between devices, line_gather(): lax.ppermute(block, 'seq', [(i, (i + k * group) % seq_count) for i in ran...  47.6 us
    ppermute x9, starting transfers between devices, line_gather(): lax.ppermute(block, 'seq', [(i, (i + k * group) % seq_count) for i in ran...  13.5 us
    ppermute x4, starting transfers between devices, grouped_branch(): got_queries.append(lax.ppermute(block, 'seq', turns[k]))  12.7 us
    ppermute x3, waiting for transfers between devices, grouped_branch(): got = lax.ppermute(own_heads, 'seq', [(i, i ^ k) for i in range(seq_count)])  11.8 us
    dynamic_update_slice x11, local copies, waits for them, and re-layouts, line_gather(): lax.dynamic_update_slice(full, got[None], (lax.rem(line + lines - k, line...  9.28 us
    select_n x4, other arithmetic, paired(): first = jnp.where(position == 0, block, got)  9.24 us
    ppermute x4, waiting for transfers between devices, grouped_branch(): back = lax.ppermute(block, 'seq', [(j, i) for i, j in turns[k]])  8.86 us
    pallas_call x1, Pallas kernels, attention(): pl.pallas_call(attention_kernel, grid_spec=grid_spec, out_shape=jax.Shape...  7.98 us
  transfers between devices with their start and end apart: 37, of which 15 were waited for; matrix products, arithmetic and copies ran while one was open for 26% of the time, Pallas kernels for 3%

profile of v3, /device:TPU:1, one launch (start us, length us, event | category | flops | bytes accessed | tf_op | source)
XLA Modules:
  0.0 240.7 jit_solution(7261296630766490163)
XLA Ops:
  3.4 1.5 fusion.13
  5.0 1.5 fusion.11
  6.5 1.3 convert_reduce_fusion
  10.2 2.1 collective-permute-start.9
  12.3 2.3 collective-permute-start.10
  17.7 5.2 %all-to-all-start = ((bf16[192,4,256]{2,0,1:T(8,128)(2,1)}), bf16[192,4,256]{2,0,1:T(8,128)(2,1)S(1)}, u32[]{:S(2)}, u32[]{:S(2)}) async-start(bf16[192,4,256]{2,0,1:T(8,128)(2,1)} %bitcast.139), calls=%async_computation | async-start | bytes 786432 | tf_op jit(solution)/shard_map/all_to_all | solution.py:311
  23.3 1.3 convert_element_type.88
  34.4 5.1 %concatenate.57.request_ref = s32[8]{0:T(128)S(1)} concatenate(s32[1]{0:T(128)} %get-tuple-element.55, s32[1]{0:T(128)} %get-tuple-element.54, s32[1]{0:T(128)} %get-tuple-element.53, s32[1]{0:T(128)} %get-tuple-element.52, s32[1]{0:T(128)} %get-tuple-element.51, s32[1]{0:T(128)} %get-tuple-element.50, s32[1]{0:T(128)} %get-tuple-element.49, s32[1]{0:T(128)} %get-tuple-element.48), dimensions={0} | concatenate | bytes 64 | tf_op jit(solution)/shard_map/concatenate | solution.py:347
  39.5 2.3 pad_maximum_fusion.4
  41.7 1.6 bitcast_dynamic-update-slice_fusion.9
  43.4 1.6 bitcast_dynamic-update-slice_fusion.8
  45.0 4.4 %all-to-all-start.1 = ((bf16[320,16,128]{2,0,1:T(8,128)(2,1)}), bf16[320,16,128]{2,0,1:T(8,128)(2,1)}, u32[]{:S(2)}, u32[]{:S(2)}) async-start(bf16[320,16,128]{2,0,1:T(8,128)(2,1)} %pad_maximum_fusion.4), calls=%async_computation.1 | async-start | bytes 2621440 | tf_op jit(solution)/shard_map/all_to_all | solution.py:295
  49.4 1.4 collective-permute-start.2
  50.8 2.1 collective-permute-start.3
  52.9 1.6 bitcast_dynamic-update-slice_fusion.7
  56.9 1.3 broadcast_in_dim.167
  59.0 24.4 %collective-permute-done.2 = bf16[768,256]{1,0:T(8,128)(2,1)S(1)} collective-permute-done((bf16[768,256]{1,0:T(8,128)(2,1)S(1)}, bf16[768,256]{1,0:T(8,128)(2,1)S(1)}, u32[]{:S(2)}, u32[]{:S(2)}) %collective-permute-start.2) | collective-permute-done | bytes 393248 | tf_op jit(solution)/shard_map/ppermute | solution.py:268
  84.2 22.0 %collective-permute-done.3 = bf16[768,256]{1,0:T(8,128)(2,1)S(1)} collective-permute-done((bf16[768,256]{1,0:T(8,128)(2,1)S(1)}, bf16[768,256]{1,0:T(8,128)(2,1)S(1)}, u32[]{:S(2)}, u32[]{:S(2)}) %collective-permute-start.3) | collective-permute-done | bytes 393248 | tf_op jit(solution)/shard_map/ppermute | solution.py:268
  107.0 1.7 broadcast_select_fusion.7
  108.7 1.4 pad_maximum_fusion.3
  110.2 1.3 collective-permute-start.1
  112.3 2.6 %copy.100 = bf16[256,3072]{1,0:T(8,128)(2,1)} copy(bf16[256,3072]{0,1:T(8,128)(2,1)} %bitcast.17) | data formatting | bytes 3145728 | tf_op jit(solution)/shard_map/dot_general | solution.py:331
  114.9 1.5 broadcast_select_fusion.5
  117.8 2.3 broadcast_select_fusion.3
  122.0 8.4 %collective-permute-start.5 = (bf16[256,128]{1,0:T(8,128)(2,1)}, bf16[256,128]{1,0:T(8,128)(2,1)}, u32[]{:S(2)}, u32[]{:S(2)}) collective-permute-start(bf16[256,128]{1,0:T(8,128)(2,1)} %copy.102), channel_id=1, source_target_pairs={{0,0},{2,8},{4,16},{6,24},{8,2},{10,10},{12,18},{14,26},{16,4},{18... | collective-permute-start | bytes 196616 | tf_op jit(solution)/shard_map/ppermute | solution.py:339
  133.6 3.4 %collective-permute-start.8 = (bf16[256,128]{1,0:T(8,128)(2,1)}, bf16[256,128]{1,0:T(8,128)(2,1)}, u32[]{:S(2)}, u32[]{:S(2)}) collective-permute-start(bf16[256,128]{1,0:T(8,128)(2,1)} %copy.105), channel_id=1, source_target_pairs={{0,6},{2,14},{4,22},{6,30},{8,0},{10,8},{12,16},{14,24},{16,2},{18... | collective-permute-start | bytes 196616 | tf_op jit(solution)/shard_map/ppermute | solution.py:339
  138.2 1.3 collective-permute-start.22
  139.6 3.7 %broadcast_select_fusion.1 = (bf16[256,3200]{1,0:T(8,128)(2,1)}, bf16[256,3200]{1,0:T(8,128)(2,1)}) fusion(bf16[256,3200]{1,0:T(8,128)(2,1)} %collective-permute-done.13, pred[]{:T(512)S(6)} %eq.66, bf16[128,3200]{1,0:T(8,128)(2,1)S(1)} %get-tuple-element.12, bf16[128,3200]{1,0:T(8,128)(2,1)S(1)} %get-tuple-element.11), kind=kLoop, calls=%fused_computation.10 | loop fusion | flops 4915200 | bytes 6553601 | tf_op jit(solution)/shard_map/jit(_where)/select_n | solution.py:278
  144.6 3.1 %multiply_reduce_fusion.2 = (f32[512]{0:T(512)S(1)}, f32[512,128]{1,0:T(8,128)S(1)}) fusion(bf16[3072,128]{1,0:T(8,128)(2,1)S(1)} %bitcast.159, bf16[256,3200]{1,0:T(8,128)(2,1)} %get-tuple-element.8, bf16[256,3200]{1,0:T(8,128)(2,1)} %get-tuple-element.7), kind=kOutput, calls=%fused_computation.46 | convolution fusion | flops 409075200 | bytes 4327424 | tf_op jit(solution)/shard_map/dot_general | solution.py:316
  147.9 1.9 fusion.5
  150.2 2.6 %collective-permute-done.8 = bf16[256,128]{1,0:T(8,128)(2,1)} collective-permute-done((bf16[256,128]{1,0:T(8,128)(2,1)}, bf16[256,128]{1,0:T(8,128)(2,1)}, u32[]{:S(2)}, u32[]{:S(2)}) %collective-permute-start.8) | collective-permute-done | bytes 65568 | tf_op jit(solution)/shard_map/ppermute | solution.py:339
  154.2 1.5 collective-permute-start.24
  158.0 8.0 %shard_map.220 = bf16[1024,128]{1,0:T(8,128)(2,1)S(1)} custom-call(s32[8]{0:T(128)S(1)} %concatenate.57.request_ref, s32[1]{0:T(128)} %bitcast.3.place_ref, bf16[1024,128]{1,0:T(8,128)(2,1)S(1)} %pad_maximum_fusion.7.q_ref, bf16[2048,128]{1,0:T(8,128)(2,1)S(1)} %get-tuple-element.16.k_ref, bf16[2048,128]{1,0:T(8,128)(2,1)S(1)} %get-tuple-element.15.v_ref, ...), custom_call_target="tpu_custom_call" | custom-call | flops 1342177280 | bytes 2097152 | tf_op jit(solution)/shard_map/pallas_call | solution.py:217
  166.0 2.4 collective-permute-start.15
  168.4 3.4 %collective-permute-start.17 = (bf16[256,128]{1,0:T(8,128)(2,1)S(1)}, bf16[256,128]{1,0:T(8,128)(2,1)S(1)}, u32[]{:S(2)}, u32[]{:S(2)}) collective-permute-start(bf16[256,128]{1,0:T(8,128)(2,1)S(1)} %get-tuple-element.27), channel_id=1, source_target_pairs={{4,0},{12,2},{20,4},{28,6},{6,8},{14,10},{22,12},{30,14},{0,16},{8... | collective-permute-start | bytes 196616 | tf_op jit(solution)/shard_map/ppermute | solution.py:353
  173.1 3.5 %collective-permute-done.15 = bf16[256,128]{1,0:T(8,128)(2,1)S(1)} collective-permute-done((bf16[256,128]{1,0:T(8,128)(2,1)S(1)}, bf16[256,128]{1,0:T(8,128)(2,1)S(1)}, u32[]{:S(2)}, u32[]{:S(2)}) %collective-permute-start.15) | collective-permute-done | bytes 65568 | tf_op jit(solution)/shard_map/ppermute | solution.py:353
  178.8 5.4 %collective-permute-done.18 = bf16[256,128]{1,0:T(8,128)(2,1)S(1)} collective-permute-done((bf16[256,128]{1,0:T(8,128)(2,1)S(1)}, bf16[256,128]{1,0:T(8,128)(2,1)S(1)}, u32[]{:S(2)}, u32[]{:S(2)}) %collective-permute-start.18) | collective-permute-done | bytes 65568 | tf_op jit(solution)/shard_map/ppermute | solution.py:353
  184.8 1.9 collective-permute-start.19
  186.6 4.0 %collective-permute-start.20 = (bf16[512,256]{1,0:T(8,128)(2,1)S(1)}, bf16[512,256]{1,0:T(8,128)(2,1)S(1)}, u32[]{:S(2)}, u32[]{:S(2)}) collective-permute-start(bf16[512,256]{1,0:T(8,128)(2,1)S(1)} %dynamic_update_slice.83), channel_id=1, source_target_pairs={{0,4},{2,6},{4,0},{6,2},{8,12},{10,14},{12,8},{14,10},{16,20},{18,... | collective-permute-start | bytes 786440 | tf_op jit(solution)/shard_map/ppermute | solution.py:362
  191.0 6.3 %collective-permute-done.20 = bf16[512,256]{1,0:T(8,128)(2,1)S(1)} collective-permute-done((bf16[512,256]{1,0:T(8,128)(2,1)S(1)}, bf16[512,256]{1,0:T(8,128)(2,1)S(1)}, u32[]{:S(2)}, u32[]{:S(2)}) %collective-permute-start.20) | collective-permute-done | bytes 262176 | tf_op jit(solution)/shard_map/ppermute | solution.py:362
  197.3 5.6 %collective-permute-done.21 = bf16[512,256]{1,0:T(8,128)(2,1)S(1)} collective-permute-done((bf16[512,256]{1,0:T(8,128)(2,1)S(1)}, bf16[512,256]{1,0:T(8,128)(2,1)S(1)}, u32[]{:S(2)}, u32[]{:S(2)}) %collective-permute-start.21) | collective-permute-done | bytes 262176 | tf_op jit(solution)/shard_map/ppermute | solution.py:362
  204.0 1.6 collective-permute-start.30
  207.9 1.4 collective-permute-start.28
  213.3 2.9 %collective-permute-done.29 = bf16[128,384]{1,0:T(8,128)(2,1)S(1)} collective-permute-done((bf16[128,384]{1,0:T(8,128)(2,1)S(1)}, bf16[128,384]{1,0:T(8,128)(2,1)S(1)}, u32[]{:S(2)}, u32[]{:S(2)}) %collective-permute-start.29) | collective-permute-done | bytes 98336 | tf_op jit(solution)/shard_map/ppermute | solution.py:381
  220.8 1.4 collective-permute-start.32
  224.8 5.2 %collective-permute-start.33 = (bf16[64,64]{0,1:T(8,128)(2,1)S(1)}, bf16[64,64]{0,1:T(8,128)(2,1)S(1)}, u32[]{:S(2)}, u32[]{:S(2)}) collective-permute-start(bf16[64,64]{0,1:T(8,128)(2,1)S(1)} %get-tuple-element.40), channel_id=1, source_target_pairs={{0,2},{2,4},{4,6},{6,8},{8,10},{10,12},{12,14},{14,16},{16,18},{18... | collective-permute-start | bytes 24584 | tf_op jit(solution)/shard_map/ppermute | solution.py:27
  233.4 1.9 collective-permute-start.34
  235.4 3.1 %collective-permute-done.34 = bf16[64,64]{0,1:T(8,128)(2,1)S(1)} collective-permute-done((bf16[64,64]{0,1:T(8,128)(2,1)S(1)}, bf16[64,64]{0,1:T(8,128)(2,1)S(1)}, u32[]{:S(2)}, u32[]{:S(2)}) %collective-permute-start.34) | collective-permute-done | bytes 8224 | tf_op jit(solution)/shard_map/ppermute | solution.py:28
  (234 shorter events, 58.4 us)
Async XLA Ops:
  0.6 219.9 %copy-start = (bf16[1536,64]{0,1:T(8,128)(2,1)S(1)}, bf16[1536,64]{0,1:T(8,128)(2,1)}, u32[]{:S(2)}) copy-start(bf16[1536,64]{0,1:T(8,128)(2,1)} %param.36) | copy-start | bytes 589828
  0.6 7.2 %copy-start.3 = (bf16[128,3072]{1,0:T(8,128)(2,1)S(1)}, bf16[128,3072]{1,0:T(8,128)(2,1)}, u32[]{:S(2)}) copy-start(bf16[128,3072]{1,0:T(8,128)(2,1)} %param.21) | copy-start | bytes 2359300
  8.3 8.6 %copy-start.11 = (bf16[192,1024]{1,0:T(8,128)(2,1)S(1)}, bf16[192,1024]{1,0:T(8,128)(2,1)}, u32[]{:S(2)}) copy-start(bf16[192,1024]{1,0:T(8,128)(2,1)} %param.27) | copy-start | bytes 1179652
  9.4 13.5 %copy-start.24 = (s32[16]{0:T(128)S(1)}, s32[16]{0:T(128)}, u32[]{:S(2)}) copy-start(s32[16]{0:T(128)} %param.39) | copy-start | bytes 196
  10.2 31.6 %collective-permute-start.9 = (bf16[32,3200]{1,0:T(8,128)(2,1)}, bf16[32,3200]{1,0:T(8,128)(2,1)}, u32[]{:S(2)}, u32[]{:S(2)}) collective-permute-start(bf16[32,3200]{1,0:T(8,128)(2,1)} %pad_maximum_fusion.8), channel_id=1, source_target_pairs={{0,8},{2,10},{4,12},{6,14},{8,16},{10,18},{12,20},{14,22},{16,24},... | collective-permute-start | bytes 614408 | tf_op jit(solution)/shard_map/ppermute | solution.py:268
  12.3 31.1 %collective-permute-start.10 = (bf16[32,3200]{1,0:T(8,128)(2,1)}, bf16[32,3200]{1,0:T(8,128)(2,1)}, u32[]{:S(2)}, u32[]{:S(2)}) collective-permute-start(bf16[32,3200]{1,0:T(8,128)(2,1)} %pad_maximum_fusion.8), channel_id=1, source_target_pairs={{0,16},{2,18},{4,20},{6,22},{8,24},{10,26},{12,28},{14,30},{16,0},... | collective-permute-start | bytes 614408 | tf_op jit(solution)/shard_map/ppermute | solution.py:268
  14.6 38.3 %collective-permute-start.11 = (bf16[32,3200]{1,0:T(8,128)(2,1)}, bf16[32,3200]{1,0:T(8,128)(2,1)}, u32[]{:S(2)}, u32[]{:S(2)}) collective-permute-start(bf16[32,3200]{1,0:T(8,128)(2,1)} %pad_maximum_fusion.8), channel_id=1, source_target_pairs={{0,24},{2,26},{4,28},{6,30},{8,0},{10,2},{12,4},{14,6},{16,8},{18,... | collective-permute-start | bytes 614408 | tf_op jit(solution)/shard_map/ppermute | solution.py:268
  15.7 91.3 %collective-permute-start = (bf16[128,3072]{1,0:T(8,128)(2,1)S(1)}, bf16[128,3072]{1,0:T(8,128)(2,1)}, u32[]{:S(2)}, u32[]{:S(2)}) collective-permute-start(bf16[128,3072]{1,0:T(8,128)(2,1)S(1)} %add_convert_fusion), channel_id=1, source_target_pairs={{0,4},{2,6},{4,0},{6,2},{8,12},{10,14},{12,8},{14,10},{16,20},{18,... | collective-permute-start | bytes 2359304 | tf_op jit(solution)/shard_map/ppermute | solution.py:277
  17.7 27.3 %all-to-all-start = ((bf16[192,4,256]{2,0,1:T(8,128)(2,1)}), bf16[192,4,256]{2,0,1:T(8,128)(2,1)S(1)}, u32[]{:S(2)}, u32[]{:S(2)}) async-start(bf16[192,4,256]{2,0,1:T(8,128)(2,1)} %bitcast.139), calls=%async_computation | async-start | bytes 786432 | tf_op jit(solution)/shard_map/all_to_all | solution.py:311
  45.0 92.0 %all-to-all-start.1 = ((bf16[320,16,128]{2,0,1:T(8,128)(2,1)}), bf16[320,16,128]{2,0,1:T(8,128)(2,1)}, u32[]{:S(2)}, u32[]{:S(2)}) async-start(bf16[320,16,128]{2,0,1:T(8,128)(2,1)} %pad_maximum_fusion.4), calls=%async_computation.1 | async-start | bytes 2621440 | tf_op jit(solution)/shard_map/all_to_all | solution.py:295
  49.4 34.0 %collective-permute-start.2 = (bf16[768,256]{1,0:T(8,128)(2,1)S(1)}, bf16[768,256]{1,0:T(8,128)(2,1)S(1)}, u32[]{:S(2)}, u32[]{:S(2)}) collective-permute-start(bf16[768,256]{1,0:T(8,128)(2,1)S(1)} %bitcast.152), channel_id=1, source_target_pairs={{0,8},{2,10},{4,12},{6,14},{8,16},{10,18},{12,20},{14,22},{16,24},... | collective-permute-start | bytes 1179656 | tf_op jit(solution)/shard_map/ppermute | solution.py:268
  50.8 55.4 %collective-permute-start.3 = (bf16[768,256]{1,0:T(8,128)(2,1)S(1)}, bf16[768,256]{1,0:T(8,128)(2,1)S(1)}, u32[]{:S(2)}, u32[]{:S(2)}) collective-permute-start(bf16[768,256]{1,0:T(8,128)(2,1)S(1)} %bitcast.153), channel_id=1, source_target_pairs={{0,16},{2,18},{4,20},{6,22},{8,24},{10,26},{12,28},{14,30},{16,0},... | collective-permute-start | bytes 1179656 | tf_op jit(solution)/shard_map/ppermute | solution.py:268
  54.5 60.3 %collective-permute-start.12 = (bf16[128,3200]{1,0:T(8,128)(2,1)}, bf16[128,3200]{1,0:T(8,128)(2,1)}, u32[]{:S(2)}, u32[]{:S(2)}) collective-permute-start(bf16[128,3200]{1,0:T(8,128)(2,1)} %bitcast.27), channel_id=1, source_target_pairs={{0,4},{2,6},{4,0},{6,2},{8,12},{10,14},{12,8},{14,10},{16,20},{18,... | collective-permute-start | bytes 2457608 | tf_op jit(solution)/shard_map/ppermute | solution.py:277
  55.7 55.8 %collective-permute-start.4 = (bf16[768,256]{1,0:T(8,128)(2,1)S(1)}, bf16[768,256]{1,0:T(8,128)(2,1)S(1)}, u32[]{:S(2)}, u32[]{:S(2)}) collective-permute-start(bf16[768,256]{1,0:T(8,128)(2,1)S(1)} %bitcast.154), channel_id=1, source_target_pairs={{0,24},{2,26},{4,28},{6,30},{8,0},{10,2},{12,4},{14,6},{16,8},{18,... | collective-permute-start | bytes 1179656 | tf_op jit(solution)/shard_map/ppermute | solution.py:268
  58.2 48.8 %copy-start.18 = (f32[3072]{0:T(1024)S(1)}, f32[3072]{0:T(1024)}, u32[]{:S(2)}) copy-start(f32[3072]{0:T(1024)} %copy-done.17) | copy-start | bytes 36868
  58.2 48.8 %copy-start.20 = (f32[1,3072]{1,0:T(1,128)S(1)}, f32[1,3072]{1,0:T(1,128)}, u32[]{:S(2)}) copy-start(f32[1,3072]{1,0:T(1,128)} %copy-done.19) | copy-start | bytes 36868
  58.2 48.8 %copy-start.27 = (f32[128]{0:T(128)S(1)}, f32[128]{0:T(128)}, u32[]{:S(2)}) copy-start(f32[128]{0:T(128)} %copy-done.26) | copy-start | bytes 1540
  58.2 48.8 %copy-start.29 = (f32[128]{0:T(128)S(1)}, f32[128]{0:T(128)}, u32[]{:S(2)}) copy-start(f32[128]{0:T(128)} %copy-done.28) | copy-start | bytes 1540
  110.2 7.6 %collective-permute-start.1 = (bf16[256,3072]{1,0:T(8,128)(2,1)}, bf16[256,3072]{1,0:T(8,128)(2,1)}, u32[]{:S(2)}, u32[]{:S(2)}) collective-permute-start(bf16[256,3072]{1,0:T(8,128)(2,1)} %pad_maximum_fusion.3), channel_id=1, source_target_pairs={{0,2},{2,0},{4,6},{6,4},{8,10},{10,8},{12,14},{14,12},{16,18},{18,... | collective-permute-start | bytes 4718600 | tf_op jit(solution)/shard_map/ppermute | solution.py:277
  117.7 20.5 %collective-permute-start.13 = (bf16[256,3200]{1,0:T(8,128)(2,1)}, bf16[256,3200]{1,0:T(8,128)(2,1)}, u32[]{:S(2)}, u32[]{:S(2)}) collective-permute-start(bf16[256,3200]{1,0:T(8,128)(2,1)} %pad_maximum_fusion.2), channel_id=1, source_target_pairs={{0,2},{2,0},{4,6},{6,4},{8,10},{10,8},{12,14},{14,12},{16,18},{18,... | collective-permute-start | bytes 4915208 | tf_op jit(solution)/shard_map/ppermute | solution.py:277
  121.1 17.1 %copy-start.14 = (bf16[192,1024]{1,0:T(8,128)(2,1)S(1)}, bf16[192,1024]{1,0:T(8,128)(2,1)}, u32[]{:S(2)}) copy-start(bf16[192,1024]{1,0:T(8,128)(2,1)} %param.30) | copy-start | bytes 1179652
  122.0 27.7 %collective-permute-start.5 = (bf16[256,128]{1,0:T(8,128)(2,1)}, bf16[256,128]{1,0:T(8,128)(2,1)}, u32[]{:S(2)}, u32[]{:S(2)}) collective-permute-start(bf16[256,128]{1,0:T(8,128)(2,1)} %copy.102), channel_id=1, source_target_pairs={{0,0},{2,8},{4,16},{6,24},{8,2},{10,10},{12,18},{14,26},{16,4},{18... | collective-permute-start | bytes 196616 | tf_op jit(solution)/shard_map/ppermute | solution.py:339
  131.2 19.0 %collective-permute-start.6 = (bf16[256,128]{1,0:T(8,128)(2,1)}, bf16[256,128]{1,0:T(8,128)(2,1)}, u32[]{:S(2)}, u32[]{:S(2)}) collective-permute-start(bf16[256,128]{1,0:T(8,128)(2,1)} %copy.103), channel_id=1, source_target_pairs={{0,2},{2,10},{4,18},{6,26},{8,4},{10,12},{12,20},{14,28},{16,6},{1... | collective-permute-start | bytes 196616 | tf_op jit(solution)/shard_map/ppermute | solution.py:339
  132.0 18.2 %collective-permute-start.7 = (bf16[256,128]{1,0:T(8,128)(2,1)}, bf16[256,128]{1,0:T(8,128)(2,1)}, u32[]{:S(2)}, u32[]{:S(2)}) collective-permute-start(bf16[256,128]{1,0:T(8,128)(2,1)} %copy.104), channel_id=1, source_target_pairs={{0,4},{2,12},{4,20},{6,28},{8,6},{10,14},{12,22},{14,30},{16,0},{1... | collective-permute-start | bytes 196616 | tf_op jit(solution)/shard_map/ppermute | solution.py:339
  133.6 19.2 %collective-permute-start.8 = (bf16[256,128]{1,0:T(8,128)(2,1)}, bf16[256,128]{1,0:T(8,128)(2,1)}, u32[]{:S(2)}, u32[]{:S(2)}) collective-permute-start(bf16[256,128]{1,0:T(8,128)(2,1)} %copy.105), channel_id=1, source_target_pairs={{0,6},{2,14},{4,22},{6,30},{8,0},{10,8},{12,16},{14,24},{16,2},{18... | collective-permute-start | bytes 196616 | tf_op jit(solution)/shard_map/ppermute | solution.py:339
  138.2 17.7 %collective-permute-start.22 = (bf16[192,1024]{1,0:T(8,128)(2,1)S(1)}, bf16[192,1024]{1,0:T(8,128)(2,1)}, u32[]{:S(2)}, u32[]{:S(2)}) collective-permute-start(bf16[192,1024]{1,0:T(8,128)(2,1)S(1)} %copy-done.14), channel_id=1, source_target_pairs={{0,8},{2,10},{4,12},{6,14},{8,16},{10,18},{12,20},{14,22},{16,24},... | collective-permute-start | bytes 1179656 | tf_op jit(solution)/shard_map/ppermute | solution.py:268
  144.6 12.6 %copy-start.2 = (bf16[4,512,1024]{2,1,0:T(8,128)(2,1)S(1)}, bf16[4,512,1024]{2,1,0:T(8,128)(2,1)}, u32[]{:S(2)}) copy-start(bf16[4,512,1024]{2,1,0:T(8,128)(2,1)} %tv_ref.1) | copy-start | bytes 12582916
  149.8 7.3 %collective-permute-start.14 = (bf16[2048,128]{1,0:T(8,128)(2,1)S(1)}, bf16[2048,128]{1,0:T(8,128)(2,1)S(1)}, u32[]{:S(2)}, u32[]{:S(2)}) collective-permute-start(bf16[2048,128]{1,0:T(8,128)(2,1)S(1)} %bitcast.160), channel_id=1, source_target_pairs={{0,2},{2,0},{4,6},{6,4},{8,10},{10,8},{12,14},{14,12},{16,18},{18,... | collective-permute-start | bytes 1572872 | tf_op jit(solution)/shard_map/ppermute | solution.py:327
  153.7 19.3 %collective-permute-start.23 = (bf16[192,1024]{1,0:T(8,128)(2,1)S(1)}, bf16[192,1024]{1,0:T(8,128)(2,1)S(1)}, u32[]{:S(2)}, u32[]{:S(2)}) collective-permute-start(bf16[192,1024]{1,0:T(8,128)(2,1)S(1)} %copy-done.14), channel_id=1, source_target_pairs={{0,16},{2,18},{4,20},{6,22},{8,24},{10,26},{12,28},{14,30},{16,0},... | collective-permute-start | bytes 1179656 | tf_op jit(solution)/shard_map/ppermute | solution.py:268
  154.2 36.5 %collective-permute-start.24 = (bf16[192,1024]{1,0:T(8,128)(2,1)S(1)}, bf16[192,1024]{1,0:T(8,128)(2,1)S(1)}, u32[]{:S(2)}, u32[]{:S(2)}) collective-permute-start(bf16[192,1024]{1,0:T(8,128)(2,1)S(1)} %copy-done.14), channel_id=1, source_target_pairs={{0,24},{2,26},{4,28},{6,30},{8,0},{10,2},{12,4},{14,6},{16,8},{18,... | collective-permute-start | bytes 1179656 | tf_op jit(solution)/shard_map/ppermute | solution.py:268
  166.0 10.6 %collective-permute-start.15 = (bf16[256,128]{1,0:T(8,128)(2,1)S(1)}, bf16[256,128]{1,0:T(8,128)(2,1)S(1)}, u32[]{:S(2)}, u32[]{:S(2)}) collective-permute-start(bf16[256,128]{1,0:T(8,128)(2,1)S(1)} %get-tuple-element.29), channel_id=1, source_target_pairs={{0,0},{8,2},{16,4},{24,6},{2,8},{10,10},{18,12},{26,14},{4,16},{12... | collective-permute-start | bytes 196616 | tf_op jit(solution)/shard_map/ppermute | solution.py:353
  168.4 9.0 %collective-permute-start.16 = (bf16[256,128]{1,0:T(8,128)(2,1)S(1)}, bf16[256,128]{1,0:T(8,128)(2,1)S(1)}, u32[]{:S(2)}, u32[]{:S(2)}) collective-permute-start(bf16[256,128]{1,0:T(8,128)(2,1)S(1)} %get-tuple-element.28), channel_id=1, source_target_pairs={{2,0},{10,2},{18,4},{26,6},{4,8},{12,10},{20,12},{28,14},{6,16},{1... | collective-permute-start | bytes 196616 | tf_op jit(solution)/shard_map/ppermute | solution.py:353
  168.4 9.7 %collective-permute-start.17 = (bf16[256,128]{1,0:T(8,128)(2,1)S(1)}, bf16[256,128]{1,0:T(8,128)(2,1)S(1)}, u32[]{:S(2)}, u32[]{:S(2)}) collective-permute-start(bf16[256,128]{1,0:T(8,128)(2,1)S(1)} %get-tuple-element.27), channel_id=1, source_target_pairs={{4,0},{12,2},{20,4},{28,6},{6,8},{14,10},{22,12},{30,14},{0,16},{8... | collective-permute-start | bytes 196616 | tf_op jit(solution)/shard_map/ppermute | solution.py:353
  173.1 11.1 %collective-permute-start.18 = (bf16[256,128]{1,0:T(8,128)(2,1)S(1)}, bf16[256,128]{1,0:T(8,128)(2,1)S(1)}, u32[]{:S(2)}, u32[]{:S(2)}) collective-permute-start(bf16[256,128]{1,0:T(8,128)(2,1)S(1)} %get-tuple-element.26), channel_id=1, source_target_pairs={{6,0},{14,2},{22,4},{30,6},{0,8},{8,10},{16,12},{24,14},{2,16},{10... | collective-permute-start | bytes 196616 | tf_op jit(solution)/shard_map/ppermute | solution.py:353
  184.8 6.2 %collective-permute-start.19 = (bf16[512,256]{1,0:T(8,128)(2,1)S(1)}, bf16[512,256]{1,0:T(8,128)(2,1)S(1)}, u32[]{:S(2)}, u32[]{:S(2)}) collective-permute-start(bf16[512,256]{1,0:T(8,128)(2,1)S(1)} %dynamic_update_slice.83), channel_id=1, source_target_pairs={{0,2},{2,0},{4,6},{6,4},{8,10},{10,8},{12,14},{14,12},{16,18},{18,... | collective-permute-start | bytes 786440 | tf_op jit(solution)/shard_map/ppermute | solution.py:362
  186.6 10.6 %collective-permute-start.20 = (bf16[512,256]{1,0:T(8,128)(2,1)S(1)}, bf16[512,256]{1,0:T(8,128)(2,1)S(1)}, u32[]{:S(2)}, u32[]{:S(2)}) collective-permute-start(bf16[512,256]{1,0:T(8,128)(2,1)S(1)} %dynamic_update_slice.83), channel_id=1, source_target_pairs={{0,4},{2,6},{4,0},{6,2},{8,12},{10,14},{12,8},{14,10},{16,20},{18,... | collective-permute-start | bytes 786440 | tf_op jit(solution)/shard_map/ppermute | solution.py:362
  190.7 12.2 %collective-permute-start.21 = (bf16[512,256]{1,0:T(8,128)(2,1)S(1)}, bf16[512,256]{1,0:T(8,128)(2,1)S(1)}, u32[]{:S(2)}, u32[]{:S(2)}) collective-permute-start(bf16[512,256]{1,0:T(8,128)(2,1)S(1)} %dynamic_update_slice.83), channel_id=1, source_target_pairs={{0,6},{2,4},{4,2},{6,0},{8,14},{10,12},{12,10},{14,8},{16,22},{18,... | collective-permute-start | bytes 786440 | tf_op jit(solution)/shard_map/ppermute | solution.py:362
  204.0 6.3 %collective-permute-start.30 = (bf16[128,384]{1,0:T(8,128)(2,1)S(1)}, bf16[128,384]{1,0:T(8,128)(2,1)S(1)}, u32[]{:S(2)}, u32[]{:S(2)}) collective-permute-start(bf16[128,384]{1,0:T(8,128)(2,1)S(1)} %get-tuple-element.17), channel_id=1, source_target_pairs={{0,6},{1,7},{2,4},{3,5},{4,2},{5,3},{6,0},{7,1},{8,14},{9,15},{10,... | collective-permute-start | bytes 294920 | tf_op jit(solution)/shard_map/ppermute | solution.py:381
  205.7 6.6 %collective-permute-start.31 = (bf16[128,384]{1,0:T(8,128)(2,1)S(1)}, bf16[128,384]{1,0:T(8,128)(2,1)S(1)}, u32[]{:S(2)}, u32[]{:S(2)}) collective-permute-start(bf16[128,384]{1,0:T(8,128)(2,1)S(1)} %get-tuple-element.18), channel_id=1, source_target_pairs={{0,7},{1,6},{2,5},{3,4},{4,3},{5,2},{6,1},{7,0},{8,15},{9,14},{10,... | collective-permute-start | bytes 294920 | tf_op jit(solution)/shard_map/ppermute | solution.py:381
  207.9 5.4 %collective-permute-start.28 = (bf16[128,384]{1,0:T(8,128)(2,1)S(1)}, bf16[128,384]{1,0:T(8,128)(2,1)S(1)}, u32[]{:S(2)}, u32[]{:S(2)}) collective-permute-start(bf16[128,384]{1,0:T(8,128)(2,1)S(1)} %get-tuple-element.20), channel_id=1, source_target_pairs={{0,4},{1,5},{2,6},{3,7},{4,0},{5,1},{6,2},{7,3},{8,12},{9,13},{10,... | collective-permute-start | bytes 294920 | tf_op jit(solution)/shard_map/ppermute | solution.py:381
  209.4 6.8 %collective-permute-start.29 = (bf16[128,384]{1,0:T(8,128)(2,1)S(1)}, bf16[128,384]{1,0:T(8,128)(2,1)S(1)}, u32[]{:S(2)}, u32[]{:S(2)}) collective-permute-start(bf16[128,384]{1,0:T(8,128)(2,1)S(1)} %get-tuple-element.19), channel_id=1, source_target_pairs={{0,5},{1,4},{2,7},{3,6},{4,1},{5,0},{6,3},{7,2},{8,13},{9,12},{10,... | collective-permute-start | bytes 294920 | tf_op jit(solution)/shard_map/ppermute | solution.py:381
  209.4 6.8 %collective-permute-start.26 = (bf16[128,384]{1,0:T(8,128)(2,1)S(1)}, bf16[128,384]{1,0:T(8,128)(2,1)S(1)}, u32[]{:S(2)}, u32[]{:S(2)}) collective-permute-start(bf16[128,384]{1,0:T(8,128)(2,1)S(1)} %get-tuple-element.22), channel_id=1, source_target_pairs={{0,2},{1,3},{2,0},{3,1},{4,6},{5,7},{6,4},{7,5},{8,10},{9,11},{10,... | collective-permute-start | bytes 294920 | tf_op jit(solution)/shard_map/ppermute | solution.py:381
  210.3 7.0 %collective-permute-start.27 = (bf16[128,384]{1,0:T(8,128)(2,1)S(1)}, bf16[128,384]{1,0:T(8,128)(2,1)S(1)}, u32[]{:S(2)}, u32[]{:S(2)}) collective-permute-start(bf16[128,384]{1,0:T(8,128)(2,1)S(1)} %get-tuple-element.21), channel_id=1, source_target_pairs={{0,3},{1,2},{2,1},{3,0},{4,7},{5,6},{6,5},{7,4},{8,11},{9,10},{10,... | collective-permute-start | bytes 294920 | tf_op jit(solution)/shard_map/ppermute | solution.py:381
  212.2 6.5 %collective-permute-start.25 = (bf16[128,384]{1,0:T(8,128)(2,1)S(1)}, bf16[128,384]{1,0:T(8,128)(2,1)S(1)}, u32[]{:S(2)}, u32[]{:S(2)}) collective-permute-start(bf16[128,384]{1,0:T(8,128)(2,1)S(1)} %get-tuple-element.23), channel_id=1, source_target_pairs={{0,1},{1,0},{2,3},{3,2},{4,5},{5,4},{6,7},{7,6},{8,9},{9,8},{10,11... | collective-permute-start | bytes 294920 | tf_op jit(solution)/shard_map/ppermute | solution.py:381
  220.6 18.6 %copy-start.8 = (bf16[128,1536]{1,0:T(8,128)(2,1)}, bf16[128,1536]{1,0:T(8,128)(2,1)S(1)}, u32[]{:S(2)}) copy-start(bf16[128,1536]{1,0:T(8,128)(2,1)S(1)} %add_convert_fusion.1) | copy-start | bytes 1179652
  220.8 2.7 %collective-permute-start.32 = (bf16[128,64]{0,1:T(8,128)(2,1)S(1)}, bf16[128,64]{0,1:T(8,128)(2,1)S(1)}, u32[]{:S(2)}, u32[]{:S(2)}) collective-permute-start(bf16[128,64]{0,1:T(8,128)(2,1)S(1)} %convolution_convert_fusion.2), channel_id=1, source_target_pairs={{0,1},{1,0},{2,3},{3,2},{4,5},{5,4},{6,7},{7,6},{8,9},{9,8},{10,11... | collective-permute-start | bytes 49160 | tf_op jit(solution)/shard_map/ppermute | solution.py:466
  224.8 10.5 %collective-permute-start.33 = (bf16[64,64]{0,1:T(8,128)(2,1)S(1)}, bf16[64,64]{0,1:T(8,128)(2,1)S(1)}, u32[]{:S(2)}, u32[]{:S(2)}) collective-permute-start(bf16[64,64]{0,1:T(8,128)(2,1)S(1)} %get-tuple-element.40), channel_id=1, source_target_pairs={{0,2},{2,4},{4,6},{6,8},{8,10},{10,12},{12,14},{14,16},{16,18},{18... | collective-permute-start | bytes 24584 | tf_op jit(solution)/shard_map/ppermute | solution.py:27
  233.4 5.1 %collective-permute-start.34 = (bf16[64,64]{0,1:T(8,128)(2,1)S(1)}, bf16[64,64]{0,1:T(8,128)(2,1)S(1)}, u32[]{:S(2)}, u32[]{:S(2)}) collective-permute-start(bf16[64,64]{0,1:T(8,128)(2,1)S(1)} %get-tuple-element.41), channel_id=1, source_target_pairs={{2,0},{4,2},{6,4},{8,6},{10,8},{12,10},{14,12},{16,14},{18,16},{20... | collective-permute-start | bytes 24584 | tf_op jit(solution)/shard_map/ppermute | solution.py:28
  (24 other events, 55.2 us)

commit v4 on v3

--- a/solution.py
+++ b/solution.py
@@ -307,11 +307,11 @@
         axis=1,
     )
     all_listed = plane_gather(line_gather(listed_x))
-    query_w = line_gather(
-        lax.all_to_all(
-            query_weight, "seq", split_axis=1, concat_axis=0, axis_index_groups=inner, tiled=True
-        )
-    )
+    lined = lax.all_to_all(
+        line_gather(query_weight).reshape(lines, depth, group * width), "seq",
+        split_axis=2, concat_axis=1, axis_index_groups=inner, tiled=True,
+    )
+    query_w = lined.reshape(model, width)
     tokens = plane_gather(modulated)
     fresh_raw = jnp.dot(all_listed[:, :model], head_weight, preferred_element_type=jnp.float32)
     fresh_keys = head_norm(fresh_raw, key_gain).reshape(-1, HD)

time: 243 us -> 247 us (1.016)
  local copies, waits for them, and re-layouts: 39 us -> 52.1 us
  waiting for transfers between devices: 80.8 us -> 70.8 us
  other arithmetic: 29.4 us -> 24.6 us
  starting transfers between devices: 67 us -> 71.4 us
    ppermute x9, waiting for transfers between devices: 47.6 us -> 14.7 us  [line_gather(): lax.ppermute(block, 'seq', [(i, (i + k * group) % seq_count) for i in ran...]
    all_to_all x1, waiting for transfers between devices: 0.01 us -> 15.6 us  [grouped_branch(): lax.all_to_all(line_gather(query_weight).reshape(lines, depth, group * wi...]
    all_to_all x1, waiting for transfers between devices: 0.01 us -> 9.59 us  [grouped_branch(): lax.all_to_all(moved, 'seq', split_axis=1, concat_axis=0, tiled=True)]
    unnamed x85 -> x97, local copies, waits for them, and re-layouts: 5.8 us -> 15 us
    all_to_all x1, starting transfers between devices: 4.39 us -> 10 us  [grouped_branch(): lax.all_to_all(moved, 'seq', split_axis=1, concat_axis=0, tiled=True)]
    ppermute x4, starting transfers between devices: 12.7 us -> 8.35 us  [grouped_branch(): got_queries.append(lax.ppermute(block, 'seq', turns[k]))]
    ppermute x4, waiting for transfers between devices: 8.86 us -> 5.16 us  [grouped_branch(): back = lax.ppermute(block, 'seq', [(j, i) for i, j in turns[k]])]
    ppermute x3, starting transfers between devices: 5.95 us -> 9.52 us  [grouped_branch(): got = lax.ppermute(own_heads, 'seq', [(i, i ^ k) for i in range(seq_count)])]
  transfers between devices with their start and end apart: 37 -> 37, of which waited for: 15 -> 16; matrix products, arithmetic and copies ran while one was open for 26% -> 29% of each run, Pallas kernels for 3% -> 3%
where the time goes in v4:
time: 247 us; the launch traced here: 245 us
  starting transfers between devices  71.4 us (29%)
  waiting for transfers between devices  70.8 us (29%)
  local copies, waits for them, and re-layouts  52.1 us (21%)
  other arithmetic  24.6 us (10%)
  matrix products  13.6 us (6%)
  Pallas kernels  7.98 us (3%)
  between operations  4.49 us (2%)
    all_to_all x1, waiting for transfers between devices, grouped_branch(): lax.all_to_all(line_gather(query_weight).reshape(lines, depth, group * wi...  15.6 us
    unnamed x97, local copies, waits for them, and re-layouts  15 us
    ppermute x9, waiting for transfers between devices, line_gather(): lax.ppermute(block, 'seq', [(i, (i + k * group) % seq_count) for i in ran...  14.7 us
    ppermute x9, starting transfers between devices, line_gather(): lax.ppermute(block, 'seq', [(i, (i + k * group) % seq_count) for i in ran...  14.6 us
    ppermute x3, waiting for transfers between devices, grouped_branch(): got = lax.ppermute(own_heads, 'seq', [(i, i ^ k) for i in range(seq_count)])  11.8 us
    dynamic_update_slice x12, local copies, waits for them, and re-layouts, line_gather(): lax.dynamic_update_slice(full, got[None], (lax.rem(line + lines - k, line...  10.9 us
    all_to_all x1, starting transfers between devices, grouped_branch(): lax.all_to_all(moved, 'seq', split_axis=1, concat_axis=0, tiled=True)  10 us
    all_to_all x1, waiting for transfers between devices, grouped_branch(): lax.all_to_all(moved, 'seq', split_axis=1, concat_axis=0, tiled=True)  9.59 us
  transfers between devices with their start and end apart: 37, of which 16 were waited for; matrix products, arithmetic and copies ran while one was open for 29% of the time, Pallas kernels for 3%

profile of v4, /device:TPU:1, one launch (start us, length us, event | category | flops | bytes accessed | tf_op | source)
XLA Modules:
  0.0 245.0 jit_solution(3316213283148447748)
XLA Ops:
  3.4 1.6 fusion.13
  5.0 1.6 fusion.11
  10.0 2.2 collective-permute-start.9
  12.2 2.3 collective-permute-start.10
  29.2 1.4 constant_dynamic-update-slice_fusion.14
  37.4 2.2 fusion.15
  39.6 1.6 bitcast_dynamic-update-slice_fusion.10
  41.2 2.8 %collective-permute-start.4 = (bf16[192,1024]{1,0:T(8,128)(2,1)}, bf16[192,1024]{1,0:T(8,128)(2,1)S(1)}, u32[]{:S(2)}, u32[]{:S(2)}) collective-permute-start(bf16[192,1024]{1,0:T(8,128)(2,1)} %param.27), channel_id=1, source_target_pairs={{0,24},{2,26},{4,28},{6,30},{8,0},{10,2},{12,4},{14,6},{16,8},{18,... | collective-permute-start | bytes 1179656 | tf_op jit(solution)/shard_map/ppermute | solution.py:268
  44.1 1.6 bitcast_dynamic-update-slice_fusion.9
  45.7 1.6 bitcast_dynamic-update-slice_fusion.8
  48.6 11.1 %collective-permute-done.3 = bf16[192,1024]{1,0:T(8,128)(2,1)S(1)} collective-permute-done((bf16[192,1024]{1,0:T(8,128)(2,1)}, bf16[192,1024]{1,0:T(8,128)(2,1)S(1)}, u32[]{:S(2)}, u32[]{:S(2)}) %collective-permute-start.3) | collective-permute-done | bytes 393248 | tf_op jit(solution)/shard_map/ppermute | solution.py:268
  59.7 2.6 %copy.110 = bf16[4,192,1024]{1,0,2:T(4,128)(2,1)} copy(bf16[4,192,1024]{2,1,0:T(8,128)(2,1)S(1)} %bitcast_dynamic-update-slice_fusion.4) | data formatting | bytes 3145728 | tf_op jit(solution)/shard_map/dynamic_update_slice | solution.py:271
  62.3 7.3 %all-to-all-start = ((bf16[4,192,1024]{1,0,2:T(4,128)(2,1)}), bf16[4,192,1024]{1,0,2:T(4,128)(2,1)}, u32[]{:S(2)}, u32[]{:S(2)}) async-start(bf16[4,192,1024]{1,0,2:T(4,128)(2,1)} %copy.110), calls=%async_computation | async-start | bytes 4194304 | tf_op jit(solution)/shard_map/all_to_all | solution.py:310
  69.7 1.7 broadcast_select_fusion.7
  74.1 4.9 %concatenate.57.request_ref = s32[8]{0:T(128)S(1)} concatenate(s32[1]{0:T(128)} %get-tuple-element.55, s32[1]{0:T(128)} %get-tuple-element.54, s32[1]{0:T(128)} %get-tuple-element.53, s32[1]{0:T(128)} %get-tuple-element.52, s32[1]{0:T(128)} %get-tuple-element.51, s32[1]{0:T(128)} %get-tuple-element.50, s32[1]{0:T(128)} %get-tuple-element.49, s32[1]{0:T(128)} %get-tuple-element.48), dimensions={0} | concatenate | bytes 64 | tf_op jit(solution)/shard_map/concatenate | solution.py:347
  79.0 15.6 %all-to-all-done = bf16[4,192,1024]{1,0,2:T(4,128)(2,1)} async-done(((bf16[4,192,1024]{1,0,2:T(4,128)(2,1)}), bf16[4,192,1024]{1,0,2:T(4,128)(2,1)}, u32[]{:S(2)}, u32[]{:S(2)}) %all-to-all-start) | async-done | bytes 1572896 | tf_op jit(solution)/shard_map/all_to_all | solution.py:310
  94.6 10.0 %all-to-all-start.1 = ((bf16[320,16,128]{2,0,1:T(8,128)(2,1)}), bf16[320,16,128]{2,0,1:T(8,128)(2,1)}, u32[]{:S(2)}, u32[]{:S(2)}) async-start(bf16[320,16,128]{2,0,1:T(8,128)(2,1)} %pad_maximum_fusion.4), calls=%async_computation.1 | async-start | bytes 2621440 | tf_op jit(solution)/shard_map/all_to_all | solution.py:295
  104.6 1.5 broadcast_select_fusion.5
  107.6 4.2 %copy.112 = bf16[4,4,192,256]{3,2,1,0:T(8,128)(2,1)} copy(bf16[4,4,192,256]{2,0,3,1:T(4,128)(2,1)} %bitcast.15) | data formatting | bytes 3145728 | tf_op jit(solution)/shard_map/all_to_all | solution.py:310
  111.8 2.6 %copy.113 = bf16[256,3072]{1,0:T(8,128)(2,1)} copy(bf16[256,3072]{0,1:T(8,128)(2,1)} %bitcast.138) | data formatting | bytes 3145728 | tf_op jit(solution)/shard_map/dot_general | solution.py:331
  114.4 2.5 %broadcast_select_fusion.3 = (bf16[256,3072]{1,0:T(8,128)(2,1)S(1)}, bf16[256,3072]{1,0:T(8,128)(2,1)S(1)}) fusion(bf16[256,3072]{1,0:T(8,128)(2,1)} %collective-permute-done.1, pred[]{:T(512)S(6)} %eq.66, bf16[128,3072]{1,0:T(8,128)(2,1)} %copy-done.4, bf16[128,3072]{1,0:T(8,128)(2,1)S(1)} %get-tuple-element.13), kind=kLoop, calls=%fused_computation.15 | loop fusion | flops 4718592 | bytes 6291457 | tf_op jit(solution)/shard_map/jit(_where)/select_n | solution.py:278
  118.2 3.7 %collective-permute-start.5 = (bf16[256,128]{1,0:T(8,128)(2,1)S(1)}, bf16[256,128]{1,0:T(8,128)(2,1)}, u32[]{:S(2)}, u32[]{:S(2)}) collective-permute-start(bf16[256,128]{1,0:T(8,128)(2,1)S(1)} %copy.132), channel_id=1, source_target_pairs={{0,0},{2,8},{4,16},{6,24},{8,2},{10,10},{12,18},{14,26},{16,4},{18... | collective-permute-start | bytes 196616 | tf_op jit(solution)/shard_map/ppermute | solution.py:339
  122.3 2.2 collective-permute-start.7
  125.2 2.3 collective-permute-start.8
  127.6 9.6 %all-to-all-done.1 = bf16[320,16,128]{2,0,1:T(8,128)(2,1)} async-done(((bf16[320,16,128]{2,0,1:T(8,128)(2,1)}), bf16[320,16,128]{2,0,1:T(8,128)(2,1)}, u32[]{:S(2)}, u32[]{:S(2)}) %all-to-all-start.1) | async-done | bytes 1310752 | tf_op jit(solution)/shard_map/all_to_all | solution.py:295
  138.4 3.8 %collective-permute-start.22 = (bf16[192,1024]{1,0:T(8,128)(2,1)}, bf16[192,1024]{1,0:T(8,128)(2,1)}, u32[]{:S(2)}, u32[]{:S(2)}) collective-permute-start(bf16[192,1024]{1,0:T(8,128)(2,1)} %param.30), channel_id=1, source_target_pairs={{0,8},{2,10},{4,12},{6,14},{8,16},{10,18},{12,20},{14,22},{16,24},... | collective-permute-start | bytes 1179656 | tf_op jit(solution)/shard_map/ppermute | solution.py:268
  142.2 2.0 broadcast_select_fusion.1
  146.4 3.1 %multiply_reduce_fusion.2 = (f32[512]{0:T(512)S(1)}, f32[512,128]{1,0:T(8,128)S(1)}) fusion(bf16[3072,128]{1,0:T(8,128)(2,1)S(1)} %bitcast.153, bf16[256,3200]{1,0:T(8,128)(2,1)} %copy-done.6, bf16[256,3200]{1,0:T(8,128)(2,1)} %copy-done.5), kind=kOutput, calls=%fused_computation.46 | convolution fusion | flops 409075200 | bytes 4327424 | tf_op jit(solution)/shard_map/dot_general | solution.py:316
  149.7 1.9 fusion.5
  151.7 4.3 %collective-permute-done.8 = bf16[256,128]{1,0:T(8,128)(2,1)} collective-permute-done((bf16[256,128]{1,0:T(8,128)(2,1)}, bf16[256,128]{1,0:T(8,128)(2,1)}, u32[]{:S(2)}, u32[]{:S(2)}) %collective-permute-start.8) | collective-permute-done | bytes 65568 | tf_op jit(solution)/shard_map/ppermute | solution.py:339
  157.0 1.9 collective-permute-start.24
  161.2 8.0 %shard_map.220 = bf16[1024,128]{1,0:T(8,128)(2,1)S(1)} custom-call(s32[8]{0:T(128)S(1)} %concatenate.57.request_ref, s32[1]{0:T(128)} %bitcast.3.place_ref, bf16[1024,128]{1,0:T(8,128)(2,1)S(1)} %pad_maximum_fusion.7.q_ref, bf16[2048,128]{1,0:T(8,128)(2,1)S(1)} %get-tuple-element.16.k_ref, bf16[2048,128]{1,0:T(8,128)(2,1)S(1)} %get-tuple-element.15.v_ref, ...), custom_call_target="tpu_custom_call" | custom-call | flops 1342177280 | bytes 2097152 | tf_op jit(solution)/shard_map/pallas_call | solution.py:217
  169.2 1.9 collective-permute-start.15
  171.2 2.4 collective-permute-start.17
  173.6 3.7 %collective-permute-done.23 = bf16[192,1024]{1,0:T(8,128)(2,1)S(1)} collective-permute-done((bf16[192,1024]{1,0:T(8,128)(2,1)S(1)}, bf16[192,1024]{1,0:T(8,128)(2,1)S(1)}, u32[]{:S(2)}, u32[]{:S(2)}) %collective-permute-start.23) | collective-permute-done | bytes 393248 | tf_op jit(solution)/shard_map/ppermute | solution.py:268
  177.3 2.1 collective-permute-done.15
  181.6 3.0 %collective-permute-done.18 = bf16[256,128]{1,0:T(8,128)(2,1)S(1)} collective-permute-done((bf16[256,128]{1,0:T(8,128)(2,1)S(1)}, bf16[256,128]{1,0:T(8,128)(2,1)S(1)}, u32[]{:S(2)}, u32[]{:S(2)}) %collective-permute-start.18) | collective-permute-done | bytes 65568 | tf_op jit(solution)/shard_map/ppermute | solution.py:353
  185.3 3.8 %collective-permute-start.19 = (bf16[512,256]{1,0:T(8,128)(2,1)S(1)}, bf16[512,256]{1,0:T(8,128)(2,1)S(1)}, u32[]{:S(2)}, u32[]{:S(2)}) collective-permute-start(bf16[512,256]{1,0:T(8,128)(2,1)S(1)} %dynamic_update_slice.83), channel_id=1, source_target_pairs={{0,2},{2,0},{4,6},{6,4},{8,10},{10,8},{12,14},{14,12},{16,18},{18,... | collective-permute-start | bytes 786440 | tf_op jit(solution)/shard_map/ppermute | solution.py:362
  189.1 5.7 %collective-permute-start.20 = (bf16[512,256]{1,0:T(8,128)(2,1)S(1)}, bf16[512,256]{1,0:T(8,128)(2,1)S(1)}, u32[]{:S(2)}, u32[]{:S(2)}) collective-permute-start(bf16[512,256]{1,0:T(8,128)(2,1)S(1)} %dynamic_update_slice.83), channel_id=1, source_target_pairs={{0,4},{2,6},{4,0},{6,2},{8,12},{10,14},{12,8},{14,10},{16,20},{18,... | collective-permute-start | bytes 786440 | tf_op jit(solution)/shard_map/ppermute | solution.py:362
  195.0 6.3 %collective-permute-done.20 = bf16[512,256]{1,0:T(8,128)(2,1)S(1)} collective-permute-done((bf16[512,256]{1,0:T(8,128)(2,1)S(1)}, bf16[512,256]{1,0:T(8,128)(2,1)S(1)}, u32[]{:S(2)}, u32[]{:S(2)}) %collective-permute-start.20) | collective-permute-done | bytes 262176 | tf_op jit(solution)/shard_map/ppermute | solution.py:362
  201.3 5.6 %collective-permute-done.21 = bf16[512,256]{1,0:T(8,128)(2,1)S(1)} collective-permute-done((bf16[512,256]{1,0:T(8,128)(2,1)S(1)}, bf16[512,256]{1,0:T(8,128)(2,1)S(1)}, u32[]{:S(2)}, u32[]{:S(2)}) %collective-permute-start.21) | collective-permute-done | bytes 262176 | tf_op jit(solution)/shard_map/ppermute | solution.py:362
  208.1 1.6 collective-permute-start.30
  212.1 1.4 collective-permute-start.28
  217.4 2.8 %collective-permute-done.29 = bf16[128,384]{1,0:T(8,128)(2,1)S(1)} collective-permute-done((bf16[128,384]{1,0:T(8,128)(2,1)S(1)}, bf16[128,384]{1,0:T(8,128)(2,1)S(1)}, u32[]{:S(2)}, u32[]{:S(2)}) %collective-permute-start.29) | collective-permute-done | bytes 98336 | tf_op jit(solution)/shard_map/ppermute | solution.py:381
  224.9 1.5 collective-permute-start.32
  228.9 5.2 %collective-permute-start.33 = (bf16[64,64]{0,1:T(8,128)(2,1)S(1)}, bf16[64,64]{0,1:T(8,128)(2,1)S(1)}, u32[]{:S(2)}, u32[]{:S(2)}) collective-permute-start(bf16[64,64]{0,1:T(8,128)(2,1)S(1)} %get-tuple-element.40), channel_id=1, source_target_pairs={{0,2},{2,4},{4,6},{6,8},{8,10},{10,12},{12,14},{14,16},{16,18},{18... | collective-permute-start | bytes 24584 | tf_op jit(solution)/shard_map/ppermute | solution.py:27
  237.7 1.9 collective-permute-start.34
  239.6 3.1 %collective-permute-done.34 = bf16[64,64]{0,1:T(8,128)(2,1)S(1)} collective-permute-done((bf16[64,64]{0,1:T(8,128)(2,1)S(1)}, bf16[64,64]{0,1:T(8,128)(2,1)S(1)}, u32[]{:S(2)}, u32[]{:S(2)}) %collective-permute-start.34) | collective-permute-done | bytes 8224 | tf_op jit(solution)/shard_map/ppermute | solution.py:28
  (247 shorter events, 62.7 us)
Async XLA Ops:
  0.6 224.0 %copy-start = (bf16[1536,64]{0,1:T(8,128)(2,1)S(1)}, bf16[1536,64]{0,1:T(8,128)(2,1)}, u32[]{:S(2)}) copy-start(bf16[1536,64]{0,1:T(8,128)(2,1)} %param.36) | copy-start | bytes 589828
  9.2 7.9 %copy-start.27 = (s32[16]{0:T(128)S(1)}, s32[16]{0:T(128)}, u32[]{:S(2)}) copy-start(s32[16]{0:T(128)} %param.39) | copy-start | bytes 196
  10.0 9.3 %copy-start.14 = (bf16[192,1024]{1,0:T(8,128)(2,1)S(1)}, bf16[192,1024]{1,0:T(8,128)(2,1)}, u32[]{:S(2)}) copy-start(bf16[192,1024]{1,0:T(8,128)(2,1)} %param.28) | copy-start | bytes 1179652
  10.0 29.6 %collective-permute-start.9 = (bf16[32,3200]{1,0:T(8,128)(2,1)S(1)}, bf16[32,3200]{1,0:T(8,128)(2,1)}, u32[]{:S(2)}, u32[]{:S(2)}) collective-permute-start(bf16[32,3200]{1,0:T(8,128)(2,1)S(1)} %pad_maximum_fusion.8), channel_id=1, source_target_pairs={{0,8},{2,10},{4,12},{6,14},{8,16},{10,18},{12,20},{14,22},{16,24},... | collective-permute-start | bytes 614408 | tf_op jit(solution)/shard_map/ppermute | solution.py:268
  12.2 29.1 %collective-permute-start.10 = (bf16[32,3200]{1,0:T(8,128)(2,1)S(1)}, bf16[32,3200]{1,0:T(8,128)(2,1)}, u32[]{:S(2)}, u32[]{:S(2)}) collective-permute-start(bf16[32,3200]{1,0:T(8,128)(2,1)S(1)} %pad_maximum_fusion.8), channel_id=1, source_target_pairs={{0,16},{2,18},{4,20},{6,22},{8,24},{10,26},{12,28},{14,30},{16,0},... | collective-permute-start | bytes 614408 | tf_op jit(solution)/shard_map/ppermute | solution.py:268
  14.5 31.2 %collective-permute-start.11 = (bf16[32,3200]{1,0:T(8,128)(2,1)S(1)}, bf16[32,3200]{1,0:T(8,128)(2,1)}, u32[]{:S(2)}, u32[]{:S(2)}) collective-permute-start(bf16[32,3200]{1,0:T(8,128)(2,1)S(1)} %pad_maximum_fusion.8), channel_id=1, source_target_pairs={{0,24},{2,26},{4,28},{6,30},{8,0},{10,2},{12,4},{14,6},{16,8},{18,... | collective-permute-start | bytes 614408 | tf_op jit(solution)/shard_map/ppermute | solution.py:268
  15.6 54.1 %collective-permute-start = (bf16[128,3072]{1,0:T(8,128)(2,1)S(1)}, bf16[128,3072]{1,0:T(8,128)(2,1)}, u32[]{:S(2)}, u32[]{:S(2)}) collective-permute-start(bf16[128,3072]{1,0:T(8,128)(2,1)S(1)} %add_convert_fusion), channel_id=1, source_target_pairs={{0,4},{2,6},{4,0},{6,2},{8,12},{10,14},{12,8},{14,10},{16,20},{18,... | collective-permute-start | bytes 2359304 | tf_op jit(solution)/shard_map/ppermute | solution.py:277
  16.8 30.8 %collective-permute-start.2 = (bf16[192,1024]{1,0:T(8,128)(2,1)}, bf16[192,1024]{1,0:T(8,128)(2,1)}, u32[]{:S(2)}, u32[]{:S(2)}) collective-permute-start(bf16[192,1024]{1,0:T(8,128)(2,1)} %param.27), channel_id=1, source_target_pairs={{0,8},{2,10},{4,12},{6,14},{8,16},{10,18},{12,20},{14,22},{16,24},... | collective-permute-start | bytes 1179656 | tf_op jit(solution)/shard_map/ppermute | solution.py:268
  39.6 20.1 %collective-permute-start.3 = (bf16[192,1024]{1,0:T(8,128)(2,1)}, bf16[192,1024]{1,0:T(8,128)(2,1)S(1)}, u32[]{:S(2)}, u32[]{:S(2)}) collective-permute-start(bf16[192,1024]{1,0:T(8,128)(2,1)} %param.27), channel_id=1, source_target_pairs={{0,16},{2,18},{4,20},{6,22},{8,24},{10,26},{12,28},{14,30},{16,0},... | collective-permute-start | bytes 1179656 | tf_op jit(solution)/shard_map/ppermute | solution.py:268
  41.2 18.4 %collective-permute-start.4 = (bf16[192,1024]{1,0:T(8,128)(2,1)}, bf16[192,1024]{1,0:T(8,128)(2,1)S(1)}, u32[]{:S(2)}, u32[]{:S(2)}) collective-permute-start(bf16[192,1024]{1,0:T(8,128)(2,1)} %param.27), channel_id=1, source_target_pairs={{0,24},{2,26},{4,28},{6,30},{8,0},{10,2},{12,4},{14,6},{16,8},{18,... | collective-permute-start | bytes 1179656 | tf_op jit(solution)/shard_map/ppermute | solution.py:268
  47.3 57.3 %collective-permute-start.12 = (bf16[128,3200]{1,0:T(8,128)(2,1)}, bf16[128,3200]{1,0:T(8,128)(2,1)}, u32[]{:S(2)}, u32[]{:S(2)}) collective-permute-start(bf16[128,3200]{1,0:T(8,128)(2,1)} %bitcast.27), channel_id=1, source_target_pairs={{0,4},{2,6},{4,0},{6,2},{8,12},{10,14},{12,8},{14,10},{16,20},{18,... | collective-permute-start | bytes 2457608 | tf_op jit(solution)/shard_map/ppermute | solution.py:277
  62.3 7.3 %copy-start.20 = (f32[3072]{0:T(1024)S(1)}, f32[3072]{0:T(1024)}, u32[]{:S(2)}) copy-start(f32[3072]{0:T(1024)} %copy-done.19) | copy-start | bytes 36868
  62.3 7.3 %copy-start.22 = (f32[1,3072]{1,0:T(1,128)S(1)}, f32[1,3072]{1,0:T(1,128)}, u32[]{:S(2)}) copy-start(f32[1,3072]{1,0:T(1,128)} %copy-done.21) | copy-start | bytes 36868
  62.3 7.4 %copy-start.31 = (f32[128]{0:T(128)S(1)}, f32[128]{0:T(128)}, u32[]{:S(2)}) copy-start(f32[128]{0:T(128)} %copy-done.30) | copy-start | bytes 1540
  62.3 7.4 %copy-start.34 = (f32[128]{0:T(128)S(1)}, f32[128]{0:T(128)}, u32[]{:S(2)}) copy-start(f32[128]{0:T(128)} %copy-done.33) | copy-start | bytes 1540
  62.3 32.3 %all-to-all-start = ((bf16[4,192,1024]{1,0,2:T(4,128)(2,1)}), bf16[4,192,1024]{1,0,2:T(4,128)(2,1)}, u32[]{:S(2)}, u32[]{:S(2)}) async-start(bf16[4,192,1024]{1,0,2:T(4,128)(2,1)} %copy.110), calls=%async_computation | async-start | bytes 4194304 | tf_op jit(solution)/shard_map/all_to_all | solution.py:310
  72.8 41.6 %collective-permute-start.1 = (bf16[256,3072]{1,0:T(8,128)(2,1)}, bf16[256,3072]{1,0:T(8,128)(2,1)}, u32[]{:S(2)}, u32[]{:S(2)}) collective-permute-start(bf16[256,3072]{1,0:T(8,128)(2,1)} %pad_maximum_fusion.3), channel_id=1, source_target_pairs={{0,2},{2,0},{4,6},{6,4},{8,10},{10,8},{12,14},{14,12},{16,18},{18,... | collective-permute-start | bytes 4718600 | tf_op jit(solution)/shard_map/ppermute | solution.py:277
  94.6 42.6 %all-to-all-start.1 = ((bf16[320,16,128]{2,0,1:T(8,128)(2,1)}), bf16[320,16,128]{2,0,1:T(8,128)(2,1)}, u32[]{:S(2)}, u32[]{:S(2)}) async-start(bf16[320,16,128]{2,0,1:T(8,128)(2,1)} %pad_maximum_fusion.4), calls=%async_computation.1 | async-start | bytes 2621440 | tf_op jit(solution)/shard_map/all_to_all | solution.py:295
  107.5 30.9 %collective-permute-start.13 = (bf16[256,3200]{1,0:T(8,128)(2,1)}, bf16[256,3200]{1,0:T(8,128)(2,1)}, u32[]{:S(2)}, u32[]{:S(2)}) collective-permute-start(bf16[256,3200]{1,0:T(8,128)(2,1)} %pad_maximum_fusion.2), channel_id=1, source_target_pairs={{0,2},{2,0},{4,6},{6,4},{8,10},{10,8},{12,14},{14,12},{16,18},{18,... | collective-permute-start | bytes 4915208 | tf_op jit(solution)/shard_map/ppermute | solution.py:277
  118.2 33.3 %collective-permute-start.5 = (bf16[256,128]{1,0:T(8,128)(2,1)S(1)}, bf16[256,128]{1,0:T(8,128)(2,1)}, u32[]{:S(2)}, u32[]{:S(2)}) collective-permute-start(bf16[256,128]{1,0:T(8,128)(2,1)S(1)} %copy.132), channel_id=1, source_target_pairs={{0,0},{2,8},{4,16},{6,24},{8,2},{10,10},{12,18},{14,26},{16,4},{18... | collective-permute-start | bytes 196616 | tf_op jit(solution)/shard_map/ppermute | solution.py:339
  122.1 29.6 %collective-permute-start.6 = (bf16[256,128]{1,0:T(8,128)(2,1)S(1)}, bf16[256,128]{1,0:T(8,128)(2,1)}, u32[]{:S(2)}, u32[]{:S(2)}) collective-permute-start(bf16[256,128]{1,0:T(8,128)(2,1)S(1)} %copy.133), channel_id=1, source_target_pairs={{0,2},{2,10},{4,18},{6,26},{8,4},{10,12},{12,20},{14,28},{16,6},{1... | collective-permute-start | bytes 196616 | tf_op jit(solution)/shard_map/ppermute | solution.py:339
  122.3 29.4 %collective-permute-start.7 = (bf16[256,128]{1,0:T(8,128)(2,1)S(1)}, bf16[256,128]{1,0:T(8,128)(2,1)}, u32[]{:S(2)}, u32[]{:S(2)}) collective-permute-start(bf16[256,128]{1,0:T(8,128)(2,1)S(1)} %copy.134), channel_id=1, source_target_pairs={{0,4},{2,12},{4,20},{6,28},{8,6},{10,14},{12,22},{14,30},{16,0},{1... | collective-permute-start | bytes 196616 | tf_op jit(solution)/shard_map/ppermute | solution.py:339
  125.2 30.8 %collective-permute-start.8 = (bf16[256,128]{1,0:T(8,128)(2,1)}, bf16[256,128]{1,0:T(8,128)(2,1)}, u32[]{:S(2)}, u32[]{:S(2)}) collective-permute-start(bf16[256,128]{1,0:T(8,128)(2,1)} %copy.135), channel_id=1, source_target_pairs={{0,6},{2,14},{4,22},{6,30},{8,0},{10,8},{12,16},{14,24},{16,2},{18... | collective-permute-start | bytes 196616 | tf_op jit(solution)/shard_map/ppermute | solution.py:339
  138.4 20.8 %collective-permute-start.22 = (bf16[192,1024]{1,0:T(8,128)(2,1)}, bf16[192,1024]{1,0:T(8,128)(2,1)}, u32[]{:S(2)}, u32[]{:S(2)}) collective-permute-start(bf16[192,1024]{1,0:T(8,128)(2,1)} %param.30), channel_id=1, source_target_pairs={{0,8},{2,10},{4,12},{6,14},{8,16},{10,18},{12,20},{14,22},{16,24},... | collective-permute-start | bytes 1179656 | tf_op jit(solution)/shard_map/ppermute | solution.py:268
  146.4 14.1 %copy-start.2 = (bf16[4,512,1024]{2,1,0:T(8,128)(2,1)S(1)}, bf16[4,512,1024]{2,1,0:T(8,128)(2,1)}, u32[]{:S(2)}) copy-start(bf16[4,512,1024]{2,1,0:T(8,128)(2,1)} %tv_ref.1) | copy-start | bytes 12582916
  149.5 7.5 %copy-start.16 = (bf16[192,1024]{1,0:T(8,128)(2,1)S(1)}, bf16[192,1024]{1,0:T(8,128)(2,1)}, u32[]{:S(2)}) copy-start(bf16[192,1024]{1,0:T(8,128)(2,1)} %param.30) | copy-start | bytes 1179652
  151.6 8.8 %collective-permute-start.14 = (bf16[2048,128]{1,0:T(8,128)(2,1)S(1)}, bf16[2048,128]{1,0:T(8,128)(2,1)S(1)}, u32[]{:S(2)}, u32[]{:S(2)}) collective-permute-start(bf16[2048,128]{1,0:T(8,128)(2,1)S(1)} %bitcast.154), channel_id=1, source_target_pairs={{0,2},{2,0},{4,6},{6,4},{8,10},{10,8},{12,14},{14,12},{16,18},{18,... | collective-permute-start | bytes 1572872 | tf_op jit(solution)/shard_map/ppermute | solution.py:327
  157.0 20.3 %collective-permute-start.23 = (bf16[192,1024]{1,0:T(8,128)(2,1)S(1)}, bf16[192,1024]{1,0:T(8,128)(2,1)S(1)}, u32[]{:S(2)}, u32[]{:S(2)}) collective-permute-start(bf16[192,1024]{1,0:T(8,128)(2,1)S(1)} %copy-done.16), channel_id=1, source_target_pairs={{0,16},{2,18},{4,20},{6,22},{8,24},{10,26},{12,28},{14,30},{16,0},... | collective-permute-start | bytes 1179656 | tf_op jit(solution)/shard_map/ppermute | solution.py:268
  157.0 37.7 %collective-permute-start.24 = (bf16[192,1024]{1,0:T(8,128)(2,1)S(1)}, bf16[192,1024]{1,0:T(8,128)(2,1)S(1)}, u32[]{:S(2)}, u32[]{:S(2)}) collective-permute-start(bf16[192,1024]{1,0:T(8,128)(2,1)S(1)} %copy-done.16), channel_id=1, source_target_pairs={{0,24},{2,26},{4,28},{6,30},{8,0},{10,2},{12,4},{14,6},{16,8},{18,... | collective-permute-start | bytes 1179656 | tf_op jit(solution)/shard_map/ppermute | solution.py:268
  169.2 10.2 %collective-permute-start.15 = (bf16[256,128]{1,0:T(8,128)(2,1)S(1)}, bf16[256,128]{1,0:T(8,128)(2,1)S(1)}, u32[]{:S(2)}, u32[]{:S(2)}) collective-permute-start(bf16[256,128]{1,0:T(8,128)(2,1)S(1)} %get-tuple-element.29), channel_id=1, source_target_pairs={{0,0},{8,2},{16,4},{24,6},{2,8},{10,10},{18,12},{26,14},{4,16},{12... | collective-permute-start | bytes 196616 | tf_op jit(solution)/shard_map/ppermute | solution.py:353
  171.2 9.1 %collective-permute-start.16 = (bf16[256,128]{1,0:T(8,128)(2,1)S(1)}, bf16[256,128]{1,0:T(8,128)(2,1)S(1)}, u32[]{:S(2)}, u32[]{:S(2)}) collective-permute-start(bf16[256,128]{1,0:T(8,128)(2,1)S(1)} %get-tuple-element.28), channel_id=1, source_target_pairs={{2,0},{10,2},{18,4},{26,6},{4,8},{12,10},{20,12},{28,14},{6,16},{1... | collective-permute-start | bytes 196616 | tf_op jit(solution)/shard_map/ppermute | solution.py:353
  171.2 9.7 %collective-permute-start.17 = (bf16[256,128]{1,0:T(8,128)(2,1)S(1)}, bf16[256,128]{1,0:T(8,128)(2,1)S(1)}, u32[]{:S(2)}, u32[]{:S(2)}) collective-permute-start(bf16[256,128]{1,0:T(8,128)(2,1)S(1)} %get-tuple-element.27), channel_id=1, source_target_pairs={{4,0},{12,2},{20,4},{28,6},{6,8},{14,10},{22,12},{30,14},{0,16},{8... | collective-permute-start | bytes 196616 | tf_op jit(solution)/shard_map/ppermute | solution.py:353
  177.2 7.4 %collective-permute-start.18 = (bf16[256,128]{1,0:T(8,128)(2,1)S(1)}, bf16[256,128]{1,0:T(8,128)(2,1)S(1)}, u32[]{:S(2)}, u32[]{:S(2)}) collective-permute-start(bf16[256,128]{1,0:T(8,128)(2,1)S(1)} %get-tuple-element.26), channel_id=1, source_target_pairs={{6,0},{14,2},{22,4},{30,6},{0,8},{8,10},{16,12},{24,14},{2,16},{10... | collective-permute-start | bytes 196616 | tf_op jit(solution)/shard_map/ppermute | solution.py:353
  185.3 9.7 %collective-permute-start.19 = (bf16[512,256]{1,0:T(8,128)(2,1)S(1)}, bf16[512,256]{1,0:T(8,128)(2,1)S(1)}, u32[]{:S(2)}, u32[]{:S(2)}) collective-permute-start(bf16[512,256]{1,0:T(8,128)(2,1)S(1)} %dynamic_update_slice.83), channel_id=1, source_target_pairs={{0,2},{2,0},{4,6},{6,4},{8,10},{10,8},{12,14},{14,12},{16,18},{18,... | collective-permute-start | bytes 786440 | tf_op jit(solution)/shard_map/ppermute | solution.py:362
  189.1 12.2 %collective-permute-start.20 = (bf16[512,256]{1,0:T(8,128)(2,1)S(1)}, bf16[512,256]{1,0:T(8,128)(2,1)S(1)}, u32[]{:S(2)}, u32[]{:S(2)}) collective-permute-start(bf16[512,256]{1,0:T(8,128)(2,1)S(1)} %dynamic_update_slice.83), channel_id=1, source_target_pairs={{0,4},{2,6},{4,0},{6,2},{8,12},{10,14},{12,8},{14,10},{16,20},{18,... | collective-permute-start | bytes 786440 | tf_op jit(solution)/shard_map/ppermute | solution.py:362
  194.8 12.2 %collective-permute-start.21 = (bf16[512,256]{1,0:T(8,128)(2,1)S(1)}, bf16[512,256]{1,0:T(8,128)(2,1)S(1)}, u32[]{:S(2)}, u32[]{:S(2)}) collective-permute-start(bf16[512,256]{1,0:T(8,128)(2,1)S(1)} %dynamic_update_slice.83), channel_id=1, source_target_pairs={{0,6},{2,4},{4,2},{6,0},{8,14},{10,12},{12,10},{14,8},{16,22},{18,... | collective-permute-start | bytes 786440 | tf_op jit(solution)/shard_map/ppermute | solution.py:362
  208.1 6.4 %collective-permute-start.30 = (bf16[128,384]{1,0:T(8,128)(2,1)S(1)}, bf16[128,384]{1,0:T(8,128)(2,1)S(1)}, u32[]{:S(2)}, u32[]{:S(2)}) collective-permute-start(bf16[128,384]{1,0:T(8,128)(2,1)S(1)} %get-tuple-element.17), channel_id=1, source_target_pairs={{0,6},{1,7},{2,4},{3,5},{4,2},{5,3},{6,0},{7,1},{8,14},{9,15},{10,... | collective-permute-start | bytes 294920 | tf_op jit(solution)/shard_map/ppermute | solution.py:381
  209.7 6.6 %collective-permute-start.31 = (bf16[128,384]{1,0:T(8,128)(2,1)S(1)}, bf16[128,384]{1,0:T(8,128)(2,1)S(1)}, u32[]{:S(2)}, u32[]{:S(2)}) collective-permute-start(bf16[128,384]{1,0:T(8,128)(2,1)S(1)} %get-tuple-element.18), channel_id=1, source_target_pairs={{0,7},{1,6},{2,5},{3,4},{4,3},{5,2},{6,1},{7,0},{8,15},{9,14},{10,... | collective-permute-start | bytes 294920 | tf_op jit(solution)/shard_map/ppermute | solution.py:381
  212.1 5.3 %collective-permute-start.28 = (bf16[128,384]{1,0:T(8,128)(2,1)S(1)}, bf16[128,384]{1,0:T(8,128)(2,1)S(1)}, u32[]{:S(2)}, u32[]{:S(2)}) collective-permute-start(bf16[128,384]{1,0:T(8,128)(2,1)S(1)} %get-tuple-element.20), channel_id=1, source_target_pairs={{0,4},{1,5},{2,6},{3,7},{4,0},{5,1},{6,2},{7,3},{8,12},{9,13},{10,... | collective-permute-start | bytes 294920 | tf_op jit(solution)/shard_map/ppermute | solution.py:381
  213.6 6.7 %collective-permute-start.29 = (bf16[128,384]{1,0:T(8,128)(2,1)S(1)}, bf16[128,384]{1,0:T(8,128)(2,1)S(1)}, u32[]{:S(2)}, u32[]{:S(2)}) collective-permute-start(bf16[128,384]{1,0:T(8,128)(2,1)S(1)} %get-tuple-element.19), channel_id=1, source_target_pairs={{0,5},{1,4},{2,7},{3,6},{4,1},{5,0},{6,3},{7,2},{8,13},{9,12},{10,... | collective-permute-start | bytes 294920 | tf_op jit(solution)/shard_map/ppermute | solution.py:381
  213.6 6.8 %collective-permute-start.26 = (bf16[128,384]{1,0:T(8,128)(2,1)S(1)}, bf16[128,384]{1,0:T(8,128)(2,1)S(1)}, u32[]{:S(2)}, u32[]{:S(2)}) collective-permute-start(bf16[128,384]{1,0:T(8,128)(2,1)S(1)} %get-tuple-element.22), channel_id=1, source_target_pairs={{0,2},{1,3},{2,0},{3,1},{4,6},{5,7},{6,4},{7,5},{8,10},{9,11},{10,... | collective-permute-start | bytes 294920 | tf_op jit(solution)/shard_map/ppermute | solution.py:381
  214.5 7.1 %collective-permute-start.27 = (bf16[128,384]{1,0:T(8,128)(2,1)S(1)}, bf16[128,384]{1,0:T(8,128)(2,1)S(1)}, u32[]{:S(2)}, u32[]{:S(2)}) collective-permute-start(bf16[128,384]{1,0:T(8,128)(2,1)S(1)} %get-tuple-element.21), channel_id=1, source_target_pairs={{0,3},{1,2},{2,1},{3,0},{4,7},{5,6},{6,5},{7,4},{8,11},{9,10},{10,... | collective-permute-start | bytes 294920 | tf_op jit(solution)/shard_map/ppermute | solution.py:381
  216.3 6.5 %collective-permute-start.25 = (bf16[128,384]{1,0:T(8,128)(2,1)S(1)}, bf16[128,384]{1,0:T(8,128)(2,1)S(1)}, u32[]{:S(2)}, u32[]{:S(2)}) collective-permute-start(bf16[128,384]{1,0:T(8,128)(2,1)S(1)} %get-tuple-element.23), channel_id=1, source_target_pairs={{0,1},{1,0},{2,3},{3,2},{4,5},{5,4},{6,7},{7,6},{8,9},{9,8},{10,11... | collective-permute-start | bytes 294920 | tf_op jit(solution)/shard_map/ppermute | solution.py:381
  224.5 9.7 %copy-start.29 = (s32[16]{0:T(128)S(1)}, s32[16]{0:T(128)}, u32[]{:S(2)}) copy-start(s32[16]{0:T(128)} %param.39) | copy-start | bytes 196
  224.6 18.7 %copy-start.9 = (bf16[128,1536]{1,0:T(8,128)(2,1)}, bf16[128,1536]{1,0:T(8,128)(2,1)S(1)}, u32[]{:S(2)}) copy-start(bf16[128,1536]{1,0:T(8,128)(2,1)S(1)} %add_convert_fusion.1) | copy-start | bytes 1179652
  224.9 2.7 %collective-permute-start.32 = (bf16[128,64]{0,1:T(8,128)(2,1)S(1)}, bf16[128,64]{0,1:T(8,128)(2,1)S(1)}, u32[]{:S(2)}, u32[]{:S(2)}) collective-permute-start(bf16[128,64]{0,1:T(8,128)(2,1)S(1)} %convolution_convert_fusion.2), channel_id=1, source_target_pairs={{0,1},{1,0},{2,3},{3,2},{4,5},{5,4},{6,7},{7,6},{8,9},{9,8},{10,11... | collective-permute-start | bytes 49160 | tf_op jit(solution)/shard_map/ppermute | solution.py:466
  228.9 10.7 %collective-permute-start.33 = (bf16[64,64]{0,1:T(8,128)(2,1)S(1)}, bf16[64,64]{0,1:T(8,128)(2,1)S(1)}, u32[]{:S(2)}, u32[]{:S(2)}) collective-permute-start(bf16[64,64]{0,1:T(8,128)(2,1)S(1)} %get-tuple-element.40), channel_id=1, source_target_pairs={{0,2},{2,4},{4,6},{6,8},{8,10},{10,12},{12,14},{14,16},{16,18},{18... | collective-permute-start | bytes 24584 | tf_op jit(solution)/shard_map/ppermute | solution.py:27
  237.7 5.1 %collective-permute-start.34 = (bf16[64,64]{0,1:T(8,128)(2,1)S(1)}, bf16[64,64]{0,1:T(8,128)(2,1)S(1)}, u32[]{:S(2)}, u32[]{:S(2)}) collective-permute-start(bf16[64,64]{0,1:T(8,128)(2,1)S(1)} %get-tuple-element.41), channel_id=1, source_target_pairs={{2,0},{4,2},{6,4},{8,6},{10,8},{12,10},{14,12},{16,14},{18,16},{20... | collective-permute-start | bytes 24584 | tf_op jit(solution)/shard_map/ppermute | solution.py:28
  (30 other events, 70.6 us)
